TPU v7x, 32 devices: a whole 2x2x4 slice. The times are simulated.
32 devices in a mesh: lat: 4 (over y, x), lon: 8 (over z, core).
Axes of the slice: x: 2, y: 2, z: 4, core: 2. Of those that a mesh axis runs over, the one named last changes fastest.
Arguments:
- background: bfloat16 [64, 256, 512], P('lat', 'lon'), may hold values from -6 to 6
- observations: bfloat16 [32768, 256], P(('lat', 'lon')), may hold values from -6 to 6
- destination: int32 [32768, 1], P(('lat', 'lon')), may hold values from 0 to 31; in each aligned block of 1024 rows (0 to 1023, 1024 to 2047, ...) at most 64 rows name the same one
- footprint: int32 [32768, 4], P(('lat', 'lon')), may hold values from 0 to 511, as said below
- weights: bfloat16 [32768, 4], P(('lat', 'lon')), may hold values from 0.099609375 to 1
- obs_proj: bfloat16 [256, 512], replicated, may hold values from -0.375 to 0.375
- depth_w: float32 [4, 7, 7, 512], replicated, may hold values from -1.5 to 1.5
- point_w: bfloat16 [4, 512, 512], replicated, may hold values from -0.25 to 0.25
- gains: float32 [4, 512], replicated, may hold values from 0.5 to 2
Outputs:
- encoded: bfloat16 [64, 256, 512], P('lat', 'lon')
Inputs may be any that keep to these rules, and one draw needn't show every extreme that they name: `destination`: each device's 1024 rows name one tile at most 64 times. footprint[i, k] = (s_i + k * 33) mod 512 for a start cell s_i, so the 4 cells of one observation are distinct.
All inputs are finite; a program needn't handle non-finite values.
Results may differ from a plain program's by a relative error of at most 0.0085.
Values may be sent and summed in bfloat16 or wider, within the bound.
No kernel may reach another device: no remote copies, remote signals or barrier semaphores. Data moves between devices by JAX's collectives and lax.ppermute only.
A program may use at most 64 MiB of HBM per device.

v0:
```python
import functools

import jax
import jax.numpy as jnp
from jax import lax
from jax.experimental import pallas as pl
from jax.experimental.pallas import tpu as pltpu
from jax.sharding import PartitionSpec as P

LANES = 128
META = 8
TAPS = 7
HALO = 3
SHIFT = 2 * HALO
EDGE = 8
TILE = 16
SUBLANES = 8
WORK = 5000
VMEM_LIMIT = 24 * 1024 * 1024
PACK_LIMIT = 58 * 1024 * 1024
BF16 = jnp.bfloat16
F32 = jnp.float32


def pack_kernel(cap, cols, dest_hbm, foot_hbm, weights_hbm, obs_hbm, send_ref, dest_ref, foot_ref, weights_ref, obs_ref, sems):
    copies = [
        pltpu.make_async_copy(source, target, sems.at[k])
        for k, (source, target) in enumerate(
            (
                (dest_hbm, dest_ref),
                (obs_hbm, obs_ref),
                (foot_hbm, foot_ref),
                (weights_hbm, weights_ref),
            )
        )
    ]
    for copy in copies:
        copy.start()
    devices = send_ref.shape[0]
    obs_rows = obs_ref.shape[0]
    per = LANES // cap
    upper = lax.broadcasted_iota(jnp.int32, (LANES, LANES), 0) <= lax.broadcasted_iota(
        jnp.int32, (LANES, LANES), 1
    )
    upper = jnp.where(upper, 1.0, 0.0).astype(BF16)
    ids = lax.broadcasted_iota(jnp.int32, (devices, obs_rows), 0)
    copies[0].wait()
    member = jnp.where(ids == dest_ref[...], 1.0, 0.0)
    seen = jnp.zeros((devices, 1), F32)
    ranks = []
    for first in range(0, obs_rows, LANES):
        part = member[:, first : first + LANES]
        count = jnp.dot(part.astype(BF16), upper, preferred_element_type=F32) + seen
        ranks.append(jnp.sum((count - 1.0) * part, axis=0, keepdims=True))
        seen = count[:, LANES - 1 :]
    rank = jnp.concatenate(ranks, axis=1).astype(jnp.int32)
    slot = lax.broadcasted_iota(jnp.int32, (cap, obs_rows), 0)
    ranked = jnp.where(slot == rank, 1.0, 0.0).astype(BF16).reshape(cap // TILE, TILE, obs_rows)
    for copy in copies[1:]:
        copy.wait()
    start = foot_ref[0:1, :]
    meta = jnp.concatenate(
        [
            lax.div(start, cols).astype(F32),
            lax.rem(start, cols).astype(F32),
            weights_ref[...].astype(F32),
            jnp.zeros((META - 2 - weights_ref.shape[0], obs_rows), F32),
        ],
        axis=0,
    ).astype(BF16)
    obs = obs_ref[...]
    lane = lax.broadcasted_iota(jnp.int32, (META, LANES), 1)
    count = min(512, devices * cap) // cap
    for first in range(0, devices, count):
        parts = []
        for d in range(first, first + count):
            mine = jnp.broadcast_to(member[d : d + 1], (TILE, obs_rows)).astype(BF16)
            parts.append((ranked * mine[None]).reshape(cap, obs_rows))
        chosen = jnp.concatenate(parts, axis=0)
        feats = jnp.dot(chosen, obs, preferred_element_type=F32).astype(BF16)
        placed = lax.dot_general(
            meta, chosen, (((1,), (1,)), ((), ())), preferred_element_type=F32
        )
        for half in range(feats.shape[1] // LANES):
            piece = feats[:, half * LANES : (half + 1) * LANES].reshape(count, cap, LANES)
            send_ref[first : first + count, half * cap : (half + 1) * cap, :] = piece
        base = send_ref.shape[1] - META
        for chunk in range(count // per):
            values = placed[:, chunk * LANES : (chunk + 1) * LANES]
            turned = [values] + [pltpu.roll(values, k * cap, 1) for k in range(1, per)]
            for own in range(per):
                wide = turned[0]
                for group in range(per):
                    wide = jnp.where(lane // cap == group, turned[(group - own) % per], wide)
                send_ref[first + chunk * per + own, base:, :] = wide.astype(BF16)


def assim_kernel(
    cap,
    step,
    got_ref,
    proj_hbm,
    back_hbm,
    edge_ref,
    inner_ref,
    lon_ref,
    corner_ref,
    proj_ref,
    back_ref,
    sems,
):
    copies = (
        pltpu.make_async_copy(proj_hbm, proj_ref, sems.at[0]),
        pltpu.make_async_copy(back_hbm, back_ref, sems.at[1]),
    )
    for copy in copies:
        copy.start()
    devices, depth, _ = got_ref.shape
    rows, cols, chans = back_ref.shape
    cells = rows * cols
    feats = proj_ref.shape[0]
    per = LANES // cap
    halves = feats // LANES
    lane = lax.broadcasted_iota(jnp.int32, (META, LANES), 1)
    cell = lax.broadcasted_iota(jnp.int32, (cells, LANES), 0)
    total = jnp.zeros((cells, feats), F32)
    for pair in range(0, devices // per, 2):
        maps = []
        blocks = []
        for chunk in (pair, pair + 1):
            meta = got_ref[chunk * per, depth - META :, :].astype(F32)
            for group in range(1, per):
                other = got_ref[chunk * per + group, depth - META :, :].astype(F32)
                meta = jnp.where(lane // cap == group, other, meta)
            start = (meta[0:1] * cols + meta[1:2]).astype(jnp.int32)
            away = cell - start
            away = jnp.where(away < 0, away + cells, away)
            amount = jnp.zeros((cells, LANES), F32)
            for entry in range(4):
                amount = jnp.where(away == entry * step, meta[2 + entry : 3 + entry], amount)
            maps.append(amount.astype(BF16))
            block = got_ref[chunk * per : (chunk + 1) * per]
            blocks.append(
                jnp.concatenate(
                    [
                        block[:, half * cap : (half + 1) * cap, :].reshape(LANES, LANES)
                        for half in range(halves)
                    ],
                    axis=1,
                )
            )
        total = total + jnp.dot(
            jnp.concatenate(maps, axis=1),
            jnp.concatenate(blocks, axis=0),
            preferred_element_type=F32,
        )
    for copy in copies:
        copy.wait()
    assim = jnp.dot(total.astype(BF16), proj_ref[...], preferred_element_type=F32)
    state = back_ref[...].astype(F32) + assim.reshape(rows, cols, chans)
    state = state.astype(BF16)
    edge_ref[...] = state[rows - SHIFT :]
    inner_ref[...] = state[: rows - SHIFT]
    lon_ref[...] = state[:, cols - EDGE :, :]
    corner_ref[...] = state[rows - SHIFT :, cols - EDGE :, :]


def gelu(half):
    inner = half * (1.5957691216057308 + 0.285419265090401 * (half * half))
    return half + half * jnp.tanh(inner)


def put(wide_ref, row, start, value):
    for g in range(wide_ref.shape[0]):
        wide_ref[g, row, start : start + value.shape[0], :] = value[:, g * LANES : (g + 1) * LANES]


def shifted(wide_ref, taps_in, base, row, target):
    for g in range(wide_ref.shape[0]):
        for r in range(TAPS + 1):
            columns = pl.ds(base + r, TILE, stride=2)
            taps_in[g, r, target] = wide_ref[g, row, columns, :]


def convolve(taps_in, taps_ref, tap_ref, spread_ref, layer, g, first, count):
    lanes = pl.ds(pl.multiple_of(g * LANES, LANES), LANES)
    for k in range(TAPS * TAPS):
        tap_ref[k] = jnp.broadcast_to(taps_ref[k, layer : layer + 1, lanes], (SUBLANES, LANES))
    for p in range(2):
        halves = []
        for h in range(0, TILE, SUBLANES):
            total = None
            for b in range(TAPS):
                seen = taps_in[g, p + b, first : first + count + TAPS - 1, h : h + SUBLANES, :]
                for a in range(TAPS):
                    term = seen[a : a + count] * tap_ref[a * TAPS + b]
                    total = term if total is None else total + term
            halves.append(total)
        total = jnp.concatenate(halves, axis=1)
        spread_ref[p, first : first + count, :, lanes] = total.astype(BF16)


def finish(taps_in, spread_ref, mix_ref, out_ref, layer, first, count):
    chans = mix_ref.shape[1]
    ones = jnp.ones((chans, LANES), BF16)
    for p in range(2):
        spread = spread_ref[p, first : first + count].reshape(count * TILE, chans)
        power = jnp.dot(spread * spread, ones, preferred_element_type=F32)
        scale = 0.5 * lax.rsqrt(power * (1.0 / chans) + 1e-05)
        mixed = jnp.dot(spread, mix_ref[layer], preferred_element_type=F32)
        for g in range(chans // LANES):
            moved = gelu(mixed[:, g * LANES : (g + 1) * LANES] * scale)
            center = taps_in[g, p + HALO, first + HALO : first + HALO + count]
            fresh = center + moved.reshape(count, TILE, LANES)
            for k in range(count):
                out_ref[g, first + k, pl.ds(p, TILE, stride=2), :] = fresh[k]


def row_of(out_ref, y):
    return jnp.concatenate([out_ref[g, y] for g in range(out_ref.shape[0])], axis=1)


def at_last():
    return lax.axis_index("lat") == lax.axis_size("lat") - 1


def inner_kernel(
    shrink,
    layer,
    edge_in,
    inner_in,
    lon_in,
    taps_ref,
    mix_ref,
    inner_ref,
    lon_ref,
    near_ref,
    wide_ref,
    taps_in,
    tap_ref,
    spread_ref,
    out_ref,
):
    cols = edge_in.shape[1]
    groups = wide_ref.shape[0]
    own = inner_in.shape[0] - (HALO if shrink else 0)
    rows = own + SHIFT
    count = rows - SHIFT
    side = cols if shrink else 0
    main = 0 if shrink else EDGE
    base = 0 if shrink else EDGE - SHIFT

    def load(ref, place, y):
        put(wide_ref, place, main, ref[y].astype(F32))
        put(wide_ref, place, side, lon_in[place].astype(F32))
        shifted(wide_ref, taps_in, base, place, place)

    @pl.loop(0, SHIFT, unroll=2)
    def _(y):
        load(edge_in, y if shrink else own + y, y)

    @pl.loop(0, own, unroll=2)
    def _(y):
        load(inner_in, y + SHIFT if shrink else y, y)

    near = rows - SHIFT if shrink else 0
    near_ref[...] = taps_in[:, :, near : near + SHIFT]

    @pl.loop(0, groups)
    def _(g):
        convolve(taps_in, taps_ref, tap_ref, spread_ref, layer, g, 0, count)

    finish(taps_in, spread_ref, mix_ref, out_ref, layer, 0, count)
    edge = slice(cols - EDGE, cols) if shrink else slice(0, EDGE)

    @pl.loop(0, count, unroll=2)
    def _(y):
        value = row_of(out_ref, y)
        inner_ref[y] = value.astype(BF16)
        lon_ref[y] = value[edge].astype(BF16)

    if not shrink:

        @pl.when(at_last())
        def _():
            taps_in[:, :, rows:] = jnp.zeros((groups, TAPS + 1, HALO, TILE, LANES), F32)

            @pl.loop(0, groups)
            def _(g):
                convolve(taps_in, taps_ref, tap_ref, spread_ref, layer, g, count, HALO)

            finish(taps_in, spread_ref, mix_ref, out_ref, layer, count, HALO)

        for k in range(HALO):
            value = row_of(out_ref, count + k)
            inner_ref[count + k] = value.astype(BF16)
            lon_ref[count + k] = value[edge].astype(BF16)


def edge_kernel(
    shrink,
    final,
    layer,
    inner_in,
    lon_in,
    lat_in,
    corner_in,
    near_ref,
    inner_new,
    lon_new,
    taps_ref,
    mix_ref,
    *refs,
):
    if final:
        state_ref, wide_ref, taps_in, tap_ref, spread_ref, out_ref = refs
    else:
        edge_ref, lon_ref, corner_ref, wide_ref, taps_in, tap_ref, spread_ref, out_ref = refs
    cols = lat_in.shape[1]
    groups = wide_ref.shape[0]
    side = cols if shrink else 0
    main = 0 if shrink else EDGE
    base = 0 if shrink else EDGE - SHIFT
    last = at_last()
    top = lax.axis_index("lat") == 0
    own = SHIFT if not shrink else 0
    for k in range(SHIFT):
        value, beside = lat_in[k].astype(F32), corner_in[k].astype(F32)
        if not shrink:
            value, beside = jnp.where(top, 0.0, value), jnp.where(top, 0.0, beside)
        elif k < HALO:
            rows = lon_in.shape[0] - HALO
            kept = inner_in.shape[0] - HALO
            value = jnp.where(last, inner_in[kept + k].astype(F32), value)
            beside = jnp.where(last, lon_in[rows + k].astype(F32), beside)
        else:
            value, beside = jnp.where(last, 0.0, value), jnp.where(last, 0.0, beside)
        put(wide_ref, k, main, value)
        put(wide_ref, k, side, beside)
        shifted(wide_ref, taps_in, base, k, k if not shrink else k + SHIFT)
    taps_in[:, :, own : own + SHIFT] = near_ref[...]

    @pl.loop(0, groups)
    def _(g):
        convolve(taps_in, taps_ref, tap_ref, spread_ref, layer, g, 0, SHIFT)

    finish(taps_in, spread_ref, mix_ref, out_ref, layer, 0, SHIFT)
    kept = inner_new.shape[0]
    for k in range(SHIFT):
        value = row_of(out_ref, k)
        if final:
            state_ref[kept + k] = value.astype(BF16)
            continue
        if not shrink and k < HALO:
            value = jnp.where(top, 0.0, value)
        value = value.astype(F32)
        edge = value[cols - EDGE :] if shrink else value[:EDGE]
        edge_ref[k] = value.astype(BF16)
        corner_ref[k] = edge.astype(BF16)
        lon_ref[kept + k if shrink else k] = edge.astype(BF16)
    if final:
        state_ref[0:kept] = inner_new[...]
    elif shrink:
        lon_ref[0:kept] = lon_new[...]
    else:
        lon_ref[SHIFT : SHIFT + kept] = lon_new[...]


def call(kernel, out_shape, inputs, scratch=(), limit=VMEM_LIMIT, space=None, work=0):
    whole = pl.BlockSpec(memory_space=pltpu.VMEM)
    single = isinstance(out_shape, jax.ShapeDtypeStruct)
    spaces = space or (pltpu.VMEM,) * len(inputs)
    return pl.pallas_call(
        kernel,
        out_shape=out_shape,
        in_specs=[pl.BlockSpec(memory_space=s) for s in spaces],
        out_specs=whole if single else [whole] * len(out_shape),
        scratch_shapes=list(scratch),
        compiler_params=pltpu.CompilerParams(vmem_limit_bytes=limit),
        cost_estimate=pl.CostEstimate(flops=work, bytes_accessed=0, transcendentals=0),
    )(*inputs)


def held(*shape):
    return jax.ShapeDtypeStruct(shape, BF16)


def scratch_of(groups, seen, made, cols, chans):
    return (
        pltpu.VMEM((groups, seen, cols + EDGE, LANES), F32),
        pltpu.VMEM((groups, TAPS + 1, seen, TILE, LANES), F32),
        pltpu.VMEM((TAPS * TAPS, SUBLANES, LANES), F32),
        pltpu.VMEM((2, made, TILE, chans), BF16),
        pltpu.VMEM((groups, made, cols, LANES), F32),
    )


def layer(state, lon_out, corner_out, taps, mix, number, shrink, final):
    edge, inner = state
    lat_in, lon_in, corner_in = exchange((edge, lon_out, corner_out), not shrink)
    cols, chans = edge.shape[1:]
    groups = chans // LANES
    rows = inner.shape[0] + SHIFT - (HALO if shrink else 0)
    spare = 0 if shrink else HALO
    made = rows - SHIFT + spare
    inner_new, lon_new, near = call(
        functools.partial(inner_kernel, shrink, number),
        (
            held(made, cols, chans),
            held(made, EDGE, chans),
            jax.ShapeDtypeStruct((groups, TAPS + 1, SHIFT, TILE, LANES), F32),
        ),
        (edge, inner, lon_in, taps, mix),
        scratch_of(groups, rows + spare, made, cols, chans),
        work=made * cols * chans * WORK,
    )
    if final:
        outs = held(made + SHIFT, cols, chans)
    else:
        outs = (
            held(SHIFT, cols, chans),
            held(made + SHIFT, EDGE, chans),
            held(SHIFT, EDGE, chans),
        )
    outs = call(
        functools.partial(edge_kernel, shrink, final, number),
        outs,
        (inner, lon_in, lat_in, corner_in, near, inner_new, lon_new, taps, mix),
        scratch_of(groups, 2 * SHIFT, SHIFT, cols, chans),
        work=SHIFT * cols * chans * WORK,
    )
    if final:
        return outs
    edge, lon_out, corner_out = outs
    return (edge, inner_new), lon_out, corner_out


def exchange(pieces, forward):
    lat, lon, corner = pieces
    count_lat = lax.axis_size("lat")
    count_lon = lax.axis_size("lon")
    along = [(i, (i + 1) % count_lat) for i in range(count_lat)]
    around = [(j, (j + 1) % count_lon) for j in range(count_lon)]
    across = [
        (i * count_lon + j, ni * count_lon + nj) for i, ni in along for j, nj in around
    ]
    if not forward:
        along, around, across = ([(t, s) for s, t in p] for p in (along, around, across))
    lon = lax.ppermute(lon, "lon", around)
    lat = lax.ppermute(lat, "lat", along)
    corner = lax.ppermute(corner, ("lat", "lon"), across)
    return lat, lon, corner


def body(
    background, observations, destination, footprint, weights, obs_proj, depth_w, point_w, gains
):
    rows, cols, chans = background.shape
    devices = lax.axis_size("lat") * lax.axis_size("lon")
    obs_rows, feats = observations.shape
    cap = 2 * obs_rows // devices
    depth = cap * (feats // LANES) + META
    foot_count = footprint.shape[1]
    send = call(
        functools.partial(pack_kernel, cap, cols),
        jax.ShapeDtypeStruct((devices, depth, LANES), BF16),
        (destination.T, footprint.T, weights.T, observations),
        (
            pltpu.VMEM((1, obs_rows), jnp.int32),
            pltpu.VMEM((foot_count, obs_rows), jnp.int32),
            pltpu.VMEM((foot_count, obs_rows), BF16),
            pltpu.VMEM((obs_rows, feats), BF16),
            pltpu.SemaphoreType.DMA((4,)),
        ),
        PACK_LIMIT,
        (pltpu.HBM,) * 4,
    )
    got = lax.all_to_all(send, ("lat", "lon"), split_axis=0, concat_axis=0, tiled=True)
    layers = depth_w.shape[0]
    taps = depth_w.transpose(1, 2, 0, 3).reshape(TAPS * TAPS, layers, chans)
    mix = (gains[:, :, None] * point_w.astype(F32)).astype(BF16)
    got, mix = lax.optimization_barrier((got, mix))
    edge, inner, lon_out, corner_out = call(
        functools.partial(assim_kernel, cap, cols + 1),
        (
            held(SHIFT, cols, chans),
            held(rows - SHIFT, cols, chans),
            held(rows, EDGE, chans),
            held(SHIFT, EDGE, chans),
        ),
        (got, obs_proj, background),
        (
            pltpu.VMEM(obs_proj.shape, BF16),
            pltpu.VMEM(background.shape, BF16),
            pltpu.SemaphoreType.DMA((2,)),
        ),
        PACK_LIMIT,
        (pltpu.VMEM, pltpu.HBM, pltpu.HBM),
    )
    state = (edge, inner)
    for n in range(layers - 1):
        state, lon_out, corner_out = layer(
            state, lon_out, corner_out, taps, mix, n, n % 2 == 1, False
        )
    n = layers - 1
    return layer(state, lon_out, corner_out, taps, mix, n, n % 2 == 1, True)


def solution(mesh):
    placed = (
        P("lat", "lon", None),
        P(("lat", "lon"), None),
        P(("lat", "lon"), None),
        P(("lat", "lon"), None),
        P(("lat", "lon"), None),
        P(),
        P(),
        P(),
        P(),
    )
    return jax.shard_map(
        body, mesh=mesh, in_specs=placed, out_specs=P("lat", "lon", None), check_vma=False
    )
```

profile of v0, /device:TPU:0, one launch (start us, length us, event | category | flops | bytes accessed | tf_op | source)
XLA Modules:
  0.0 96.1 jit_solution(6740686517431933407)
XLA Ops:
  0.0 4.7 %shard_map.91 = bf16[32,136,128]{2,1,0:T(8,128)(2,1)} custom-call(s32[1,1024]{1,0:T(1,128)} %bitcast.16, s32[4,1024]{1,0:T(4,128)} %bitcast.14, bf16[4,1024]{1,0:T(4,128)(2,1)} %bitcast.15, bf16[1024,256]{1,0:T(8,128)(2,1)} %obs_hbm.1), custom_call_target="tpu_custom_call" | custom-call | tf_op jit(solution)/shard_map/pallas_call | solution.py:373
  4.7 7.4 %all-to-all-start = ((bf16[32,136,128]{2,1,0:T(8,128)(2,1)}), bf16[32,136,128]{2,1,0:T(8,128)(2,1)}, u32[]{:S(2)}, u32[]{:S(2)}) async-start(bf16[32,136,128]{2,1,0:T(8,128)(2,1)} %shard_map.91), calls=%async_computation | async-start | bytes 2228224 | tf_op jit(solution)/shard_map/all_to_all | solution.py:478
  12.2 2.1 %multiply_convert_fusion.mix_ref = bf16[4,512,512]{2,1,0:T(8,128)(2,1)S(1)} fusion(bf16[4,512,512]{2,1,0:T(8,128)(2,1)} %param.16, f32[4,512]{1,0:T(4,128)S(1)} %copy-done.4), kind=kLoop, calls=%fused_computation | loop fusion | flops 3145728 | bytes 4202496 | tf_op jit(solution)/shard_map/convert_element_type | solution.py:481
  14.3 26.8 %all-to-all-done.got_ref = bf16[32,136,128]{2,1,0:T(8,128)(2,1)} async-done(((bf16[32,136,128]{2,1,0:T(8,128)(2,1)}), bf16[32,136,128]{2,1,0:T(8,128)(2,1)}, u32[]{:S(2)}, u32[]{:S(2)}) %all-to-all-start) | async-done | bytes 1114144 | tf_op jit(solution)/shard_map/all_to_all | solution.py:478
  41.1 4.4 %shard_map.92 = (bf16[6,32,512]{2,1,0:T(8,128)(2,1)}, bf16[10,32,512]{2,1,0:T(8,128)(2,1)}, bf16[16,8,512]{2,1,0:T(8,128)(2,1)}, bf16[6,8,512]{2,1,0:T(8,128)(2,1)}) custom-call(bf16[32,136,128]{2,1,0:T(8,128)(2,1)} %all-to-all-done.got_ref, bf16[256,512]{1,0:T(8,128)(2,1)} %proj_hbm.1, bf16[16,32,512]{2,1,0:T(8,128)(2,1)} %back_hbm.1), custom_call_target="tpu_custom_call" | custom-call | tf_op jit(solution)/shard_map/pallas_call | solution.py:373
  47.3 4.7 %collective-permute-done.lon_in = bf16[16,8,512]{2,1,0:T(8,128)(2,1)S(1)} collective-permute-done((bf16[16,8,512]{2,1,0:T(8,128)(2,1)}, bf16[16,8,512]{2,1,0:T(8,128)(2,1)S(1)}, u32[]{:S(2)}, u32[]{:S(2)}) %collective-permute-start) | collective-permute-done | bytes 131104 | tf_op jit(solution)/shard_map/ppermute | solution.py:449
  52.0 1.0 %copy-done.1 = bf16[10,32,512]{2,1,0:T(8,128)(2,1)S(1)} copy-done((bf16[10,32,512]{2,1,0:T(8,128)(2,1)S(1)}, bf16[10,32,512]{2,1,0:T(8,128)(2,1)}, u32[]{:S(2)}) %copy-start.1) | copy-done | bytes 327704
  53.0 0.9 copy-done.3
  53.9 3.2 %shard_map.93 = (bf16[13,32,512]{2,1,0:T(8,128)(2,1)S(1)}, bf16[13,8,512]{2,1,0:T(8,128)(2,1)S(1)}, f32[4,8,6,16,128]{4,3,2,1,0:T(8,128)S(1)}) custom-call(bf16[6,32,512]{2,1,0:T(8,128)(2,1)S(1)} %copy-done.3, bf16[10,32,512]{2,1,0:T(8,128)(2,1)S(1)} %copy-done.1, bf16[16,8,512]{2,1,0:T(8,128)(2,1)S(1)} %collective-permute-done.lon_in, ...), custom_call_target="tpu_custom_call" | custom-call | flops 1064960000 | tf_op jit(solution)/shard_map/pallas_call | solution.py:373
  57.2 2.6 %shard_map.94 = (bf16[6,32,512]{2,1,0:T(8,128)(2,1)S(1)}, bf16[19,8,512]{2,1,0:T(8,128)(2,1)S(1)}, bf16[6,8,512]{2,1,0:T(8,128)(2,1)S(1)}) custom-call(bf16[10,32,512]{2,1,0:T(8,128)(2,1)S(1)} %copy-done.2, bf16[16,8,512]{2,1,0:T(8,128)(2,1)S(1)} %collective-permute-done.lon_in, bf16[6,32,512]{2,1,0:T(8,128)(2,1)S(1)} %collective-permute-done.1.lat_in, ...), custom_call_target="tpu_custom_call" | custom-call | flops 491520000 | tf_op jit(solution)/shard_map/pallas_call | solution.py:373
  59.9 1.8 %collective-permute-start.4 = (bf16[6,32,512]{2,1,0:T(8,128)(2,1)S(1)}, bf16[6,32,512]{2,1,0:T(8,128)(2,1)S(1)}, u32[]{:S(2)}, u32[]{:S(2)}) collective-permute-start(bf16[6,32,512]{2,1,0:T(8,128)(2,1)S(1)} %get-tuple-element.42.edge_in), channel_id=1, source_target_pairs={{8,0},{16,8},{24,16},{0,24},{9,1},{17,9},{25,17},{1,25},{10,2},{18... | collective-permute-start | bytes 589832 | tf_op jit(solution)/shard_map/ppermute | solution.py:450
  61.7 0.9 collective-permute-done.3.lon_in
  62.6 4.1 %shard_map.95 = (bf16[10,32,512]{2,1,0:T(8,128)(2,1)S(1)}, bf16[10,8,512]{2,1,0:T(8,128)(2,1)S(1)}, f32[4,8,6,16,128]{4,3,2,1,0:T(8,128)S(1)}) custom-call(bf16[6,32,512]{2,1,0:T(8,128)(2,1)S(1)} %get-tuple-element.42.edge_in, bf16[13,32,512]{2,1,0:T(8,128)(2,1)S(1)} %get-tuple-element.37.inner_new.inner_in, ...), custom_call_target="tpu_custom_call" | custom-call | flops 819200000 | tf_op jit(solution)/shard_map/pallas_call | solution.py:373
  66.8 1.5 %collective-permute-done.5.corner_in = bf16[6,8,512]{2,1,0:T(8,128)(2,1)S(1)} collective-permute-done((bf16[6,8,512]{2,1,0:T(8,128)(2,1)S(1)}, bf16[6,8,512]{2,1,0:T(8,128)(2,1)S(1)}, u32[]{:S(2)}, u32[]{:S(2)}) %collective-permute-start.5) | collective-permute-done | bytes 49184 | tf_op jit(solution)/shard_map/ppermute | solution.py:451
  68.3 2.6 %shard_map.96 = (bf16[6,32,512]{2,1,0:T(8,128)(2,1)S(1)}, bf16[16,8,512]{2,1,0:T(8,128)(2,1)S(1)}, bf16[6,8,512]{2,1,0:T(8,128)(2,1)S(1)}) custom-call(bf16[13,32,512]{2,1,0:T(8,128)(2,1)S(1)} %get-tuple-element.37.inner_new.inner_in, bf16[19,8,512]{2,1,0:T(8,128)(2,1)S(1)} %collective-permute-done.3.lon_in, ...), custom_call_target="tpu_custom_call" | custom-call | flops 491520000 | tf_op jit(solution)/shard_map/pallas_call | solution.py:373
  71.5 0.9 collective-permute-start.8
  72.4 4.7 %collective-permute-done.6.lon_in = bf16[16,8,512]{2,1,0:T(8,128)(2,1)S(1)} collective-permute-done((bf16[16,8,512]{2,1,0:T(8,128)(2,1)S(1)}, bf16[16,8,512]{2,1,0:T(8,128)(2,1)S(1)}, u32[]{:S(2)}, u32[]{:S(2)}) %collective-permute-start.6) | collective-permute-done | bytes 131104 | tf_op jit(solution)/shard_map/ppermute | solution.py:449
  77.1 3.2 %shard_map.97 = (bf16[13,32,512]{2,1,0:T(8,128)(2,1)S(1)}, bf16[13,8,512]{2,1,0:T(8,128)(2,1)S(1)}, f32[4,8,6,16,128]{4,3,2,1,0:T(8,128)S(1)}) custom-call(bf16[6,32,512]{2,1,0:T(8,128)(2,1)S(1)} %get-tuple-element.47.edge_in, bf16[10,32,512]{2,1,0:T(8,128)(2,1)S(1)} %get-tuple-element.45.inner_new.inner_in, ...), custom_call_target="tpu_custom_call" | custom-call | flops 1064960000 | tf_op jit(solution)/shard_map/pallas_call | solution.py:373
  80.4 2.6 %shard_map.98 = (bf16[6,32,512]{2,1,0:T(8,128)(2,1)S(1)}, bf16[19,8,512]{2,1,0:T(8,128)(2,1)S(1)}, bf16[6,8,512]{2,1,0:T(8,128)(2,1)S(1)}) custom-call(bf16[10,32,512]{2,1,0:T(8,128)(2,1)S(1)} %get-tuple-element.45.inner_new.inner_in, bf16[16,8,512]{2,1,0:T(8,128)(2,1)S(1)} %collective-permute-done.6.lon_in, ...), custom_call_target="tpu_custom_call" | custom-call | flops 491520000 | tf_op jit(solution)/shard_map/pallas_call | solution.py:373
  83.0 2.4 %collective-permute-start.9 = (bf16[19,8,512]{2,1,0:T(8,128)(2,1)S(1)}, bf16[19,8,512]{2,1,0:T(8,128)(2,1)S(1)}, u32[]{:S(2)}, u32[]{:S(2)}) collective-permute-start(bf16[19,8,512]{2,1,0:T(8,128)(2,1)S(1)} %get-tuple-element.53), channel_id=1, source_target_pairs={{1,0},{2,1},{3,2},{4,3},{5,4},{6,5},{7,6},{0,7},{9,8},{10,9},{11,1... | collective-permute-start | bytes 466952 | tf_op jit(solution)/shard_map/ppermute | solution.py:449
  85.4 1.6 %collective-permute-start.10 = (bf16[6,32,512]{2,1,0:T(8,128)(2,1)S(1)}, bf16[6,32,512]{2,1,0:T(8,128)(2,1)S(1)}, u32[]{:S(2)}, u32[]{:S(2)}) collective-permute-start(bf16[6,32,512]{2,1,0:T(8,128)(2,1)S(1)} %get-tuple-element.54.edge_in), channel_id=1, source_target_pairs={{8,0},{16,8},{24,16},{0,24},{9,1},{17,9},{25,17},{1,25},{10,2},{18... | collective-permute-start | bytes 589832 | tf_op jit(solution)/shard_map/ppermute | solution.py:450
  87.0 1.1 %collective-permute-done.9.lon_in = bf16[19,8,512]{2,1,0:T(8,128)(2,1)S(1)} collective-permute-done((bf16[19,8,512]{2,1,0:T(8,128)(2,1)S(1)}, bf16[19,8,512]{2,1,0:T(8,128)(2,1)S(1)}, u32[]{:S(2)}, u32[]{:S(2)}) %collective-permute-start.9) | collective-permute-done | bytes 155680 | tf_op jit(solution)/shard_map/ppermute | solution.py:449
  88.1 4.1 %shard_map.99 = (bf16[10,32,512]{2,1,0:T(8,128)(2,1)S(1)}, bf16[10,8,512]{2,1,0:T(8,128)(2,1)S(1)}, f32[4,8,6,16,128]{4,3,2,1,0:T(8,128)S(1)}) custom-call(bf16[6,32,512]{2,1,0:T(8,128)(2,1)S(1)} %get-tuple-element.54.edge_in, bf16[13,32,512]{2,1,0:T(8,128)(2,1)S(1)} %get-tuple-element.49.inner_new.inner_in, ...), custom_call_target="tpu_custom_call" | custom-call | flops 819200000 | tf_op jit(solution)/shard_map/pallas_call | solution.py:373
  92.8 3.4 %shard_map.100 = bf16[16,32,512]{2,1,0:T(8,128)(2,1)} custom-call(bf16[13,32,512]{2,1,0:T(8,128)(2,1)S(1)} %get-tuple-element.49.inner_new.inner_in, bf16[19,8,512]{2,1,0:T(8,128)(2,1)S(1)} %collective-permute-done.9.lon_in, bf16[6,32,512]{2,1,0:T(8,128)(2,1)S(1)} %collective-permute-done.10.lat_in, ...), custom_call_target="tpu_custom_call" | custom-call | flops 491520000 | tf_op jit(solution)/shard_map/pallas_call | solution.py:373
  (23 shorter events, 3.0 us)
Async XLA Ops:
  0.0 12.2 %copy-start.4 = (f32[4,512]{1,0:T(4,128)S(1)}, f32[4,512]{1,0:T(4,128)}, u32[]{:S(2)}) copy-start(f32[4,512]{1,0:T(4,128)} %param.17) | copy-start | bytes 24580
  4.7 36.4 %all-to-all-start = ((bf16[32,136,128]{2,1,0:T(8,128)(2,1)}), bf16[32,136,128]{2,1,0:T(8,128)(2,1)}, u32[]{:S(2)}, u32[]{:S(2)}) async-start(bf16[32,136,128]{2,1,0:T(8,128)(2,1)} %shard_map.91), calls=%async_computation | async-start | bytes 2228224 | tf_op jit(solution)/shard_map/all_to_all | solution.py:478
  12.2 39.9 %copy-start = (f32[4,7,7,512]{3,0,2,1:T(4,128)S(1)}, f32[4,7,7,512]{3,0,2,1:T(4,128)}, u32[]{:S(2)}) copy-start(f32[4,7,7,512]{3,0,2,1:T(4,128)} %param.15) | copy-start | bytes 1204228
  45.6 6.5 %collective-permute-start = (bf16[16,8,512]{2,1,0:T(8,128)(2,1)}, bf16[16,8,512]{2,1,0:T(8,128)(2,1)S(1)}, u32[]{:S(2)}, u32[]{:S(2)}) collective-permute-start(bf16[16,8,512]{2,1,0:T(8,128)(2,1)} %get-tuple-element.35), channel_id=1, source_target_pairs={{0,1},{1,2},{2,3},{3,4},{4,5},{5,6},{6,7},{7,0},{8,9},{9,10},{10,1... | collective-permute-start | bytes 393224 | tf_op jit(solution)/shard_map/ppermute | solution.py:449
  45.6 11.6 %collective-permute-start.1 = (bf16[6,32,512]{2,1,0:T(8,128)(2,1)}, bf16[6,32,512]{2,1,0:T(8,128)(2,1)S(1)}, u32[]{:S(2)}, u32[]{:S(2)}) collective-permute-start(bf16[6,32,512]{2,1,0:T(8,128)(2,1)} %get-tuple-element.33.edge_in), channel_id=1, source_target_pairs={{0,8},{8,16},{16,24},{24,0},{1,9},{9,17},{17,25},{25,1},{2,10},{10... | collective-permute-start | bytes 589832 | tf_op jit(solution)/shard_map/ppermute | solution.py:450
  46.5 10.7 %collective-permute-start.2 = (bf16[6,8,512]{2,1,0:T(8,128)(2,1)}, bf16[6,8,512]{2,1,0:T(8,128)(2,1)S(1)}, u32[]{:S(2)}, u32[]{:S(2)}) collective-permute-start(bf16[6,8,512]{2,1,0:T(8,128)(2,1)} %get-tuple-element.38), channel_id=1, source_target_pairs={{0,9},{1,10},{2,11},{3,12},{4,13},{5,14},{6,15},{7,8},{8,17},{9,18... | collective-permute-start | bytes 147464 | tf_op jit(solution)/shard_map/ppermute | solution.py:451
  52.0 1.0 %copy-start.1 = (bf16[10,32,512]{2,1,0:T(8,128)(2,1)S(1)}, bf16[10,32,512]{2,1,0:T(8,128)(2,1)}, u32[]{:S(2)}) copy-start(bf16[10,32,512]{2,1,0:T(8,128)(2,1)} %get-tuple-element.34.inner_in) | copy-start | bytes 983044
  53.0 0.9 copy-start.3
  53.9 3.3 %copy-start.2 = (bf16[10,32,512]{2,1,0:T(8,128)(2,1)S(1)}, bf16[10,32,512]{2,1,0:T(8,128)(2,1)}, u32[]{:S(2)}) copy-start(bf16[10,32,512]{2,1,0:T(8,128)(2,1)} %get-tuple-element.34.inner_in) | copy-start | bytes 983044
  59.8 2.8 %collective-permute-start.3 = (bf16[19,8,512]{2,1,0:T(8,128)(2,1)S(1)}, bf16[19,8,512]{2,1,0:T(8,128)(2,1)S(1)}, u32[]{:S(2)}, u32[]{:S(2)}) collective-permute-start(bf16[19,8,512]{2,1,0:T(8,128)(2,1)S(1)} %get-tuple-element.41), channel_id=1, source_target_pairs={{1,0},{2,1},{3,2},{4,3},{5,4},{6,5},{7,6},{0,7},{9,8},{10,9},{11,1... | collective-permute-start | bytes 466952 | tf_op jit(solution)/shard_map/ppermute | solution.py:449
  59.9 8.4 %collective-permute-start.4 = (bf16[6,32,512]{2,1,0:T(8,128)(2,1)S(1)}, bf16[6,32,512]{2,1,0:T(8,128)(2,1)S(1)}, u32[]{:S(2)}, u32[]{:S(2)}) collective-permute-start(bf16[6,32,512]{2,1,0:T(8,128)(2,1)S(1)} %get-tuple-element.42.edge_in), channel_id=1, source_target_pairs={{8,0},{16,8},{24,16},{0,24},{9,1},{17,9},{25,17},{1,25},{10,2},{18... | collective-permute-start | bytes 589832 | tf_op jit(solution)/shard_map/ppermute | solution.py:450
  61.7 6.5 %collective-permute-start.5 = (bf16[6,8,512]{2,1,0:T(8,128)(2,1)S(1)}, bf16[6,8,512]{2,1,0:T(8,128)(2,1)S(1)}, u32[]{:S(2)}, u32[]{:S(2)}) collective-permute-start(bf16[6,8,512]{2,1,0:T(8,128)(2,1)S(1)} %get-tuple-element.43), channel_id=1, source_target_pairs={{9,0},{10,1},{11,2},{12,3},{13,4},{14,5},{15,6},{8,7},{17,8},{18,9... | collective-permute-start | bytes 147464 | tf_op jit(solution)/shard_map/ppermute | solution.py:451
  70.9 6.2 %collective-permute-start.6 = (bf16[16,8,512]{2,1,0:T(8,128)(2,1)S(1)}, bf16[16,8,512]{2,1,0:T(8,128)(2,1)S(1)}, u32[]{:S(2)}, u32[]{:S(2)}) collective-permute-start(bf16[16,8,512]{2,1,0:T(8,128)(2,1)S(1)} %get-tuple-element.48), channel_id=1, source_target_pairs={{0,1},{1,2},{2,3},{3,4},{4,5},{5,6},{6,7},{7,0},{8,9},{9,10},{10,1... | collective-permute-start | bytes 393224 | tf_op jit(solution)/shard_map/ppermute | solution.py:449
  70.9 9.4 %collective-permute-start.7 = (bf16[6,32,512]{2,1,0:T(8,128)(2,1)S(1)}, bf16[6,32,512]{2,1,0:T(8,128)(2,1)S(1)}, u32[]{:S(2)}, u32[]{:S(2)}) collective-permute-start(bf16[6,32,512]{2,1,0:T(8,128)(2,1)S(1)} %get-tuple-element.47.edge_in), channel_id=1, source_target_pairs={{0,8},{8,16},{16,24},{24,0},{1,9},{9,17},{17,25},{25,1},{2,10},{10... | collective-permute-start | bytes 589832 | tf_op jit(solution)/shard_map/ppermute | solution.py:450
  71.5 8.8 %collective-permute-start.8 = (bf16[6,8,512]{2,1,0:T(8,128)(2,1)S(1)}, bf16[6,8,512]{2,1,0:T(8,128)(2,1)S(1)}, u32[]{:S(2)}, u32[]{:S(2)}) collective-permute-start(bf16[6,8,512]{2,1,0:T(8,128)(2,1)S(1)} %get-tuple-element.50), channel_id=1, source_target_pairs={{0,9},{1,10},{2,11},{3,12},{4,13},{5,14},{6,15},{7,8},{8,17},{9,18... | collective-permute-start | bytes 147464 | tf_op jit(solution)/shard_map/ppermute | solution.py:451
  83.0 5.2 %collective-permute-start.9 = (bf16[19,8,512]{2,1,0:T(8,128)(2,1)S(1)}, bf16[19,8,512]{2,1,0:T(8,128)(2,1)S(1)}, u32[]{:S(2)}, u32[]{:S(2)}) collective-permute-start(bf16[19,8,512]{2,1,0:T(8,128)(2,1)S(1)} %get-tuple-element.53), channel_id=1, source_target_pairs={{1,0},{2,1},{3,2},{4,3},{5,4},{6,5},{7,6},{0,7},{9,8},{10,9},{11,1... | collective-permute-start | bytes 466952 | tf_op jit(solution)/shard_map/ppermute | solution.py:449
  85.4 7.4 %collective-permute-start.10 = (bf16[6,32,512]{2,1,0:T(8,128)(2,1)S(1)}, bf16[6,32,512]{2,1,0:T(8,128)(2,1)S(1)}, u32[]{:S(2)}, u32[]{:S(2)}) collective-permute-start(bf16[6,32,512]{2,1,0:T(8,128)(2,1)S(1)} %get-tuple-element.54.edge_in), channel_id=1, source_target_pairs={{8,0},{16,8},{24,16},{0,24},{9,1},{17,9},{25,17},{1,25},{10,2},{18... | collective-permute-start | bytes 589832 | tf_op jit(solution)/shard_map/ppermute | solution.py:450
  87.0 5.3 %collective-permute-start.11 = (bf16[6,8,512]{2,1,0:T(8,128)(2,1)S(1)}, bf16[6,8,512]{2,1,0:T(8,128)(2,1)S(1)}, u32[]{:S(2)}, u32[]{:S(2)}) collective-permute-start(bf16[6,8,512]{2,1,0:T(8,128)(2,1)S(1)} %get-tuple-element.55), channel_id=1, source_target_pairs={{9,0},{10,1},{11,2},{12,3},{13,4},{14,5},{15,6},{8,7},{17,8},{18,9... | collective-permute-start | bytes 147464 | tf_op jit(solution)/shard_map/ppermute | solution.py:451
where the time goes:
time: 96.5 us; the launch traced here: 96.1 us
  waiting for transfers between devices  40.2 us (42%)
  Pallas kernels  35.1 us (36%)
  starting transfers between devices  16.6 us (17%)
  other arithmetic  2.11 us (2%)
  local copies, waits for them, and re-layouts  1.91 us (2%)
    pallas_call x10, Pallas kernels, call(): pl.pallas_call(kernel, out_shape=out_shape, in_specs=[pl.BlockSpec(memory...  35.1 us
    all_to_all x1, waiting for transfers between devices, body(): lax.all_to_all(send, ('lat', 'lon'), split_axis=0, concat_axis=0, tiled=T...  26.8 us
    ppermute x4, waiting for transfers between devices, exchange(): lon = lax.ppermute(lon, 'lon', around)  11.4 us
    all_to_all x1, starting transfers between devices, body(): lax.all_to_all(send, ('lat', 'lon'), split_axis=0, concat_axis=0, tiled=T...  7.42 us
    ppermute x4, starting transfers between devices, exchange(): lat = lax.ppermute(lat, 'lat', along)  4.89 us
    ppermute x4, starting transfers between devices, exchange(): lon = lax.ppermute(lon, 'lon', around)  2.58 us
    convert_element_type x1, other arithmetic, body(): mix = (gains[:, :, None] * point_w.astype(F32)).astype(BF16)  2.11 us
  transfers between devices with their start and end apart: 13, of which 7 were waited for; matrix products, arithmetic and copies ran while one was open for 2% of the time, Pallas kernels for 15%

commit v1 on v0

--- a/solution.py
+++ b/solution.py
@@ -14,7 +14,6 @@
 SHIFT = 2 * HALO
 EDGE = 8
 TILE = 16
-SUBLANES = 8
 WORK = 5000
 VMEM_LIMIT = 24 * 1024 * 1024
 PACK_LIMIT = 58 * 1024 * 1024
@@ -95,26 +94,20 @@
                 send_ref[first + chunk * per + own, base:, :] = wide.astype(BF16)
 
 
-def assim_kernel(
-    cap,
-    step,
-    got_ref,
-    proj_hbm,
-    back_hbm,
-    edge_ref,
-    inner_ref,
-    lon_ref,
-    corner_ref,
-    proj_ref,
-    back_ref,
-    sems,
-):
+def fetch_kernel(proj_hbm, back_hbm, proj_ref, back_ref, sems):
     copies = (
         pltpu.make_async_copy(proj_hbm, proj_ref, sems.at[0]),
         pltpu.make_async_copy(back_hbm, back_ref, sems.at[1]),
     )
     for copy in copies:
         copy.start()
+    for copy in copies:
+        copy.wait()
+
+
+def assim_kernel(
+    cap, step, got_ref, proj_ref, back_ref, edge_ref, inner_ref, lon_ref, corner_ref, wide_ref
+):
     devices, depth, _ = got_ref.shape
     rows, cols, chans = back_ref.shape
     cells = rows * cols
@@ -154,14 +147,17 @@
             jnp.concatenate(blocks, axis=0),
             preferred_element_type=F32,
         )
-    for copy in copies:
-        copy.wait()
     assim = jnp.dot(total.astype(BF16), proj_ref[...], preferred_element_type=F32)
     state = back_ref[...].astype(F32) + assim.reshape(rows, cols, chans)
+    for g in range(chans // LANES):
+        wide_ref[g] = state[:, cols - EDGE :, lanes_of(g)].reshape(rows * EDGE, LANES)
     state = state.astype(BF16)
     edge_ref[...] = state[rows - SHIFT :]
     inner_ref[...] = state[: rows - SHIFT]
-    lon_ref[...] = state[:, cols - EDGE :, :]
+    for x in range(SHIFT):
+        for g in range(chans // LANES):
+            column = wide_ref[g, pl.ds(EDGE - SHIFT + x, rows, stride=EDGE), :]
+            lon_ref[x, :, lanes_of(g)] = column.astype(BF16)
     corner_ref[...] = state[rows - SHIFT :, cols - EDGE :, :]
 
 
@@ -179,25 +175,24 @@
     for g in range(wide_ref.shape[0]):
         for r in range(TAPS + 1):
             columns = pl.ds(base + r, TILE, stride=2)
-            taps_in[g, r, target] = wide_ref[g, row, columns, :]
+            taps_in[g, r, target] = wide_ref[g, row, columns, :].astype(BF16)
 
 
 def convolve(taps_in, taps_ref, tap_ref, spread_ref, layer, g, first, count):
     lanes = pl.ds(pl.multiple_of(g * LANES, LANES), LANES)
     for k in range(TAPS * TAPS):
-        tap_ref[k] = jnp.broadcast_to(taps_ref[k, layer : layer + 1, lanes], (SUBLANES, LANES))
+        row = taps_ref[k, layer : layer + 1, lanes]
+        tap_ref[k] = jnp.broadcast_to(row, (TILE, LANES)).astype(BF16)
     for p in range(2):
-        halves = []
-        for h in range(0, TILE, SUBLANES):
-            total = None
-            for b in range(TAPS):
-                seen = taps_in[g, p + b, first : first + count + TAPS - 1, h : h + SUBLANES, :]
-                for a in range(TAPS):
-                    term = seen[a : a + count] * tap_ref[a * TAPS + b]
-                    total = term if total is None else total + term
-            halves.append(total)
-        total = jnp.concatenate(halves, axis=1)
-        spread_ref[p, first : first + count, :, lanes] = total.astype(BF16)
+        total = None
+        for b in range(TAPS):
+            seen = taps_in[g, p + b, first : first + count + TAPS - 1]
+            part = None
+            for a in range(TAPS):
+                term = seen[a : a + count] * tap_ref[a * TAPS + b]
+                part = term if part is None else part + term
+            total = part if total is None else total + part
+        spread_ref[p, first : first + count, :, lanes] = total
 
 
 def finish(taps_in, spread_ref, mix_ref, out_ref, layer, first, count):
@@ -210,7 +205,7 @@
         mixed = jnp.dot(spread, mix_ref[layer], preferred_element_type=F32)
         for g in range(chans // LANES):
             moved = gelu(mixed[:, g * LANES : (g + 1) * LANES] * scale)
-            center = taps_in[g, p + HALO, first + HALO : first + HALO + count]
+            center = taps_in[g, p + HALO, first + HALO : first + HALO + count].astype(F32)
             fresh = center + moved.reshape(count, TILE, LANES)
             for k in range(count):
                 out_ref[g, first + k, pl.ds(p, TILE, stride=2), :] = fresh[k]
@@ -218,6 +213,15 @@
 
 def row_of(out_ref, y):
     return jnp.concatenate([out_ref[g, y] for g in range(out_ref.shape[0])], axis=1)
+
+
+def flat(ref):
+    groups, rows, width, lanes = ref.shape
+    return ref.reshape(groups, rows * width, lanes)
+
+
+def lanes_of(g):
+    return slice(g * LANES, (g + 1) * LANES)
 
 
 def at_last():
@@ -243,16 +247,21 @@
 ):
     cols = edge_in.shape[1]
     groups = wide_ref.shape[0]
+    width = wide_ref.shape[2]
     own = inner_in.shape[0] - (HALO if shrink else 0)
     rows = own + SHIFT
     count = rows - SHIFT
-    side = cols if shrink else 0
     main = 0 if shrink else EDGE
     base = 0 if shrink else EDGE - SHIFT
+    side = cols if shrink else base
+
+    for g in range(groups):
+        for x in range(SHIFT):
+            column = lon_in[x, 0:rows, lanes_of(g)].astype(F32)
+            flat(wide_ref)[g, pl.ds(side + x, rows, stride=width), :] = column
 
     def load(ref, place, y):
         put(wide_ref, place, main, ref[y].astype(F32))
-        put(wide_ref, place, side, lon_in[place].astype(F32))
         shifted(wide_ref, taps_in, base, place, place)
 
     @pl.loop(0, SHIFT, unroll=2)
@@ -271,19 +280,22 @@
         convolve(taps_in, taps_ref, tap_ref, spread_ref, layer, g, 0, count)
 
     finish(taps_in, spread_ref, mix_ref, out_ref, layer, 0, count)
-    edge = slice(cols - EDGE, cols) if shrink else slice(0, EDGE)
+    edge = cols - SHIFT if shrink else 0
+    above = 0 if shrink else SHIFT
+    for g in range(groups):
+        for x in range(SHIFT):
+            column = flat(out_ref)[g, pl.ds(edge + x, count, stride=cols), :]
+            lon_ref[g, x, above : above + count, :] = column
 
     @pl.loop(0, count, unroll=2)
     def _(y):
-        value = row_of(out_ref, y)
-        inner_ref[y] = value.astype(BF16)
-        lon_ref[y] = value[edge].astype(BF16)
+        inner_ref[y] = row_of(out_ref, y).astype(BF16)
 
     if not shrink:
 
         @pl.when(at_last())
         def _():
-            taps_in[:, :, rows:] = jnp.zeros((groups, TAPS + 1, HALO, TILE, LANES), F32)
+            taps_in[:, :, rows:] = jnp.zeros((groups, TAPS + 1, HALO, TILE, LANES), BF16)
 
             @pl.loop(0, groups)
             def _(g):
@@ -292,9 +304,7 @@
             finish(taps_in, spread_ref, mix_ref, out_ref, layer, count, HALO)
 
         for k in range(HALO):
-            value = row_of(out_ref, count + k)
-            inner_ref[count + k] = value.astype(BF16)
-            lon_ref[count + k] = value[edge].astype(BF16)
+            inner_ref[count + k] = row_of(out_ref, count + k).astype(BF16)
 
 
 def edge_kernel(
@@ -313,26 +323,33 @@
     *refs,
 ):
     if final:
-        state_ref, wide_ref, taps_in, tap_ref, spread_ref, out_ref = refs
+        state_ref, wide_ref, taps_in, tap_ref, spread_ref, out_ref, spare_ref, mix_lon = refs
     else:
-        edge_ref, lon_ref, corner_ref, wide_ref, taps_in, tap_ref, spread_ref, out_ref = refs
+        edge_ref, lon_ref, corner_ref = refs[:3]
+        wide_ref, taps_in, tap_ref, spread_ref, out_ref, spare_ref, mix_lon = refs[3:]
     cols = lat_in.shape[1]
     groups = wide_ref.shape[0]
+    main = 0 if shrink else EDGE
     side = cols if shrink else 0
-    main = 0 if shrink else EDGE
     base = 0 if shrink else EDGE - SHIFT
     last = at_last()
     top = lax.axis_index("lat") == 0
     own = SHIFT if not shrink else 0
+    if shrink:
+        for g in range(groups):
+            for k in range(2):
+                spare = lon_in[SHIFT + k, :, lanes_of(g)].astype(F32)
+                spare_ref[g, k * TILE : (k + 1) * TILE, :] = spare
     for k in range(SHIFT):
         value, beside = lat_in[k].astype(F32), corner_in[k].astype(F32)
         if not shrink:
             value, beside = jnp.where(top, 0.0, value), jnp.where(top, 0.0, beside)
         elif k < HALO:
-            rows = lon_in.shape[0] - HALO
             kept = inner_in.shape[0] - HALO
             value = jnp.where(last, inner_in[kept + k].astype(F32), value)
-            beside = jnp.where(last, lon_in[rows + k].astype(F32), beside)
+            beside = beside[:SHIFT]
+            extra = [spare_ref[g, pl.ds(k, SHIFT, stride=HALO), :] for g in range(groups)]
+            beside = jnp.where(last, jnp.concatenate(extra, axis=1), beside)
         else:
             value, beside = jnp.where(last, 0.0, value), jnp.where(last, 0.0, beside)
         put(wide_ref, k, main, value)
@@ -346,24 +363,38 @@
 
     finish(taps_in, spread_ref, mix_ref, out_ref, layer, 0, SHIFT)
     kept = inner_new.shape[0]
+    if final:
+        for k in range(SHIFT):
+            state_ref[kept + k] = row_of(out_ref, k).astype(BF16)
+        state_ref[0:kept] = inner_new[...]
+        return
+
     for k in range(SHIFT):
         value = row_of(out_ref, k)
-        if final:
-            state_ref[kept + k] = value.astype(BF16)
-            continue
         if not shrink and k < HALO:
             value = jnp.where(top, 0.0, value)
-        value = value.astype(F32)
-        edge = value[cols - EDGE :] if shrink else value[:EDGE]
         edge_ref[k] = value.astype(BF16)
-        corner_ref[k] = edge.astype(BF16)
-        lon_ref[kept + k if shrink else k] = edge.astype(BF16)
-    if final:
-        state_ref[0:kept] = inner_new[...]
-    elif shrink:
-        lon_ref[0:kept] = lon_new[...]
-    else:
-        lon_ref[SHIFT : SHIFT + kept] = lon_new[...]
+        corner_ref[k] = (value[cols - EDGE :] if shrink else value[:EDGE]).astype(BF16)
+    edge = cols - SHIFT if shrink else 0
+    place = TILE - SHIFT if shrink else 0
+    for g in range(groups):
+        for x in range(SHIFT):
+            column = flat(out_ref)[g, pl.ds(edge + x, SHIFT, stride=cols), :]
+            if not shrink:
+                outside = lax.broadcasted_iota(jnp.int32, (SHIFT, LANES), 0) < HALO
+                column = jnp.where(jnp.logical_and(top, outside), 0.0, column)
+            mix_lon[g, x] = lon_new[g, x]
+            mix_lon[g, x, place : place + SHIFT, :] = column
+            lon_ref[x, :, lanes_of(g)] = mix_lon[g, x].astype(BF16)
+    if not shrink:
+        for k in range(HALO):
+            value = inner_new[kept - HALO + k, 0:TILE, :].astype(F32)
+            for g in range(groups):
+                spare_ref[g, pl.ds(k, SHIFT, stride=HALO), :] = value[:SHIFT, lanes_of(g)]
+        for g in range(groups):
+            for k in range(2):
+                spare = spare_ref[g, k * TILE : (k + 1) * TILE, :]
+                lon_ref[SHIFT + k, :, lanes_of(g)] = spare.astype(BF16)
 
 
 def call(kernel, out_shape, inputs, scratch=(), limit=VMEM_LIMIT, space=None, work=0):
@@ -388,8 +419,8 @@
 def scratch_of(groups, seen, made, cols, chans):
     return (
         pltpu.VMEM((groups, seen, cols + EDGE, LANES), F32),
-        pltpu.VMEM((groups, TAPS + 1, seen, TILE, LANES), F32),
-        pltpu.VMEM((TAPS * TAPS, SUBLANES, LANES), F32),
+        pltpu.VMEM((groups, TAPS + 1, seen, TILE, LANES), BF16),
+        pltpu.VMEM((TAPS * TAPS, TILE, LANES), BF16),
         pltpu.VMEM((2, made, TILE, chans), BF16),
         pltpu.VMEM((groups, made, cols, LANES), F32),
     )
@@ -407,8 +438,8 @@
         functools.partial(inner_kernel, shrink, number),
         (
             held(made, cols, chans),
-            held(made, EDGE, chans),
-            jax.ShapeDtypeStruct((groups, TAPS + 1, SHIFT, TILE, LANES), F32),
+            jax.ShapeDtypeStruct((groups, SHIFT, rows, LANES), F32),
+            held(groups, TAPS + 1, SHIFT, TILE, LANES),
         ),
         (edge, inner, lon_in, taps, mix),
         scratch_of(groups, rows + spare, made, cols, chans),
@@ -419,14 +450,18 @@
     else:
         outs = (
             held(SHIFT, cols, chans),
-            held(made + SHIFT, EDGE, chans),
+            held(SHIFT if shrink else EDGE, rows, chans),
             held(SHIFT, EDGE, chans),
         )
     outs = call(
         functools.partial(edge_kernel, shrink, final, number),
         outs,
         (inner, lon_in, lat_in, corner_in, near, inner_new, lon_new, taps, mix),
-        scratch_of(groups, 2 * SHIFT, SHIFT, cols, chans),
+        scratch_of(groups, 2 * SHIFT, SHIFT, cols, chans)
+        + (
+            pltpu.VMEM((groups, 2 * TILE, LANES), F32),
+            pltpu.VMEM((groups, SHIFT, rows, LANES), F32),
+        ),
         work=SHIFT * cols * chans * WORK,
     )
     if final:
@@ -479,23 +514,24 @@
     layers = depth_w.shape[0]
     taps = depth_w.transpose(1, 2, 0, 3).reshape(TAPS * TAPS, layers, chans)
     mix = (gains[:, :, None] * point_w.astype(F32)).astype(BF16)
-    got, mix = lax.optimization_barrier((got, mix))
+    proj, back = call(
+        fetch_kernel,
+        (held(*obs_proj.shape), held(*background.shape)),
+        (obs_proj, background),
+        (pltpu.SemaphoreType.DMA((2,)),),
+        space=(pltpu.HBM, pltpu.HBM),
+    )
+    got, mix, proj, back = lax.optimization_barrier((got, mix, proj, back))
     edge, inner, lon_out, corner_out = call(
         functools.partial(assim_kernel, cap, cols + 1),
         (
             held(SHIFT, cols, chans),
             held(rows - SHIFT, cols, chans),
-            held(rows, EDGE, chans),
+            held(SHIFT, rows, chans),
             held(SHIFT, EDGE, chans),
         ),
-        (got, obs_proj, background),
-        (
-            pltpu.VMEM(obs_proj.shape, BF16),
-            pltpu.VMEM(background.shape, BF16),
-            pltpu.SemaphoreType.DMA((2,)),
-        ),
-        PACK_LIMIT,
-        (pltpu.VMEM, pltpu.HBM, pltpu.HBM),
+        (got, proj, back),
+        (pltpu.VMEM((chans // LANES, rows * EDGE, LANES), F32),),
     )
     state = (edge, inner)
     for n in range(layers - 1):

time: 96.5 us -> 90.3 us (0.936)
  Pallas kernels: 35.1 us -> 30.6 us
  local copies, waits for them, and re-layouts: 1.91 us -> 0.02 us
    pallas_call x10 -> x11, Pallas kernels: 35.1 us -> 30.6 us  [call(): pl.pallas_call(kernel, out_shape=out_shape, in_specs=[pl.BlockSpec(memory...]
    unnamed x10 -> x8, local copies, waits for them, and re-layouts: 1.91 us -> 0.02 us
    ppermute x4, waiting for transfers between devices: 0.46 us -> 1.81 us  [exchange(): lat = lax.ppermute(lat, 'lat', along)]
    ppermute x4, waiting for transfers between devices: 11.4 us -> 10.4 us  [exchange(): lon = lax.ppermute(lon, 'lon', around)]
  transfers between devices with their start and end apart: 13 -> 13, of which waited for: 7 -> 8; matrix products, arithmetic and copies ran while one was open for 2% -> 2% of each run, Pallas kernels for 15% -> 15%
where the time goes in v1:
time: 90.3 us; the launch traced here: 90 us
  waiting for transfers between devices  40.8 us (45%)
  Pallas kernels  30.6 us (34%)
  starting transfers between devices  16.2 us (18%)
  other arithmetic  2.1 us (2%)
    pallas_call x11, Pallas kernels, call(): pl.pallas_call(kernel, out_shape=out_shape, in_specs=[pl.BlockSpec(memory...  30.6 us
    all_to_all x1, waiting for transfers between devices, body(): lax.all_to_all(send, ('lat', 'lon'), split_axis=0, concat_axis=0, tiled=T...  26.7 us
    ppermute x4, waiting for transfers between devices, exchange(): lon = lax.ppermute(lon, 'lon', around)  10.4 us
    all_to_all x1, starting transfers between devices, body(): lax.all_to_all(send, ('lat', 'lon'), split_axis=0, concat_axis=0, tiled=T...  7.42 us
    ppermute x4, starting transfers between devices, exchange(): lat = lax.ppermute(lat, 'lat', along)  4.94 us
    ppermute x4, starting transfers between devices, exchange(): lon = lax.ppermute(lon, 'lon', around)  2.48 us
    convert_element_type x1, other arithmetic, body(): mix = (gains[:, :, None] * point_w.astype(F32)).astype(BF16)  2.1 us
    ppermute x4, waiting for transfers between devices, exchange(): corner = lax.ppermute(corner, ('lat', 'lon'), across)  1.92 us
  transfers between devices with their start and end apart: 13, of which 8 were waited for; matrix products, arithmetic and copies ran while one was open for 2% of the time, Pallas kernels for 15%

profile of v1, /device:TPU:0, one launch (start us, length us, event | category | flops | bytes accessed | tf_op | source)
XLA Modules:
  0.0 90.0 jit_solution(13046045480188804681)
XLA Ops:
  0.0 4.8 %shard_map.91 = bf16[32,136,128]{2,1,0:T(8,128)(2,1)} custom-call(s32[1,1024]{1,0:T(1,128)} %bitcast.16, s32[4,1024]{1,0:T(4,128)} %bitcast.14, bf16[4,1024]{1,0:T(4,128)(2,1)} %bitcast.15, bf16[1024,256]{1,0:T(8,128)(2,1)} %obs_hbm.1), custom_call_target="tpu_custom_call" | custom-call | tf_op jit(solution)/shard_map/pallas_call | solution.py:404
  4.8 7.4 %all-to-all-start = ((bf16[32,136,128]{2,1,0:T(8,128)(2,1)}), bf16[32,136,128]{2,1,0:T(8,128)(2,1)}, u32[]{:S(2)}, u32[]{:S(2)}) async-start(bf16[32,136,128]{2,1,0:T(8,128)(2,1)} %shard_map.91), calls=%async_computation | async-start | bytes 2228224 | tf_op jit(solution)/shard_map/all_to_all | solution.py:513
  12.3 2.1 %multiply_convert_fusion.mix_ref = bf16[4,512,512]{2,1,0:T(8,128)(2,1)S(1)} fusion(bf16[4,512,512]{2,1,0:T(8,128)(2,1)} %param.16, f32[4,512]{1,0:T(4,128)S(1)} %copy-done.3), kind=kLoop, calls=%fused_computation | loop fusion | flops 3145728 | bytes 4202496 | tf_op jit(solution)/shard_map/convert_element_type | solution.py:516
  14.5 26.7 %all-to-all-done.got_ref = bf16[32,136,128]{2,1,0:T(8,128)(2,1)} async-done(((bf16[32,136,128]{2,1,0:T(8,128)(2,1)}), bf16[32,136,128]{2,1,0:T(8,128)(2,1)}, u32[]{:S(2)}, u32[]{:S(2)}) %all-to-all-start) | async-done | bytes 1114144 | tf_op jit(solution)/shard_map/all_to_all | solution.py:513
  41.2 3.5 %shard_map.93 = (bf16[6,32,512]{2,1,0:T(8,128)(2,1)S(1)}, bf16[10,32,512]{2,1,0:T(8,128)(2,1)S(1)}, bf16[6,16,512]{2,1,0:T(8,128)(2,1)S(1)}, bf16[6,8,512]{2,1,0:T(8,128)(2,1)S(1)}) custom-call(bf16[32,136,128]{2,1,0:T(8,128)(2,1)} %all-to-all-done.got_ref, bf16[256,512]{1,0:T(8,128)(2,1)S(1)} %get-tuple-element.39.proj_ref, ...), custom_call_target="tpu_custom_call" | custom-call | tf_op jit(solution)/shard_map/pallas_call | solution.py:404
  44.8 0.8 collective-permute-start.1
  45.6 0.9 collective-permute-start.2
  46.5 4.1 %collective-permute-done.lon_in = bf16[6,16,512]{2,1,0:T(8,128)(2,1)S(1)} collective-permute-done((bf16[6,16,512]{2,1,0:T(8,128)(2,1)S(1)}, bf16[6,16,512]{2,1,0:T(8,128)(2,1)S(1)}, u32[]{:S(2)}, u32[]{:S(2)}) %collective-permute-start) | collective-permute-done | bytes 98336 | tf_op jit(solution)/shard_map/ppermute | solution.py:484
  50.6 3.3 %shard_map.94 = (bf16[13,32,512]{2,1,0:T(8,128)(2,1)S(1)}, f32[4,6,16,128]{3,2,1,0:T(8,128)S(1)}, bf16[4,8,6,16,128]{4,3,2,1,0:T(8,128)(2,1)S(1)}) custom-call(bf16[6,32,512]{2,1,0:T(8,128)(2,1)S(1)} %get-tuple-element.41.edge_in, bf16[10,32,512]{2,1,0:T(8,128)(2,1)S(1)} %get-tuple-element.42.inner_in, bf16[6,16,512]{2,1,0:T(8,128)(2,1)S(1)} %collective-permute-done.lon_in, ...), custom_call_target="tpu_custom_call" | custom-call | flops 1064960000 | tf_op jit(solution)/shard_map/pallas_call | solution.py:404
  53.9 2.0 %shard_map.95 = (bf16[6,32,512]{2,1,0:T(8,128)(2,1)S(1)}, bf16[8,16,512]{2,1,0:T(8,128)(2,1)S(1)}, bf16[6,8,512]{2,1,0:T(8,128)(2,1)S(1)}) custom-call(bf16[10,32,512]{2,1,0:T(8,128)(2,1)S(1)} %get-tuple-element.42.inner_in, bf16[6,16,512]{2,1,0:T(8,128)(2,1)S(1)} %collective-permute-done.lon_in, bf16[6,32,512]{2,1,0:T(8,128)(2,1)S(1)} %collective-permute-done.1.lat_in, ...), custom_call_target="tpu_custom_call" | custom-call | flops 491520000 | tf_op jit(solution)/shard_map/pallas_call | solution.py:404
  56.3 1.7 %collective-permute-start.4 = (bf16[6,32,512]{2,1,0:T(8,128)(2,1)S(1)}, bf16[6,32,512]{2,1,0:T(8,128)(2,1)S(1)}, u32[]{:S(2)}, u32[]{:S(2)}) collective-permute-start(bf16[6,32,512]{2,1,0:T(8,128)(2,1)S(1)} %get-tuple-element.50.edge_in), channel_id=1, source_target_pairs={{8,0},{16,8},{24,16},{0,24},{9,1},{17,9},{25,17},{1,25},{10,2},{18... | collective-permute-start | bytes 589832 | tf_op jit(solution)/shard_map/ppermute | solution.py:485
  58.3 0.6 collective-permute-done.3.lon_in
  58.8 3.4 %shard_map.96 = (bf16[10,32,512]{2,1,0:T(8,128)(2,1)S(1)}, f32[4,6,16,128]{3,2,1,0:T(8,128)S(1)}, bf16[4,8,6,16,128]{4,3,2,1,0:T(8,128)(2,1)S(1)}) custom-call(bf16[6,32,512]{2,1,0:T(8,128)(2,1)S(1)} %get-tuple-element.50.edge_in, bf16[13,32,512]{2,1,0:T(8,128)(2,1)S(1)} %get-tuple-element.45.inner_new.inner_in, ...), custom_call_target="tpu_custom_call" | custom-call | flops 819200000 | tf_op jit(solution)/shard_map/pallas_call | solution.py:404
  62.2 1.9 %collective-permute-done.5.corner_in = bf16[6,8,512]{2,1,0:T(8,128)(2,1)S(1)} collective-permute-done((bf16[6,8,512]{2,1,0:T(8,128)(2,1)S(1)}, bf16[6,8,512]{2,1,0:T(8,128)(2,1)S(1)}, u32[]{:S(2)}, u32[]{:S(2)}) %collective-permute-start.5) | collective-permute-done | bytes 49184 | tf_op jit(solution)/shard_map/ppermute | solution.py:486
  64.4 2.0 %shard_map.97 = (bf16[6,32,512]{2,1,0:T(8,128)(2,1)S(1)}, bf16[6,16,512]{2,1,0:T(8,128)(2,1)S(1)}, bf16[6,8,512]{2,1,0:T(8,128)(2,1)S(1)}) custom-call(bf16[13,32,512]{2,1,0:T(8,128)(2,1)S(1)} %get-tuple-element.45.inner_new.inner_in, bf16[8,16,512]{2,1,0:T(8,128)(2,1)S(1)} %collective-permute-done.3.lon_in, ...), custom_call_target="tpu_custom_call" | custom-call | flops 491520000 | tf_op jit(solution)/shard_map/pallas_call | solution.py:404
  66.5 0.6 collective-permute-start.7
  67.2 5.1 %collective-permute-done.6.lon_in = bf16[6,16,512]{2,1,0:T(8,128)(2,1)S(1)} collective-permute-done((bf16[6,16,512]{2,1,0:T(8,128)(2,1)S(1)}, bf16[6,16,512]{2,1,0:T(8,128)(2,1)S(1)}, u32[]{:S(2)}, u32[]{:S(2)}) %collective-permute-start.6) | collective-permute-done | bytes 98336 | tf_op jit(solution)/shard_map/ppermute | solution.py:484
  72.3 3.3 %shard_map.98 = (bf16[13,32,512]{2,1,0:T(8,128)(2,1)S(1)}, f32[4,6,16,128]{3,2,1,0:T(8,128)S(1)}, bf16[4,8,6,16,128]{4,3,2,1,0:T(8,128)(2,1)S(1)}) custom-call(bf16[6,32,512]{2,1,0:T(8,128)(2,1)S(1)} %get-tuple-element.55.edge_in, bf16[10,32,512]{2,1,0:T(8,128)(2,1)S(1)} %get-tuple-element.53.inner_new.inner_in, ...), custom_call_target="tpu_custom_call" | custom-call | flops 1064960000 | tf_op jit(solution)/shard_map/pallas_call | solution.py:404
  75.6 2.0 %shard_map.99 = (bf16[6,32,512]{2,1,0:T(8,128)(2,1)S(1)}, bf16[8,16,512]{2,1,0:T(8,128)(2,1)S(1)}, bf16[6,8,512]{2,1,0:T(8,128)(2,1)S(1)}) custom-call(bf16[10,32,512]{2,1,0:T(8,128)(2,1)S(1)} %get-tuple-element.53.inner_new.inner_in, bf16[6,16,512]{2,1,0:T(8,128)(2,1)S(1)} %collective-permute-done.6.lon_in, ...), custom_call_target="tpu_custom_call" | custom-call | flops 491520000 | tf_op jit(solution)/shard_map/pallas_call | solution.py:404
  77.7 2.0 %collective-permute-start.9 = (bf16[8,16,512]{2,1,0:T(8,128)(2,1)S(1)}, bf16[8,16,512]{2,1,0:T(8,128)(2,1)S(1)}, u32[]{:S(2)}, u32[]{:S(2)}) collective-permute-start(bf16[8,16,512]{2,1,0:T(8,128)(2,1)S(1)} %get-tuple-element.61), channel_id=1, source_target_pairs={{1,0},{2,1},{3,2},{4,3},{5,4},{6,5},{7,6},{0,7},{9,8},{10,9},{11,1... | collective-permute-start | bytes 393224 | tf_op jit(solution)/shard_map/ppermute | solution.py:484
  79.7 1.8 %collective-permute-start.10 = (bf16[6,32,512]{2,1,0:T(8,128)(2,1)S(1)}, bf16[6,32,512]{2,1,0:T(8,128)(2,1)S(1)}, u32[]{:S(2)}, u32[]{:S(2)}) collective-permute-start(bf16[6,32,512]{2,1,0:T(8,128)(2,1)S(1)} %get-tuple-element.62.edge_in), channel_id=1, source_target_pairs={{8,0},{16,8},{24,16},{0,24},{9,1},{17,9},{25,17},{1,25},{10,2},{18... | collective-permute-start | bytes 589832 | tf_op jit(solution)/shard_map/ppermute | solution.py:485
  82.2 3.4 %shard_map.100 = (bf16[10,32,512]{2,1,0:T(8,128)(2,1)S(1)}, f32[4,6,16,128]{3,2,1,0:T(8,128)S(1)}, bf16[4,8,6,16,128]{4,3,2,1,0:T(8,128)(2,1)S(1)}) custom-call(bf16[6,32,512]{2,1,0:T(8,128)(2,1)S(1)} %get-tuple-element.62.edge_in, bf16[13,32,512]{2,1,0:T(8,128)(2,1)S(1)} %get-tuple-element.57.inner_new.inner_in, ...), custom_call_target="tpu_custom_call" | custom-call | flops 819200000 | tf_op jit(solution)/shard_map/pallas_call | solution.py:404
  85.6 1.6 %collective-permute-done.10.lat_in = bf16[6,32,512]{2,1,0:T(8,128)(2,1)S(1)} collective-permute-done((bf16[6,32,512]{2,1,0:T(8,128)(2,1)S(1)}, bf16[6,32,512]{2,1,0:T(8,128)(2,1)S(1)}, u32[]{:S(2)}, u32[]{:S(2)}) %collective-permute-start.10) | collective-permute-done | bytes 196640 | tf_op jit(solution)/shard_map/ppermute | solution.py:485
  87.2 2.8 %shard_map.101 = bf16[16,32,512]{2,1,0:T(8,128)(2,1)} custom-call(bf16[13,32,512]{2,1,0:T(8,128)(2,1)S(1)} %get-tuple-element.57.inner_new.inner_in, bf16[8,16,512]{2,1,0:T(8,128)(2,1)S(1)} %collective-permute-done.9.lon_in, bf16[6,32,512]{2,1,0:T(8,128)(2,1)S(1)} %collective-permute-done.10.lat_in, ...), custom_call_target="tpu_custom_call" | custom-call | flops 491520000 | tf_op jit(solution)/shard_map/pallas_call | solution.py:404
  (22 shorter events, 1.9 us)
Async XLA Ops:
  0.0 12.2 %copy-start.2 = (bf16[256,512]{1,0:T(8,128)(2,1)S(1)}, bf16[256,512]{1,0:T(8,128)(2,1)}, u32[]{:S(2)}) copy-start(bf16[256,512]{1,0:T(8,128)(2,1)} %proj_hbm.1) | copy-start | bytes 786436
  0.0 12.2 %copy-start.1 = (bf16[16,32,512]{2,1,0:T(8,128)(2,1)S(1)}, bf16[16,32,512]{2,1,0:T(8,128)(2,1)}, u32[]{:S(2)}) copy-start(bf16[16,32,512]{2,1,0:T(8,128)(2,1)} %back_hbm.1) | copy-start | bytes 1572868
  0.0 12.3 %copy-start.3 = (f32[4,512]{1,0:T(4,128)S(1)}, f32[4,512]{1,0:T(4,128)}, u32[]{:S(2)}) copy-start(f32[4,512]{1,0:T(4,128)} %param.17) | copy-start | bytes 24580
  4.8 36.4 %all-to-all-start = ((bf16[32,136,128]{2,1,0:T(8,128)(2,1)}), bf16[32,136,128]{2,1,0:T(8,128)(2,1)}, u32[]{:S(2)}, u32[]{:S(2)}) async-start(bf16[32,136,128]{2,1,0:T(8,128)(2,1)} %shard_map.91), calls=%async_computation | async-start | bytes 2228224 | tf_op jit(solution)/shard_map/all_to_all | solution.py:513
  12.3 38.2 %copy-start = (f32[4,7,7,512]{3,0,2,1:T(4,128)S(1)}, f32[4,7,7,512]{3,0,2,1:T(4,128)}, u32[]{:S(2)}) copy-start(f32[4,7,7,512]{3,0,2,1:T(4,128)} %param.15) | copy-start | bytes 1204228
  44.7 5.9 %collective-permute-start = (bf16[6,16,512]{2,1,0:T(8,128)(2,1)S(1)}, bf16[6,16,512]{2,1,0:T(8,128)(2,1)S(1)}, u32[]{:S(2)}, u32[]{:S(2)}) collective-permute-start(bf16[6,16,512]{2,1,0:T(8,128)(2,1)S(1)} %get-tuple-element.43), channel_id=1, source_target_pairs={{0,1},{1,2},{2,3},{3,4},{4,5},{5,6},{6,7},{7,0},{8,9},{9,10},{10,1... | collective-permute-start | bytes 294920 | tf_op jit(solution)/shard_map/ppermute | solution.py:484
  44.8 9.2 %collective-permute-start.1 = (bf16[6,32,512]{2,1,0:T(8,128)(2,1)S(1)}, bf16[6,32,512]{2,1,0:T(8,128)(2,1)S(1)}, u32[]{:S(2)}, u32[]{:S(2)}) collective-permute-start(bf16[6,32,512]{2,1,0:T(8,128)(2,1)S(1)} %get-tuple-element.41.edge_in), channel_id=1, source_target_pairs={{0,8},{8,16},{16,24},{24,0},{1,9},{9,17},{17,25},{25,1},{2,10},{10... | collective-permute-start | bytes 589832 | tf_op jit(solution)/shard_map/ppermute | solution.py:485
  45.6 8.3 %collective-permute-start.2 = (bf16[6,8,512]{2,1,0:T(8,128)(2,1)S(1)}, bf16[6,8,512]{2,1,0:T(8,128)(2,1)S(1)}, u32[]{:S(2)}, u32[]{:S(2)}) collective-permute-start(bf16[6,8,512]{2,1,0:T(8,128)(2,1)S(1)} %get-tuple-element.46), channel_id=1, source_target_pairs={{0,9},{1,10},{2,11},{3,12},{4,13},{5,14},{6,15},{7,8},{8,17},{9,18... | collective-permute-start | bytes 147464 | tf_op jit(solution)/shard_map/ppermute | solution.py:486
  55.9 2.9 %collective-permute-start.3 = (bf16[8,16,512]{2,1,0:T(8,128)(2,1)S(1)}, bf16[8,16,512]{2,1,0:T(8,128)(2,1)S(1)}, u32[]{:S(2)}, u32[]{:S(2)}) collective-permute-start(bf16[8,16,512]{2,1,0:T(8,128)(2,1)S(1)} %get-tuple-element.49), channel_id=1, source_target_pairs={{1,0},{2,1},{3,2},{4,3},{5,4},{6,5},{7,6},{0,7},{9,8},{10,9},{11,1... | collective-permute-start | bytes 393224 | tf_op jit(solution)/shard_map/ppermute | solution.py:484
  56.3 8.1 %collective-permute-start.4 = (bf16[6,32,512]{2,1,0:T(8,128)(2,1)S(1)}, bf16[6,32,512]{2,1,0:T(8,128)(2,1)S(1)}, u32[]{:S(2)}, u32[]{:S(2)}) collective-permute-start(bf16[6,32,512]{2,1,0:T(8,128)(2,1)S(1)} %get-tuple-element.50.edge_in), channel_id=1, source_target_pairs={{8,0},{16,8},{24,16},{0,24},{9,1},{17,9},{25,17},{1,25},{10,2},{18... | collective-permute-start | bytes 589832 | tf_op jit(solution)/shard_map/ppermute | solution.py:485
  58.0 6.1 %collective-permute-start.5 = (bf16[6,8,512]{2,1,0:T(8,128)(2,1)S(1)}, bf16[6,8,512]{2,1,0:T(8,128)(2,1)S(1)}, u32[]{:S(2)}, u32[]{:S(2)}) collective-permute-start(bf16[6,8,512]{2,1,0:T(8,128)(2,1)S(1)} %get-tuple-element.51), channel_id=1, source_target_pairs={{9,0},{10,1},{11,2},{12,3},{13,4},{14,5},{15,6},{8,7},{17,8},{18,9... | collective-permute-start | bytes 147464 | tf_op jit(solution)/shard_map/ppermute | solution.py:486
  66.4 5.9 %collective-permute-start.6 = (bf16[6,16,512]{2,1,0:T(8,128)(2,1)S(1)}, bf16[6,16,512]{2,1,0:T(8,128)(2,1)S(1)}, u32[]{:S(2)}, u32[]{:S(2)}) collective-permute-start(bf16[6,16,512]{2,1,0:T(8,128)(2,1)S(1)} %get-tuple-element.56), channel_id=1, source_target_pairs={{0,1},{1,2},{2,3},{3,4},{4,5},{5,6},{6,7},{7,0},{8,9},{9,10},{10,1... | collective-permute-start | bytes 294920 | tf_op jit(solution)/shard_map/ppermute | solution.py:484
  66.5 9.1 %collective-permute-start.7 = (bf16[6,32,512]{2,1,0:T(8,128)(2,1)S(1)}, bf16[6,32,512]{2,1,0:T(8,128)(2,1)S(1)}, u32[]{:S(2)}, u32[]{:S(2)}) collective-permute-start(bf16[6,32,512]{2,1,0:T(8,128)(2,1)S(1)} %get-tuple-element.55.edge_in), channel_id=1, source_target_pairs={{0,8},{8,16},{16,24},{24,0},{1,9},{9,17},{17,25},{25,1},{2,10},{10... | collective-permute-start | bytes 589832 | tf_op jit(solution)/shard_map/ppermute | solution.py:485
  67.1 8.5 %collective-permute-start.8 = (bf16[6,8,512]{2,1,0:T(8,128)(2,1)S(1)}, bf16[6,8,512]{2,1,0:T(8,128)(2,1)S(1)}, u32[]{:S(2)}, u32[]{:S(2)}) collective-permute-start(bf16[6,8,512]{2,1,0:T(8,128)(2,1)S(1)} %get-tuple-element.58), channel_id=1, source_target_pairs={{0,9},{1,10},{2,11},{3,12},{4,13},{5,14},{6,15},{7,8},{8,17},{9,18... | collective-permute-start | bytes 147464 | tf_op jit(solution)/shard_map/ppermute | solution.py:486
  77.7 4.5 %collective-permute-start.9 = (bf16[8,16,512]{2,1,0:T(8,128)(2,1)S(1)}, bf16[8,16,512]{2,1,0:T(8,128)(2,1)S(1)}, u32[]{:S(2)}, u32[]{:S(2)}) collective-permute-start(bf16[8,16,512]{2,1,0:T(8,128)(2,1)S(1)} %get-tuple-element.61), channel_id=1, source_target_pairs={{1,0},{2,1},{3,2},{4,3},{5,4},{6,5},{7,6},{0,7},{9,8},{10,9},{11,1... | collective-permute-start | bytes 393224 | tf_op jit(solution)/shard_map/ppermute | solution.py:484
  79.7 7.5 %collective-permute-start.10 = (bf16[6,32,512]{2,1,0:T(8,128)(2,1)S(1)}, bf16[6,32,512]{2,1,0:T(8,128)(2,1)S(1)}, u32[]{:S(2)}, u32[]{:S(2)}) collective-permute-start(bf16[6,32,512]{2,1,0:T(8,128)(2,1)S(1)} %get-tuple-element.62.edge_in), channel_id=1, source_target_pairs={{8,0},{16,8},{24,16},{0,24},{9,1},{17,9},{25,17},{1,25},{10,2},{18... | collective-permute-start | bytes 589832 | tf_op jit(solution)/shard_map/ppermute | solution.py:485
  81.4 4.2 %collective-permute-start.11 = (bf16[6,8,512]{2,1,0:T(8,128)(2,1)S(1)}, bf16[6,8,512]{2,1,0:T(8,128)(2,1)S(1)}, u32[]{:S(2)}, u32[]{:S(2)}) collective-permute-start(bf16[6,8,512]{2,1,0:T(8,128)(2,1)S(1)} %get-tuple-element.63), channel_id=1, source_target_pairs={{9,0},{10,1},{11,2},{12,3},{13,4},{14,5},{15,6},{8,7},{17,8},{18,9... | collective-permute-start | bytes 147464 | tf_op jit(solution)/shard_map/ppermute | solution.py:486

commit v2 on v1

--- a/solution.py
+++ b/solution.py
@@ -14,6 +14,7 @@
 SHIFT = 2 * HALO
 EDGE = 8
 TILE = 16
+CHUNK = 4
 WORK = 5000
 VMEM_LIMIT = 24 * 1024 * 1024
 PACK_LIMIT = 58 * 1024 * 1024
@@ -147,18 +148,29 @@
             jnp.concatenate(blocks, axis=0),
             preferred_element_type=F32,
         )
-    assim = jnp.dot(total.astype(BF16), proj_ref[...], preferred_element_type=F32)
-    state = back_ref[...].astype(F32) + assim.reshape(rows, cols, chans)
-    for g in range(chans // LANES):
-        wide_ref[g] = state[:, cols - EDGE :, lanes_of(g)].reshape(rows * EDGE, LANES)
-    state = state.astype(BF16)
-    edge_ref[...] = state[rows - SHIFT :]
-    inner_ref[...] = state[: rows - SHIFT]
+    field = total.astype(BF16)
+    for y0 in range(0, rows, CHUNK):
+        assim = jnp.dot(
+            field[y0 * cols : (y0 + CHUNK) * cols], proj_ref[...], preferred_element_type=F32
+        )
+        state = back_ref[y0 : y0 + CHUNK].astype(F32) + assim.reshape(CHUNK, cols, chans)
+        side = state[:, cols - EDGE :, :]
+        for g in range(chans // LANES):
+            wide_ref[g, y0 * EDGE : (y0 + CHUNK) * EDGE] = side[:, :, lanes_of(g)].reshape(
+                CHUNK * EDGE, LANES
+            )
+        state = state.astype(BF16)
+        for k in range(CHUNK):
+            y = y0 + k
+            if y < rows - SHIFT:
+                inner_ref[y] = state[k]
+            else:
+                edge_ref[y - (rows - SHIFT)] = state[k]
+                corner_ref[y - (rows - SHIFT)] = state[k, cols - EDGE :, :]
     for x in range(SHIFT):
         for g in range(chans // LANES):
             column = wide_ref[g, pl.ds(EDGE - SHIFT + x, rows, stride=EDGE), :]
             lon_ref[x, :, lanes_of(g)] = column.astype(BF16)
-    corner_ref[...] = state[rows - SHIFT :, cols - EDGE :, :]
 
 
 def gelu(half):
@@ -179,10 +191,7 @@
 
 
 def convolve(taps_in, taps_ref, tap_ref, spread_ref, layer, g, first, count):
-    lanes = pl.ds(pl.multiple_of(g * LANES, LANES), LANES)
-    for k in range(TAPS * TAPS):
-        row = taps_ref[k, layer : layer + 1, lanes]
-        tap_ref[k] = jnp.broadcast_to(row, (TILE, LANES)).astype(BF16)
+    lanes = load_taps(taps_ref, tap_ref, layer, g)
     for p in range(2):
         total = None
         for b in range(TAPS):
@@ -193,6 +202,31 @@
                 part = term if part is None else part + term
             total = part if total is None else total + part
         spread_ref[p, first : first + count, :, lanes] = total
+
+
+def own_row(shrink, row):
+    if shrink:
+        return row if row < SHIFT else None
+    return row - SHIFT if row >= SHIFT else None
+
+
+def partial_sums(taps_in, tap_ref, g, p, k, rows):
+    total = None
+    for b in range(TAPS):
+        for a in range(TAPS):
+            row = rows(k + a)
+            if row is not None:
+                term = taps_in[g, p + b, row] * tap_ref[a * TAPS + b]
+                total = term if total is None else total + term
+    return total
+
+
+def load_taps(taps_ref, tap_ref, layer, g):
+    lanes = pl.ds(pl.multiple_of(g * LANES, LANES), LANES)
+    for k in range(TAPS * TAPS):
+        row = taps_ref[k, layer : layer + 1, lanes]
+        tap_ref[k] = jnp.broadcast_to(row, (TILE, LANES)).astype(BF16)
+    return lanes
 
 
 def finish(taps_in, spread_ref, mix_ref, out_ref, layer, first, count):
@@ -239,6 +273,7 @@
     inner_ref,
     lon_ref,
     near_ref,
+    part_ref,
     wide_ref,
     taps_in,
     tap_ref,
@@ -273,11 +308,20 @@
         load(inner_in, y + SHIFT if shrink else y, y)
 
     near = rows - SHIFT if shrink else 0
-    near_ref[...] = taps_in[:, :, near : near + SHIFT]
+    centers = near + (HALO if shrink else 0)
+    near_ref[...] = taps_in[:, HALO : HALO + 2, centers : centers + HALO]
+
+    def near_row(row):
+        own_one = own_row(shrink, row)
+        return None if own_one is None else near + own_one
 
     @pl.loop(0, groups)
     def _(g):
         convolve(taps_in, taps_ref, tap_ref, spread_ref, layer, g, 0, count)
+        lanes = pl.ds(pl.multiple_of(g * LANES, LANES), LANES)
+        for p in range(2):
+            for k in range(SHIFT):
+                part_ref[p, k, :, lanes] = partial_sums(taps_in, tap_ref, g, p, k, near_row)
 
     finish(taps_in, spread_ref, mix_ref, out_ref, layer, 0, count)
     edge = cols - SHIFT if shrink else 0
@@ -316,6 +360,7 @@
     lat_in,
     corner_in,
     near_ref,
+    part_ref,
     inner_new,
     lon_new,
     taps_ref,
@@ -355,11 +400,19 @@
         put(wide_ref, k, main, value)
         put(wide_ref, k, side, beside)
         shifted(wide_ref, taps_in, base, k, k if not shrink else k + SHIFT)
-    taps_in[:, :, own : own + SHIFT] = near_ref[...]
+    centers = own + (HALO if shrink else 0)
+    taps_in[:, HALO : HALO + 2, centers : centers + HALO] = near_ref[...]
+
+    def halo_row(row):
+        return row if own_row(shrink, row) is None else None
 
     @pl.loop(0, groups)
     def _(g):
-        convolve(taps_in, taps_ref, tap_ref, spread_ref, layer, g, 0, SHIFT)
+        lanes = load_taps(taps_ref, tap_ref, layer, g)
+        for p in range(2):
+            for k in range(SHIFT):
+                total = partial_sums(taps_in, tap_ref, g, p, k, halo_row)
+                spread_ref[p, k, :, lanes] = total + part_ref[p, k, :, lanes]
 
     finish(taps_in, spread_ref, mix_ref, out_ref, layer, 0, SHIFT)
     kept = inner_new.shape[0]
@@ -434,12 +487,13 @@
     rows = inner.shape[0] + SHIFT - (HALO if shrink else 0)
     spare = 0 if shrink else HALO
     made = rows - SHIFT + spare
-    inner_new, lon_new, near = call(
+    inner_new, lon_new, near, part = call(
         functools.partial(inner_kernel, shrink, number),
         (
             held(made, cols, chans),
             jax.ShapeDtypeStruct((groups, SHIFT, rows, LANES), F32),
-            held(groups, TAPS + 1, SHIFT, TILE, LANES),
+            held(groups, 2, HALO, TILE, LANES),
+            held(2, SHIFT, TILE, chans),
         ),
         (edge, inner, lon_in, taps, mix),
         scratch_of(groups, rows + spare, made, cols, chans),
@@ -456,7 +510,7 @@
     outs = call(
         functools.partial(edge_kernel, shrink, final, number),
         outs,
-        (inner, lon_in, lat_in, corner_in, near, inner_new, lon_new, taps, mix),
+        (inner, lon_in, lat_in, corner_in, near, part, inner_new, lon_new, taps, mix),
         scratch_of(groups, 2 * SHIFT, SHIFT, cols, chans)
         + (
             pltpu.VMEM((groups, 2 * TILE, LANES), F32),

time: 90.3 us -> 90.6 us (level)
  waiting for transfers between devices: 40.8 us -> 38.1 us
  Pallas kernels: 30.6 us -> 33 us
    pallas_call x11, Pallas kernels: 30.6 us -> 33 us  [call(): pl.pallas_call(kernel, out_shape=out_shape, in_specs=[pl.BlockSpec(memory...]
    ppermute x4, waiting for transfers between devices: 10.4 us -> 9.07 us  [exchange(): lon = lax.ppermute(lon, 'lon', around)]
    ppermute x4, waiting for transfers between devices: 1.81 us -> 0.84 us  [exchange(): lat = lax.ppermute(lat, 'lat', along)]
  transfers between devices with their start and end apart: 13 -> 13, of which waited for: 8 -> 7; matrix products, arithmetic and copies ran while one was open for 2% -> 2% of each run, Pallas kernels for 15% -> 19%
where the time goes in v2:
time: 90.6 us; the launch traced here: 90.3 us
  waiting for transfers between devices  38.1 us (42%)
  Pallas kernels  33 us (36%)
  starting transfers between devices  17 us (19%)
  other arithmetic  2.11 us (2%)
    pallas_call x11, Pallas kernels, call(): pl.pallas_call(kernel, out_shape=out_shape, in_specs=[pl.BlockSpec(memory...  33 us
    all_to_all x1, waiting for transfers between devices, body(): lax.all_to_all(send, ('lat', 'lon'), split_axis=0, concat_axis=0, tiled=T...  26.7 us
    ppermute x4, waiting for transfers between devices, exchange(): lon = lax.ppermute(lon, 'lon', around)  9.07 us
    all_to_all x1, starting transfers between devices, body(): lax.all_to_all(send, ('lat', 'lon'), split_axis=0, concat_axis=0, tiled=T...  7.42 us
    ppermute x4, starting transfers between devices, exchange(): lat = lax.ppermute(lat, 'lat', along)  5.54 us
    convert_element_type x1, other arithmetic, body(): mix = (gains[:, :, None] * point_w.astype(F32)).astype(BF16)  2.11 us
    ppermute x4, starting transfers between devices, exchange(): corner = lax.ppermute(corner, ('lat', 'lon'), across)  2.07 us
    ppermute x4, starting transfers between devices, exchange(): lon = lax.ppermute(lon, 'lon', around)  1.92 us
  transfers between devices with their start and end apart: 13, of which 7 were waited for; matrix products, arithmetic and copies ran while one was open for 2% of the time, Pallas kernels for 19%

profile of v2, /device:TPU:0, one launch (start us, length us, event | category | flops | bytes accessed | tf_op | source)
XLA Modules:
  0.0 90.3 jit_solution(3561607118766757809)
XLA Ops:
  0.0 4.8 %shard_map.91 = bf16[32,136,128]{2,1,0:T(8,128)(2,1)} custom-call(s32[1,1024]{1,0:T(1,128)} %bitcast.16, s32[4,1024]{1,0:T(4,128)} %bitcast.14, bf16[4,1024]{1,0:T(4,128)(2,1)} %bitcast.15, bf16[1024,256]{1,0:T(8,128)(2,1)} %obs_hbm.1), custom_call_target="tpu_custom_call" | custom-call | tf_op jit(solution)/shard_map/pallas_call | solution.py:457
  4.8 7.4 %all-to-all-start = ((bf16[32,136,128]{2,1,0:T(8,128)(2,1)}), bf16[32,136,128]{2,1,0:T(8,128)(2,1)}, u32[]{:S(2)}, u32[]{:S(2)}) async-start(bf16[32,136,128]{2,1,0:T(8,128)(2,1)} %shard_map.91), calls=%async_computation | async-start | bytes 2228224 | tf_op jit(solution)/shard_map/all_to_all | solution.py:567
  12.3 2.1 %multiply_convert_fusion.mix_ref = bf16[4,512,512]{2,1,0:T(8,128)(2,1)S(1)} fusion(bf16[4,512,512]{2,1,0:T(8,128)(2,1)} %param.16, f32[4,512]{1,0:T(4,128)S(1)} %copy-done.3), kind=kLoop, calls=%fused_computation | loop fusion | flops 3145728 | bytes 4202496 | tf_op jit(solution)/shard_map/convert_element_type | solution.py:570
  14.5 26.7 %all-to-all-done.got_ref = bf16[32,136,128]{2,1,0:T(8,128)(2,1)} async-done(((bf16[32,136,128]{2,1,0:T(8,128)(2,1)}), bf16[32,136,128]{2,1,0:T(8,128)(2,1)}, u32[]{:S(2)}, u32[]{:S(2)}) %all-to-all-start) | async-done | bytes 1114144 | tf_op jit(solution)/shard_map/all_to_all | solution.py:567
  41.2 3.5 %shard_map.93 = (bf16[6,32,512]{2,1,0:T(8,128)(2,1)S(1)}, bf16[10,32,512]{2,1,0:T(8,128)(2,1)S(1)}, bf16[6,16,512]{2,1,0:T(8,128)(2,1)S(1)}, bf16[6,8,512]{2,1,0:T(8,128)(2,1)S(1)}) custom-call(bf16[32,136,128]{2,1,0:T(8,128)(2,1)} %all-to-all-done.got_ref, bf16[256,512]{1,0:T(8,128)(2,1)S(1)} %get-tuple-element.43.proj_ref, ...), custom_call_target="tpu_custom_call" | custom-call | tf_op jit(solution)/shard_map/pallas_call | solution.py:457
  44.7 0.8 collective-permute-start.1
  45.6 0.9 collective-permute-start.2
  46.4 4.1 %collective-permute-done.lon_in = bf16[6,16,512]{2,1,0:T(8,128)(2,1)S(1)} collective-permute-done((bf16[6,16,512]{2,1,0:T(8,128)(2,1)S(1)}, bf16[6,16,512]{2,1,0:T(8,128)(2,1)S(1)}, u32[]{:S(2)}, u32[]{:S(2)}) %collective-permute-start) | collective-permute-done | bytes 98336 | tf_op jit(solution)/shard_map/ppermute | solution.py:538
  50.6 4.3 %shard_map.94 = (bf16[13,32,512]{2,1,0:T(8,128)(2,1)S(1)}, f32[4,6,16,128]{3,2,1,0:T(8,128)S(1)}, bf16[4,2,3,16,128]{4,3,2,1,0:T(8,128)(2,1)S(1)}, bf16[2,6,16,512]{3,2,1,0:T(8,128)(2,1)S(1)}) custom-call(bf16[6,32,512]{2,1,0:T(8,128)(2,1)S(1)} %get-tuple-element.45.edge_in, bf16[10,32,512]{2,1,0:T(8,128)(2,1)S(1)} %get-tuple-element.46.inner_in, ...), custom_call_target="tpu_custom_call" | custom-call | flops 1064960000 | tf_op jit(solution)/shard_map/pallas_call | solution.py:457
  54.9 1.6 %shard_map.95 = (bf16[6,32,512]{2,1,0:T(8,128)(2,1)S(1)}, bf16[8,16,512]{2,1,0:T(8,128)(2,1)S(1)}, bf16[6,8,512]{2,1,0:T(8,128)(2,1)S(1)}) custom-call(bf16[10,32,512]{2,1,0:T(8,128)(2,1)S(1)} %get-tuple-element.46.inner_in, bf16[6,16,512]{2,1,0:T(8,128)(2,1)S(1)} %collective-permute-done.lon_in, bf16[6,32,512]{2,1,0:T(8,128)(2,1)S(1)} %collective-permute-done.1.lat_in, ...), custom_call_target="tpu_custom_call" | custom-call | flops 491520000 | tf_op jit(solution)/shard_map/pallas_call | solution.py:457
  56.6 2.0 %collective-permute-start.4 = (bf16[6,32,512]{2,1,0:T(8,128)(2,1)S(1)}, bf16[6,32,512]{2,1,0:T(8,128)(2,1)S(1)}, u32[]{:S(2)}, u32[]{:S(2)}) collective-permute-start(bf16[6,32,512]{2,1,0:T(8,128)(2,1)S(1)} %get-tuple-element.55.edge_in), channel_id=1, source_target_pairs={{8,0},{16,8},{24,16},{0,24},{9,1},{17,9},{25,17},{1,25},{10,2},{18... | collective-permute-start | bytes 589832 | tf_op jit(solution)/shard_map/ppermute | solution.py:539
  59.1 4.4 %shard_map.96 = (bf16[10,32,512]{2,1,0:T(8,128)(2,1)S(1)}, f32[4,6,16,128]{3,2,1,0:T(8,128)S(1)}, bf16[4,2,3,16,128]{4,3,2,1,0:T(8,128)(2,1)S(1)}, bf16[2,6,16,512]{3,2,1,0:T(8,128)(2,1)S(1)}) custom-call(bf16[6,32,512]{2,1,0:T(8,128)(2,1)S(1)} %get-tuple-element.55.edge_in, bf16[13,32,512]{2,1,0:T(8,128)(2,1)S(1)} %get-tuple-element.49.inner_new.inner_in, ...), custom_call_target="tpu_custom_call" | custom-call | flops 819200000 | tf_op jit(solution)/shard_map/pallas_call | solution.py:457
  63.5 1.4 %collective-permute-done.5.corner_in = bf16[6,8,512]{2,1,0:T(8,128)(2,1)S(1)} collective-permute-done((bf16[6,8,512]{2,1,0:T(8,128)(2,1)S(1)}, bf16[6,8,512]{2,1,0:T(8,128)(2,1)S(1)}, u32[]{:S(2)}, u32[]{:S(2)}) %collective-permute-start.5) | collective-permute-done | bytes 49184 | tf_op jit(solution)/shard_map/ppermute | solution.py:540
  64.9 1.6 %shard_map.97 = (bf16[6,32,512]{2,1,0:T(8,128)(2,1)S(1)}, bf16[6,16,512]{2,1,0:T(8,128)(2,1)S(1)}, bf16[6,8,512]{2,1,0:T(8,128)(2,1)S(1)}) custom-call(bf16[13,32,512]{2,1,0:T(8,128)(2,1)S(1)} %get-tuple-element.49.inner_new.inner_in, bf16[8,16,512]{2,1,0:T(8,128)(2,1)S(1)} %collective-permute-done.3.lon_in, ...), custom_call_target="tpu_custom_call" | custom-call | flops 491520000 | tf_op jit(solution)/shard_map/pallas_call | solution.py:457
  66.6 0.6 collective-permute-start.7
  67.2 1.2 %collective-permute-start.8 = (bf16[6,8,512]{2,1,0:T(8,128)(2,1)S(1)}, bf16[6,8,512]{2,1,0:T(8,128)(2,1)S(1)}, u32[]{:S(2)}, u32[]{:S(2)}) collective-permute-start(bf16[6,8,512]{2,1,0:T(8,128)(2,1)S(1)} %get-tuple-element.64), channel_id=1, source_target_pairs={{0,9},{1,10},{2,11},{3,12},{4,13},{5,14},{6,15},{7,8},{8,17},{9,18... | collective-permute-start | bytes 147464 | tf_op jit(solution)/shard_map/ppermute | solution.py:540
  68.4 4.0 %collective-permute-done.6.lon_in = bf16[6,16,512]{2,1,0:T(8,128)(2,1)S(1)} collective-permute-done((bf16[6,16,512]{2,1,0:T(8,128)(2,1)S(1)}, bf16[6,16,512]{2,1,0:T(8,128)(2,1)S(1)}, u32[]{:S(2)}, u32[]{:S(2)}) %collective-permute-start.6) | collective-permute-done | bytes 98336 | tf_op jit(solution)/shard_map/ppermute | solution.py:538
  72.4 4.3 %shard_map.98 = (bf16[13,32,512]{2,1,0:T(8,128)(2,1)S(1)}, f32[4,6,16,128]{3,2,1,0:T(8,128)S(1)}, bf16[4,2,3,16,128]{4,3,2,1,0:T(8,128)(2,1)S(1)}, bf16[2,6,16,512]{3,2,1,0:T(8,128)(2,1)S(1)}) custom-call(bf16[6,32,512]{2,1,0:T(8,128)(2,1)S(1)} %get-tuple-element.61.edge_in, bf16[10,32,512]{2,1,0:T(8,128)(2,1)S(1)} %get-tuple-element.59.inner_new.inner_in, ...), custom_call_target="tpu_custom_call" | custom-call | flops 1064960000 | tf_op jit(solution)/shard_map/pallas_call | solution.py:457
  76.7 1.6 %shard_map.99 = (bf16[6,32,512]{2,1,0:T(8,128)(2,1)S(1)}, bf16[8,16,512]{2,1,0:T(8,128)(2,1)S(1)}, bf16[6,8,512]{2,1,0:T(8,128)(2,1)S(1)}) custom-call(bf16[10,32,512]{2,1,0:T(8,128)(2,1)S(1)} %get-tuple-element.59.inner_new.inner_in, bf16[6,16,512]{2,1,0:T(8,128)(2,1)S(1)} %collective-permute-done.6.lon_in, ...), custom_call_target="tpu_custom_call" | custom-call | flops 491520000 | tf_op jit(solution)/shard_map/pallas_call | solution.py:457
  78.4 1.8 %collective-permute-start.9 = (bf16[8,16,512]{2,1,0:T(8,128)(2,1)S(1)}, bf16[8,16,512]{2,1,0:T(8,128)(2,1)S(1)}, u32[]{:S(2)}, u32[]{:S(2)}) collective-permute-start(bf16[8,16,512]{2,1,0:T(8,128)(2,1)S(1)} %get-tuple-element.68), channel_id=1, source_target_pairs={{1,0},{2,1},{3,2},{4,3},{5,4},{6,5},{7,6},{0,7},{9,8},{10,9},{11,1... | collective-permute-start | bytes 393224 | tf_op jit(solution)/shard_map/ppermute | solution.py:538
  80.1 2.1 %collective-permute-start.10 = (bf16[6,32,512]{2,1,0:T(8,128)(2,1)S(1)}, bf16[6,32,512]{2,1,0:T(8,128)(2,1)S(1)}, u32[]{:S(2)}, u32[]{:S(2)}) collective-permute-start(bf16[6,32,512]{2,1,0:T(8,128)(2,1)S(1)} %get-tuple-element.69.edge_in), channel_id=1, source_target_pairs={{8,0},{16,8},{24,16},{0,24},{9,1},{17,9},{25,17},{1,25},{10,2},{18... | collective-permute-start | bytes 589832 | tf_op jit(solution)/shard_map/ppermute | solution.py:539
  82.6 4.4 %shard_map.100 = (bf16[10,32,512]{2,1,0:T(8,128)(2,1)S(1)}, f32[4,6,16,128]{3,2,1,0:T(8,128)S(1)}, bf16[4,2,3,16,128]{4,3,2,1,0:T(8,128)(2,1)S(1)}, bf16[2,6,16,512]{3,2,1,0:T(8,128)(2,1)S(1)}) custom-call(bf16[6,32,512]{2,1,0:T(8,128)(2,1)S(1)} %get-tuple-element.69.edge_in, bf16[13,32,512]{2,1,0:T(8,128)(2,1)S(1)} %get-tuple-element.63.inner_new.inner_in, ...), custom_call_target="tpu_custom_call" | custom-call | flops 819200000 | tf_op jit(solution)/shard_map/pallas_call | solution.py:457
  87.1 0.8 collective-permute-done.10.lat_in
  87.9 2.4 %shard_map.101 = bf16[16,32,512]{2,1,0:T(8,128)(2,1)} custom-call(bf16[13,32,512]{2,1,0:T(8,128)(2,1)S(1)} %get-tuple-element.63.inner_new.inner_in, bf16[8,16,512]{2,1,0:T(8,128)(2,1)S(1)} %collective-permute-done.9.lon_in, bf16[6,32,512]{2,1,0:T(8,128)(2,1)S(1)} %collective-permute-done.10.lat_in, ...), custom_call_target="tpu_custom_call" | custom-call | flops 491520000 | tf_op jit(solution)/shard_map/pallas_call | solution.py:457
  (22 shorter events, 1.2 us)
Async XLA Ops:
  0.0 12.2 %copy-start.2 = (bf16[256,512]{1,0:T(8,128)(2,1)S(1)}, bf16[256,512]{1,0:T(8,128)(2,1)}, u32[]{:S(2)}) copy-start(bf16[256,512]{1,0:T(8,128)(2,1)} %proj_hbm.1) | copy-start | bytes 786436
  0.0 12.2 %copy-start.1 = (bf16[16,32,512]{2,1,0:T(8,128)(2,1)S(1)}, bf16[16,32,512]{2,1,0:T(8,128)(2,1)}, u32[]{:S(2)}) copy-start(bf16[16,32,512]{2,1,0:T(8,128)(2,1)} %back_hbm.1) | copy-start | bytes 1572868
  0.0 12.3 %copy-start.3 = (f32[4,512]{1,0:T(4,128)S(1)}, f32[4,512]{1,0:T(4,128)}, u32[]{:S(2)}) copy-start(f32[4,512]{1,0:T(4,128)} %param.17) | copy-start | bytes 24580
  4.8 36.4 %all-to-all-start = ((bf16[32,136,128]{2,1,0:T(8,128)(2,1)}), bf16[32,136,128]{2,1,0:T(8,128)(2,1)}, u32[]{:S(2)}, u32[]{:S(2)}) async-start(bf16[32,136,128]{2,1,0:T(8,128)(2,1)} %shard_map.91), calls=%async_computation | async-start | bytes 2228224 | tf_op jit(solution)/shard_map/all_to_all | solution.py:567
  12.3 38.2 %copy-start = (f32[4,7,7,512]{3,0,2,1:T(4,128)S(1)}, f32[4,7,7,512]{3,0,2,1:T(4,128)}, u32[]{:S(2)}) copy-start(f32[4,7,7,512]{3,0,2,1:T(4,128)} %param.15) | copy-start | bytes 1204228
  44.7 5.9 %collective-permute-start = (bf16[6,16,512]{2,1,0:T(8,128)(2,1)S(1)}, bf16[6,16,512]{2,1,0:T(8,128)(2,1)S(1)}, u32[]{:S(2)}, u32[]{:S(2)}) collective-permute-start(bf16[6,16,512]{2,1,0:T(8,128)(2,1)S(1)} %get-tuple-element.47), channel_id=1, source_target_pairs={{0,1},{1,2},{2,3},{3,4},{4,5},{5,6},{6,7},{7,0},{8,9},{9,10},{10,1... | collective-permute-start | bytes 294920 | tf_op jit(solution)/shard_map/ppermute | solution.py:538
  44.7 10.1 %collective-permute-start.1 = (bf16[6,32,512]{2,1,0:T(8,128)(2,1)S(1)}, bf16[6,32,512]{2,1,0:T(8,128)(2,1)S(1)}, u32[]{:S(2)}, u32[]{:S(2)}) collective-permute-start(bf16[6,32,512]{2,1,0:T(8,128)(2,1)S(1)} %get-tuple-element.45.edge_in), channel_id=1, source_target_pairs={{0,8},{8,16},{16,24},{24,0},{1,9},{9,17},{17,25},{25,1},{2,10},{10... | collective-permute-start | bytes 589832 | tf_op jit(solution)/shard_map/ppermute | solution.py:539
  45.6 9.3 %collective-permute-start.2 = (bf16[6,8,512]{2,1,0:T(8,128)(2,1)S(1)}, bf16[6,8,512]{2,1,0:T(8,128)(2,1)S(1)}, u32[]{:S(2)}, u32[]{:S(2)}) collective-permute-start(bf16[6,8,512]{2,1,0:T(8,128)(2,1)S(1)} %get-tuple-element.50), channel_id=1, source_target_pairs={{0,9},{1,10},{2,11},{3,12},{4,13},{5,14},{6,15},{7,8},{8,17},{9,18... | collective-permute-start | bytes 147464 | tf_op jit(solution)/shard_map/ppermute | solution.py:540
  56.5 2.6 %collective-permute-start.3 = (bf16[8,16,512]{2,1,0:T(8,128)(2,1)S(1)}, bf16[8,16,512]{2,1,0:T(8,128)(2,1)S(1)}, u32[]{:S(2)}, u32[]{:S(2)}) collective-permute-start(bf16[8,16,512]{2,1,0:T(8,128)(2,1)S(1)} %get-tuple-element.54), channel_id=1, source_target_pairs={{1,0},{2,1},{3,2},{4,3},{5,4},{6,5},{7,6},{0,7},{9,8},{10,9},{11,1... | collective-permute-start | bytes 393224 | tf_op jit(solution)/shard_map/ppermute | solution.py:538
  56.6 8.4 %collective-permute-start.4 = (bf16[6,32,512]{2,1,0:T(8,128)(2,1)S(1)}, bf16[6,32,512]{2,1,0:T(8,128)(2,1)S(1)}, u32[]{:S(2)}, u32[]{:S(2)}) collective-permute-start(bf16[6,32,512]{2,1,0:T(8,128)(2,1)S(1)} %get-tuple-element.55.edge_in), channel_id=1, source_target_pairs={{8,0},{16,8},{24,16},{0,24},{9,1},{17,9},{25,17},{1,25},{10,2},{18... | collective-permute-start | bytes 589832 | tf_op jit(solution)/shard_map/ppermute | solution.py:539
  58.6 6.3 %collective-permute-start.5 = (bf16[6,8,512]{2,1,0:T(8,128)(2,1)S(1)}, bf16[6,8,512]{2,1,0:T(8,128)(2,1)S(1)}, u32[]{:S(2)}, u32[]{:S(2)}) collective-permute-start(bf16[6,8,512]{2,1,0:T(8,128)(2,1)S(1)} %get-tuple-element.56), channel_id=1, source_target_pairs={{9,0},{10,1},{11,2},{12,3},{13,4},{14,5},{15,6},{8,7},{17,8},{18,9... | collective-permute-start | bytes 147464 | tf_op jit(solution)/shard_map/ppermute | solution.py:540
  66.5 5.9 %collective-permute-start.6 = (bf16[6,16,512]{2,1,0:T(8,128)(2,1)S(1)}, bf16[6,16,512]{2,1,0:T(8,128)(2,1)S(1)}, u32[]{:S(2)}, u32[]{:S(2)}) collective-permute-start(bf16[6,16,512]{2,1,0:T(8,128)(2,1)S(1)} %get-tuple-element.62), channel_id=1, source_target_pairs={{0,1},{1,2},{2,3},{3,4},{4,5},{5,6},{6,7},{7,0},{8,9},{9,10},{10,1... | collective-permute-start | bytes 294920 | tf_op jit(solution)/shard_map/ppermute | solution.py:538
  66.6 10.1 %collective-permute-start.7 = (bf16[6,32,512]{2,1,0:T(8,128)(2,1)S(1)}, bf16[6,32,512]{2,1,0:T(8,128)(2,1)S(1)}, u32[]{:S(2)}, u32[]{:S(2)}) collective-permute-start(bf16[6,32,512]{2,1,0:T(8,128)(2,1)S(1)} %get-tuple-element.61.edge_in), channel_id=1, source_target_pairs={{0,8},{8,16},{16,24},{24,0},{1,9},{9,17},{17,25},{25,1},{2,10},{10... | collective-permute-start | bytes 589832 | tf_op jit(solution)/shard_map/ppermute | solution.py:539
  67.2 9.5 %collective-permute-start.8 = (bf16[6,8,512]{2,1,0:T(8,128)(2,1)S(1)}, bf16[6,8,512]{2,1,0:T(8,128)(2,1)S(1)}, u32[]{:S(2)}, u32[]{:S(2)}) collective-permute-start(bf16[6,8,512]{2,1,0:T(8,128)(2,1)S(1)} %get-tuple-element.64), channel_id=1, source_target_pairs={{0,9},{1,10},{2,11},{3,12},{4,13},{5,14},{6,15},{7,8},{8,17},{9,18... | collective-permute-start | bytes 147464 | tf_op jit(solution)/shard_map/ppermute | solution.py:540
  78.4 4.3 %collective-permute-start.9 = (bf16[8,16,512]{2,1,0:T(8,128)(2,1)S(1)}, bf16[8,16,512]{2,1,0:T(8,128)(2,1)S(1)}, u32[]{:S(2)}, u32[]{:S(2)}) collective-permute-start(bf16[8,16,512]{2,1,0:T(8,128)(2,1)S(1)} %get-tuple-element.68), channel_id=1, source_target_pairs={{1,0},{2,1},{3,2},{4,3},{5,4},{6,5},{7,6},{0,7},{9,8},{10,9},{11,1... | collective-permute-start | bytes 393224 | tf_op jit(solution)/shard_map/ppermute | solution.py:538
  80.1 7.8 %collective-permute-start.10 = (bf16[6,32,512]{2,1,0:T(8,128)(2,1)S(1)}, bf16[6,32,512]{2,1,0:T(8,128)(2,1)S(1)}, u32[]{:S(2)}, u32[]{:S(2)}) collective-permute-start(bf16[6,32,512]{2,1,0:T(8,128)(2,1)S(1)} %get-tuple-element.69.edge_in), channel_id=1, source_target_pairs={{8,0},{16,8},{24,16},{0,24},{9,1},{17,9},{25,17},{1,25},{10,2},{18... | collective-permute-start | bytes 589832 | tf_op jit(solution)/shard_map/ppermute | solution.py:539
  82.2 4.9 %collective-permute-start.11 = (bf16[6,8,512]{2,1,0:T(8,128)(2,1)S(1)}, bf16[6,8,512]{2,1,0:T(8,128)(2,1)S(1)}, u32[]{:S(2)}, u32[]{:S(2)}) collective-permute-start(bf16[6,8,512]{2,1,0:T(8,128)(2,1)S(1)} %get-tuple-element.70), channel_id=1, source_target_pairs={{9,0},{10,1},{11,2},{12,3},{13,4},{14,5},{15,6},{8,7},{17,8},{18,9... | collective-permute-start | bytes 147464 | tf_op jit(solution)/shard_map/ppermute | solution.py:540

commit v3 on v1

--- a/solution.py
+++ b/solution.py
@@ -178,10 +178,11 @@
             taps_in[g, r, target] = wide_ref[g, row, columns, :].astype(BF16)
 
 
-def convolve(taps_in, taps_ref, tap_ref, spread_ref, layer, g, first, count):
+def convolve(taps_in, taps_ref, gains_ref, tap_ref, spread_ref, layer, g, first, count):
     lanes = pl.ds(pl.multiple_of(g * LANES, LANES), LANES)
+    gain = gains_ref[layer : layer + 1, lanes]
     for k in range(TAPS * TAPS):
-        row = taps_ref[k, layer : layer + 1, lanes]
+        row = taps_ref[k, layer : layer + 1, lanes] * gain
         tap_ref[k] = jnp.broadcast_to(row, (TILE, LANES)).astype(BF16)
     for p in range(2):
         total = None
@@ -195,12 +196,16 @@
         spread_ref[p, first : first + count, :, lanes] = total
 
 
-def finish(taps_in, spread_ref, mix_ref, out_ref, layer, first, count):
+def finish(taps_in, gains_ref, spread_ref, mix_ref, out_ref, layer, first, count):
     chans = mix_ref.shape[1]
     ones = jnp.ones((chans, LANES), BF16)
+    gain = gains_ref[layer : layer + 1, :]
+    inverse = jnp.broadcast_to(1.0 / (gain * gain), (TILE, chans)).astype(BF16)
     for p in range(2):
         spread = spread_ref[p, first : first + count].reshape(count * TILE, chans)
-        power = jnp.dot(spread * spread, ones, preferred_element_type=F32)
+        square = spread * spread
+        square = (square.reshape(count, TILE, chans) * inverse[None]).reshape(count * TILE, chans)
+        power = jnp.dot(square, ones, preferred_element_type=F32)
         scale = 0.5 * lax.rsqrt(power * (1.0 / chans) + 1e-05)
         mixed = jnp.dot(spread, mix_ref[layer], preferred_element_type=F32)
         for g in range(chans // LANES):
@@ -235,6 +240,7 @@
     inner_in,
     lon_in,
     taps_ref,
+    gains_ref,
     mix_ref,
     inner_ref,
     lon_ref,
@@ -277,9 +283,9 @@
 
     @pl.loop(0, groups)
     def _(g):
-        convolve(taps_in, taps_ref, tap_ref, spread_ref, layer, g, 0, count)
-
-    finish(taps_in, spread_ref, mix_ref, out_ref, layer, 0, count)
+        convolve(taps_in, taps_ref, gains_ref, tap_ref, spread_ref, layer, g, 0, count)
+
+    finish(taps_in, gains_ref, spread_ref, mix_ref, out_ref, layer, 0, count)
     edge = cols - SHIFT if shrink else 0
     above = 0 if shrink else SHIFT
     for g in range(groups):
@@ -299,9 +305,9 @@
 
             @pl.loop(0, groups)
             def _(g):
-                convolve(taps_in, taps_ref, tap_ref, spread_ref, layer, g, count, HALO)
-
-            finish(taps_in, spread_ref, mix_ref, out_ref, layer, count, HALO)
+                convolve(taps_in, taps_ref, gains_ref, tap_ref, spread_ref, layer, g, count, HALO)
+
+            finish(taps_in, gains_ref, spread_ref, mix_ref, out_ref, layer, count, HALO)
 
         for k in range(HALO):
             inner_ref[count + k] = row_of(out_ref, count + k).astype(BF16)
@@ -319,6 +325,7 @@
     inner_new,
     lon_new,
     taps_ref,
+    gains_ref,
     mix_ref,
     *refs,
 ):
@@ -359,9 +366,9 @@
 
     @pl.loop(0, groups)
     def _(g):
-        convolve(taps_in, taps_ref, tap_ref, spread_ref, layer, g, 0, SHIFT)
-
-    finish(taps_in, spread_ref, mix_ref, out_ref, layer, 0, SHIFT)
+        convolve(taps_in, taps_ref, gains_ref, tap_ref, spread_ref, layer, g, 0, SHIFT)
+
+    finish(taps_in, gains_ref, spread_ref, mix_ref, out_ref, layer, 0, SHIFT)
     kept = inner_new.shape[0]
     if final:
         for k in range(SHIFT):
@@ -426,7 +433,7 @@
     )
 
 
-def layer(state, lon_out, corner_out, taps, mix, number, shrink, final):
+def layer(state, lon_out, corner_out, taps, gains, mix, number, shrink, final):
     edge, inner = state
     lat_in, lon_in, corner_in = exchange((edge, lon_out, corner_out), not shrink)
     cols, chans = edge.shape[1:]
@@ -441,7 +448,7 @@
             jax.ShapeDtypeStruct((groups, SHIFT, rows, LANES), F32),
             held(groups, TAPS + 1, SHIFT, TILE, LANES),
         ),
-        (edge, inner, lon_in, taps, mix),
+        (edge, inner, lon_in, taps, gains, mix),
         scratch_of(groups, rows + spare, made, cols, chans),
         work=made * cols * chans * WORK,
     )
@@ -456,7 +463,7 @@
     outs = call(
         functools.partial(edge_kernel, shrink, final, number),
         outs,
-        (inner, lon_in, lat_in, corner_in, near, inner_new, lon_new, taps, mix),
+        (inner, lon_in, lat_in, corner_in, near, inner_new, lon_new, taps, gains, mix),
         scratch_of(groups, 2 * SHIFT, SHIFT, cols, chans)
         + (
             pltpu.VMEM((groups, 2 * TILE, LANES), F32),
@@ -513,7 +520,6 @@
     got = lax.all_to_all(send, ("lat", "lon"), split_axis=0, concat_axis=0, tiled=True)
     layers = depth_w.shape[0]
     taps = depth_w.transpose(1, 2, 0, 3).reshape(TAPS * TAPS, layers, chans)
-    mix = (gains[:, :, None] * point_w.astype(F32)).astype(BF16)
     proj, back = call(
         fetch_kernel,
         (held(*obs_proj.shape), held(*background.shape)),
@@ -521,7 +527,7 @@
         (pltpu.SemaphoreType.DMA((2,)),),
         space=(pltpu.HBM, pltpu.HBM),
     )
-    got, mix, proj, back = lax.optimization_barrier((got, mix, proj, back))
+    got, proj, back = lax.optimization_barrier((got, proj, back))
     edge, inner, lon_out, corner_out = call(
         functools.partial(assim_kernel, cap, cols + 1),
         (
@@ -536,10 +542,10 @@
     state = (edge, inner)
     for n in range(layers - 1):
         state, lon_out, corner_out = layer(
-            state, lon_out, corner_out, taps, mix, n, n % 2 == 1, False
+            state, lon_out, corner_out, taps, gains, point_w, n, n % 2 == 1, False
         )
     n = layers - 1
-    return layer(state, lon_out, corner_out, taps, mix, n, n % 2 == 1, True)
+    return layer(state, lon_out, corner_out, taps, gains, point_w, n, n % 2 == 1, True)
 
 
 def solution(mesh):

time: 90.3 us -> 91.6 us (1.014)
  other arithmetic: 2.1 us -> 0 us
  local copies, waits for them, and re-layouts: 0.02 us -> 1.67 us
  waiting for transfers between devices: 40.8 us -> 42.3 us
    convert_element_type x1 -> x0, other arithmetic: 2.1 us -> none  [body(): mix = (gains[:, :, None] * point_w.astype(F32)).astype(BF16)]
    unnamed x8 -> x14, local copies, waits for them, and re-layouts: 0.02 us -> 1.67 us
    all_to_all x1, waiting for transfers between devices: 26.7 us -> 28.2 us  [body(): lax.all_to_all(send, ('lat', 'lon'), split_axis=0, concat_axis=0, tiled=T...]
  transfers between devices with their start and end apart: 13 -> 13, of which waited for: 8 -> 9; matrix products, arithmetic and copies ran while one was open for 2% -> 0% of each run, Pallas kernels for 15% -> 15%
where the time goes in v3:
time: 91.6 us; the launch traced here: 91.3 us
  waiting for transfers between devices  42.3 us (46%)
  Pallas kernels  31.1 us (34%)
  starting transfers between devices  16.2 us (18%)
  local copies, waits for them, and re-layouts  1.67 us (2%)
    pallas_call x11, Pallas kernels, call(): pl.pallas_call(kernel, out_shape=out_shape, in_specs=[pl.BlockSpec(memory...  31.1 us
    all_to_all x1, waiting for transfers between devices, body(): lax.all_to_all(send, ('lat', 'lon'), split_axis=0, concat_axis=0, tiled=T...  28.2 us
    ppermute x4, waiting for transfers between devices, exchange(): lon = lax.ppermute(lon, 'lon', around)  10.2 us
    all_to_all x1, starting transfers between devices, body(): lax.all_to_all(send, ('lat', 'lon'), split_axis=0, concat_axis=0, tiled=T...  7.42 us
    ppermute x4, starting transfers between devices, exchange(): lat = lax.ppermute(lat, 'lat', along)  5.33 us
    ppermute x4, starting transfers between devices, exchange(): lon = lax.ppermute(lon, 'lon', around)  2.21 us
    ppermute x4, waiting for transfers between devices, exchange(): corner = lax.ppermute(corner, ('lat', 'lon'), across)  2.15 us
  transfers between devices with their start and end apart: 13, of which 9 were waited for; matrix products, arithmetic and copies ran while one was open for 0% of the time, Pallas kernels for 15%

profile of v3, /device:TPU:0, one launch (start us, length us, event | category | flops | bytes accessed | tf_op | source)
XLA Modules:
  0.0 91.3 jit_solution(152112780777310312)
XLA Ops:
  0.0 4.7 %shard_map.91 = bf16[32,136,128]{2,1,0:T(8,128)(2,1)} custom-call(s32[1,1024]{1,0:T(1,128)} %bitcast.16, s32[4,1024]{1,0:T(4,128)} %bitcast.14, bf16[4,1024]{1,0:T(4,128)(2,1)} %bitcast.15, bf16[1024,256]{1,0:T(8,128)(2,1)} %obs_hbm.1), custom_call_target="tpu_custom_call" | custom-call | tf_op jit(solution)/shard_map/pallas_call | solution.py:411
  4.7 7.4 %all-to-all-start = ((bf16[32,136,128]{2,1,0:T(8,128)(2,1)}), bf16[32,136,128]{2,1,0:T(8,128)(2,1)}, u32[]{:S(2)}, u32[]{:S(2)}) async-start(bf16[32,136,128]{2,1,0:T(8,128)(2,1)} %shard_map.91), calls=%async_computation | async-start | bytes 2228224 | tf_op jit(solution)/shard_map/all_to_all | solution.py:520
  12.3 0.7 copy-done.5
  13.0 28.2 %all-to-all-done.got_ref = bf16[32,136,128]{2,1,0:T(8,128)(2,1)} async-done(((bf16[32,136,128]{2,1,0:T(8,128)(2,1)}), bf16[32,136,128]{2,1,0:T(8,128)(2,1)}, u32[]{:S(2)}, u32[]{:S(2)}) %all-to-all-start) | async-done | bytes 1114144 | tf_op jit(solution)/shard_map/all_to_all | solution.py:520
  41.2 0.9 %copy-done.6 = bf16[256,512]{1,0:T(8,128)(2,1)S(1)} copy-done((bf16[256,512]{1,0:T(8,128)(2,1)S(1)}, bf16[256,512]{1,0:T(8,128)(2,1)}, u32[]{:S(2)}) %copy-start.6) | copy-done | bytes 262168
  42.1 3.5 %shard_map.93 = (bf16[6,32,512]{2,1,0:T(8,128)(2,1)S(1)}, bf16[10,32,512]{2,1,0:T(8,128)(2,1)S(1)}, bf16[6,16,512]{2,1,0:T(8,128)(2,1)S(1)}, bf16[6,8,512]{2,1,0:T(8,128)(2,1)S(1)}) custom-call(bf16[32,136,128]{2,1,0:T(8,128)(2,1)} %all-to-all-done.got_ref, bf16[256,512]{1,0:T(8,128)(2,1)S(1)} %copy-done.6, bf16[16,32,512]{2,1,0:T(8,128)(2,1)S(1)} %get-tuple-element.39.back_ref), custom_call_target="tpu_custom_call" | custom-call | tf_op jit(solution)/shard_map/pallas_call | solution.py:411
  45.6 0.8 collective-permute-start.1
  46.5 0.9 collective-permute-start.2
  47.4 4.1 %collective-permute-done.lon_in = bf16[6,16,512]{2,1,0:T(8,128)(2,1)S(1)} collective-permute-done((bf16[6,16,512]{2,1,0:T(8,128)(2,1)S(1)}, bf16[6,16,512]{2,1,0:T(8,128)(2,1)S(1)}, u32[]{:S(2)}, u32[]{:S(2)}) %collective-permute-start) | collective-permute-done | bytes 98336 | tf_op jit(solution)/shard_map/ppermute | solution.py:491
  51.5 3.3 %shard_map.94 = (bf16[13,32,512]{2,1,0:T(8,128)(2,1)S(1)}, f32[4,6,16,128]{3,2,1,0:T(8,128)S(1)}, bf16[4,8,6,16,128]{4,3,2,1,0:T(8,128)(2,1)S(1)}) custom-call(bf16[6,32,512]{2,1,0:T(8,128)(2,1)S(1)} %get-tuple-element.40.edge_in, bf16[10,32,512]{2,1,0:T(8,128)(2,1)S(1)} %get-tuple-element.41.inner_in, bf16[6,16,512]{2,1,0:T(8,128)(2,1)S(1)} %collective-permute-done.lon_in, ...), custom_call_target="tpu_custom_call" | custom-call | flops 1064960000 | tf_op jit(solution)/shard_map/pallas_call | solution.py:411
  54.9 2.1 %shard_map.95 = (bf16[6,32,512]{2,1,0:T(8,128)(2,1)S(1)}, bf16[8,16,512]{2,1,0:T(8,128)(2,1)S(1)}, bf16[6,8,512]{2,1,0:T(8,128)(2,1)S(1)}) custom-call(bf16[10,32,512]{2,1,0:T(8,128)(2,1)S(1)} %get-tuple-element.41.inner_in, bf16[6,16,512]{2,1,0:T(8,128)(2,1)S(1)} %collective-permute-done.lon_in, bf16[6,32,512]{2,1,0:T(8,128)(2,1)S(1)} %collective-permute-done.1.lat_in, ...), custom_call_target="tpu_custom_call" | custom-call | flops 491520000 | tf_op jit(solution)/shard_map/pallas_call | solution.py:411
  57.2 1.8 %collective-permute-start.4 = (bf16[6,32,512]{2,1,0:T(8,128)(2,1)S(1)}, bf16[6,32,512]{2,1,0:T(8,128)(2,1)S(1)}, u32[]{:S(2)}, u32[]{:S(2)}) collective-permute-start(bf16[6,32,512]{2,1,0:T(8,128)(2,1)S(1)} %get-tuple-element.48.edge_in), channel_id=1, source_target_pairs={{8,0},{16,8},{24,16},{0,24},{9,1},{17,9},{25,17},{1,25},{10,2},{18... | collective-permute-start | bytes 589832 | tf_op jit(solution)/shard_map/ppermute | solution.py:492
  59.8 3.5 %shard_map.96 = (bf16[10,32,512]{2,1,0:T(8,128)(2,1)S(1)}, f32[4,6,16,128]{3,2,1,0:T(8,128)S(1)}, bf16[4,8,6,16,128]{4,3,2,1,0:T(8,128)(2,1)S(1)}) custom-call(bf16[6,32,512]{2,1,0:T(8,128)(2,1)S(1)} %get-tuple-element.48.edge_in, bf16[13,32,512]{2,1,0:T(8,128)(2,1)S(1)} %get-tuple-element.43.inner_new.inner_in, ...), custom_call_target="tpu_custom_call" | custom-call | flops 819200000 | tf_op jit(solution)/shard_map/pallas_call | solution.py:411
  63.2 2.0 %collective-permute-done.5.corner_in = bf16[6,8,512]{2,1,0:T(8,128)(2,1)S(1)} collective-permute-done((bf16[6,8,512]{2,1,0:T(8,128)(2,1)S(1)}, bf16[6,8,512]{2,1,0:T(8,128)(2,1)S(1)}, u32[]{:S(2)}, u32[]{:S(2)}) %collective-permute-start.5) | collective-permute-done | bytes 49184 | tf_op jit(solution)/shard_map/ppermute | solution.py:493
  65.4 2.1 %shard_map.97 = (bf16[6,32,512]{2,1,0:T(8,128)(2,1)S(1)}, bf16[6,16,512]{2,1,0:T(8,128)(2,1)S(1)}, bf16[6,8,512]{2,1,0:T(8,128)(2,1)S(1)}) custom-call(bf16[13,32,512]{2,1,0:T(8,128)(2,1)S(1)} %get-tuple-element.43.inner_new.inner_in, bf16[8,16,512]{2,1,0:T(8,128)(2,1)S(1)} %collective-permute-done.3.lon_in, ...), custom_call_target="tpu_custom_call" | custom-call | flops 491520000 | tf_op jit(solution)/shard_map/pallas_call | solution.py:411
  67.5 0.6 collective-permute-start.7
  68.3 5.0 %collective-permute-done.6.lon_in = bf16[6,16,512]{2,1,0:T(8,128)(2,1)S(1)} collective-permute-done((bf16[6,16,512]{2,1,0:T(8,128)(2,1)S(1)}, bf16[6,16,512]{2,1,0:T(8,128)(2,1)S(1)}, u32[]{:S(2)}, u32[]{:S(2)}) %collective-permute-start.6) | collective-permute-done | bytes 98336 | tf_op jit(solution)/shard_map/ppermute | solution.py:491
  73.3 3.5 %shard_map.98 = (bf16[13,32,512]{2,1,0:T(8,128)(2,1)S(1)}, f32[4,6,16,128]{3,2,1,0:T(8,128)S(1)}, bf16[4,8,6,16,128]{4,3,2,1,0:T(8,128)(2,1)S(1)}) custom-call(bf16[6,32,512]{2,1,0:T(8,128)(2,1)S(1)} %get-tuple-element.53.edge_in, bf16[10,32,512]{2,1,0:T(8,128)(2,1)S(1)} %get-tuple-element.51.inner_new.inner_in, ...), custom_call_target="tpu_custom_call" | custom-call | flops 1064960000 | tf_op jit(solution)/shard_map/pallas_call | solution.py:411
  76.9 2.1 %shard_map.99 = (bf16[6,32,512]{2,1,0:T(8,128)(2,1)S(1)}, bf16[8,16,512]{2,1,0:T(8,128)(2,1)S(1)}, bf16[6,8,512]{2,1,0:T(8,128)(2,1)S(1)}) custom-call(bf16[10,32,512]{2,1,0:T(8,128)(2,1)S(1)} %get-tuple-element.51.inner_new.inner_in, bf16[6,16,512]{2,1,0:T(8,128)(2,1)S(1)} %collective-permute-done.6.lon_in, ...), custom_call_target="tpu_custom_call" | custom-call | flops 491520000 | tf_op jit(solution)/shard_map/pallas_call | solution.py:411
  78.9 1.8 %collective-permute-start.9 = (bf16[8,16,512]{2,1,0:T(8,128)(2,1)S(1)}, bf16[8,16,512]{2,1,0:T(8,128)(2,1)S(1)}, u32[]{:S(2)}, u32[]{:S(2)}) collective-permute-start(bf16[8,16,512]{2,1,0:T(8,128)(2,1)S(1)} %get-tuple-element.59), channel_id=1, source_target_pairs={{1,0},{2,1},{3,2},{4,3},{5,4},{6,5},{7,6},{0,7},{9,8},{10,9},{11,1... | collective-permute-start | bytes 393224 | tf_op jit(solution)/shard_map/ppermute | solution.py:491
  80.7 2.1 %collective-permute-start.10 = (bf16[6,32,512]{2,1,0:T(8,128)(2,1)S(1)}, bf16[6,32,512]{2,1,0:T(8,128)(2,1)S(1)}, u32[]{:S(2)}, u32[]{:S(2)}) collective-permute-start(bf16[6,32,512]{2,1,0:T(8,128)(2,1)S(1)} %get-tuple-element.60.edge_in), channel_id=1, source_target_pairs={{8,0},{16,8},{24,16},{0,24},{9,1},{17,9},{25,17},{1,25},{10,2},{18... | collective-permute-start | bytes 589832 | tf_op jit(solution)/shard_map/ppermute | solution.py:492
  83.2 3.5 %shard_map.100 = (bf16[10,32,512]{2,1,0:T(8,128)(2,1)S(1)}, f32[4,6,16,128]{3,2,1,0:T(8,128)S(1)}, bf16[4,8,6,16,128]{4,3,2,1,0:T(8,128)(2,1)S(1)}) custom-call(bf16[6,32,512]{2,1,0:T(8,128)(2,1)S(1)} %get-tuple-element.60.edge_in, bf16[13,32,512]{2,1,0:T(8,128)(2,1)S(1)} %get-tuple-element.55.inner_new.inner_in, ...), custom_call_target="tpu_custom_call" | custom-call | flops 819200000 | tf_op jit(solution)/shard_map/pallas_call | solution.py:411
  86.9 1.6 %collective-permute-done.10.lat_in = bf16[6,32,512]{2,1,0:T(8,128)(2,1)S(1)} collective-permute-done((bf16[6,32,512]{2,1,0:T(8,128)(2,1)S(1)}, bf16[6,32,512]{2,1,0:T(8,128)(2,1)S(1)}, u32[]{:S(2)}, u32[]{:S(2)}) %collective-permute-start.10) | collective-permute-done | bytes 196640 | tf_op jit(solution)/shard_map/ppermute | solution.py:492
  88.5 2.8 %shard_map.101 = bf16[16,32,512]{2,1,0:T(8,128)(2,1)} custom-call(bf16[13,32,512]{2,1,0:T(8,128)(2,1)S(1)} %get-tuple-element.55.inner_new.inner_in, bf16[8,16,512]{2,1,0:T(8,128)(2,1)S(1)} %collective-permute-done.9.lon_in, bf16[6,32,512]{2,1,0:T(8,128)(2,1)S(1)} %collective-permute-done.10.lat_in, ...), custom_call_target="tpu_custom_call" | custom-call | flops 491520000 | tf_op jit(solution)/shard_map/pallas_call | solution.py:411
  (27 shorter events, 2.2 us)
Async XLA Ops:
  4.7 7.5 %copy-start.2 = (bf16[16,32,512]{2,1,0:T(8,128)(2,1)S(1)}, bf16[16,32,512]{2,1,0:T(8,128)(2,1)}, u32[]{:S(2)}) copy-start(bf16[16,32,512]{2,1,0:T(8,128)(2,1)} %back_hbm.1) | copy-start | bytes 1572868
  4.7 7.4 %copy-start.4 = (bf16[256,512]{1,0:T(8,128)(2,1)S(1)}, bf16[256,512]{1,0:T(8,128)(2,1)}, u32[]{:S(2)}) copy-start(bf16[256,512]{1,0:T(8,128)(2,1)} %proj_hbm.1) | copy-start | bytes 786436
  4.7 36.4 %all-to-all-start = ((bf16[32,136,128]{2,1,0:T(8,128)(2,1)}), bf16[32,136,128]{2,1,0:T(8,128)(2,1)}, u32[]{:S(2)}, u32[]{:S(2)}) async-start(bf16[32,136,128]{2,1,0:T(8,128)(2,1)} %shard_map.91), calls=%async_computation | async-start | bytes 2228224 | tf_op jit(solution)/shard_map/all_to_all | solution.py:520
  12.2 39.3 %copy-start = (bf16[4,512,512]{2,1,0:T(8,128)(2,1)S(1)}, bf16[4,512,512]{2,1,0:T(8,128)(2,1)}, u32[]{:S(2)}) copy-start(bf16[4,512,512]{2,1,0:T(8,128)(2,1)} %mix_ref.15) | copy-start | bytes 6291460
  12.3 0.7 copy-start.5
  13.0 38.5 %copy-start.1 = (f32[4,7,7,512]{3,0,2,1:T(4,128)S(1)}, f32[4,7,7,512]{3,0,2,1:T(4,128)}, u32[]{:S(2)}) copy-start(f32[4,7,7,512]{3,0,2,1:T(4,128)} %param.15) | copy-start | bytes 1204228
  13.0 38.5 %copy-start.3 = (f32[4,512]{1,0:T(4,128)S(1)}, f32[4,512]{1,0:T(4,128)}, u32[]{:S(2)}) copy-start(f32[4,512]{1,0:T(4,128)} %gains_ref.15) | copy-start | bytes 24580
  41.2 1.0 %copy-start.6 = (bf16[256,512]{1,0:T(8,128)(2,1)S(1)}, bf16[256,512]{1,0:T(8,128)(2,1)}, u32[]{:S(2)}) copy-start(bf16[256,512]{1,0:T(8,128)(2,1)} %copy-done.5) | copy-start | bytes 786436
  45.6 5.9 %collective-permute-start = (bf16[6,16,512]{2,1,0:T(8,128)(2,1)S(1)}, bf16[6,16,512]{2,1,0:T(8,128)(2,1)S(1)}, u32[]{:S(2)}, u32[]{:S(2)}) collective-permute-start(bf16[6,16,512]{2,1,0:T(8,128)(2,1)S(1)} %get-tuple-element.42), channel_id=1, source_target_pairs={{0,1},{1,2},{2,3},{3,4},{4,5},{5,6},{6,7},{7,0},{8,9},{9,10},{10,1... | collective-permute-start | bytes 294920 | tf_op jit(solution)/shard_map/ppermute | solution.py:491
  45.6 9.2 %collective-permute-start.1 = (bf16[6,32,512]{2,1,0:T(8,128)(2,1)S(1)}, bf16[6,32,512]{2,1,0:T(8,128)(2,1)S(1)}, u32[]{:S(2)}, u32[]{:S(2)}) collective-permute-start(bf16[6,32,512]{2,1,0:T(8,128)(2,1)S(1)} %get-tuple-element.40.edge_in), channel_id=1, source_target_pairs={{0,8},{8,16},{16,24},{24,0},{1,9},{9,17},{17,25},{25,1},{2,10},{10... | collective-permute-start | bytes 589832 | tf_op jit(solution)/shard_map/ppermute | solution.py:492
  46.5 8.3 %collective-permute-start.2 = (bf16[6,8,512]{2,1,0:T(8,128)(2,1)S(1)}, bf16[6,8,512]{2,1,0:T(8,128)(2,1)S(1)}, u32[]{:S(2)}, u32[]{:S(2)}) collective-permute-start(bf16[6,8,512]{2,1,0:T(8,128)(2,1)S(1)} %get-tuple-element.44), channel_id=1, source_target_pairs={{0,9},{1,10},{2,11},{3,12},{4,13},{5,14},{6,15},{7,8},{8,17},{9,18... | collective-permute-start | bytes 147464 | tf_op jit(solution)/shard_map/ppermute | solution.py:493
  56.9 2.8 %collective-permute-start.3 = (bf16[8,16,512]{2,1,0:T(8,128)(2,1)S(1)}, bf16[8,16,512]{2,1,0:T(8,128)(2,1)S(1)}, u32[]{:S(2)}, u32[]{:S(2)}) collective-permute-start(bf16[8,16,512]{2,1,0:T(8,128)(2,1)S(1)} %get-tuple-element.47), channel_id=1, source_target_pairs={{1,0},{2,1},{3,2},{4,3},{5,4},{6,5},{7,6},{0,7},{9,8},{10,9},{11,1... | collective-permute-start | bytes 393224 | tf_op jit(solution)/shard_map/ppermute | solution.py:491
  57.2 8.1 %collective-permute-start.4 = (bf16[6,32,512]{2,1,0:T(8,128)(2,1)S(1)}, bf16[6,32,512]{2,1,0:T(8,128)(2,1)S(1)}, u32[]{:S(2)}, u32[]{:S(2)}) collective-permute-start(bf16[6,32,512]{2,1,0:T(8,128)(2,1)S(1)} %get-tuple-element.48.edge_in), channel_id=1, source_target_pairs={{8,0},{16,8},{24,16},{0,24},{9,1},{17,9},{25,17},{1,25},{10,2},{18... | collective-permute-start | bytes 589832 | tf_op jit(solution)/shard_map/ppermute | solution.py:492
  59.1 6.1 %collective-permute-start.5 = (bf16[6,8,512]{2,1,0:T(8,128)(2,1)S(1)}, bf16[6,8,512]{2,1,0:T(8,128)(2,1)S(1)}, u32[]{:S(2)}, u32[]{:S(2)}) collective-permute-start(bf16[6,8,512]{2,1,0:T(8,128)(2,1)S(1)} %get-tuple-element.49), channel_id=1, source_target_pairs={{9,0},{10,1},{11,2},{12,3},{13,4},{14,5},{15,6},{8,7},{17,8},{18,9... | collective-permute-start | bytes 147464 | tf_op jit(solution)/shard_map/ppermute | solution.py:493
  67.4 5.9 %collective-permute-start.6 = (bf16[6,16,512]{2,1,0:T(8,128)(2,1)S(1)}, bf16[6,16,512]{2,1,0:T(8,128)(2,1)S(1)}, u32[]{:S(2)}, u32[]{:S(2)}) collective-permute-start(bf16[6,16,512]{2,1,0:T(8,128)(2,1)S(1)} %get-tuple-element.54), channel_id=1, source_target_pairs={{0,1},{1,2},{2,3},{3,4},{4,5},{5,6},{6,7},{7,0},{8,9},{9,10},{10,1... | collective-permute-start | bytes 294920 | tf_op jit(solution)/shard_map/ppermute | solution.py:491
  67.5 9.4 %collective-permute-start.7 = (bf16[6,32,512]{2,1,0:T(8,128)(2,1)S(1)}, bf16[6,32,512]{2,1,0:T(8,128)(2,1)S(1)}, u32[]{:S(2)}, u32[]{:S(2)}) collective-permute-start(bf16[6,32,512]{2,1,0:T(8,128)(2,1)S(1)} %get-tuple-element.53.edge_in), channel_id=1, source_target_pairs={{0,8},{8,16},{16,24},{24,0},{1,9},{9,17},{17,25},{25,1},{2,10},{10... | collective-permute-start | bytes 589832 | tf_op jit(solution)/shard_map/ppermute | solution.py:492
  68.1 8.8 %collective-permute-start.8 = (bf16[6,8,512]{2,1,0:T(8,128)(2,1)S(1)}, bf16[6,8,512]{2,1,0:T(8,128)(2,1)S(1)}, u32[]{:S(2)}, u32[]{:S(2)}) collective-permute-start(bf16[6,8,512]{2,1,0:T(8,128)(2,1)S(1)} %get-tuple-element.56), channel_id=1, source_target_pairs={{0,9},{1,10},{2,11},{3,12},{4,13},{5,14},{6,15},{7,8},{8,17},{9,18... | collective-permute-start | bytes 147464 | tf_op jit(solution)/shard_map/ppermute | solution.py:493
  78.9 4.3 %collective-permute-start.9 = (bf16[8,16,512]{2,1,0:T(8,128)(2,1)S(1)}, bf16[8,16,512]{2,1,0:T(8,128)(2,1)S(1)}, u32[]{:S(2)}, u32[]{:S(2)}) collective-permute-start(bf16[8,16,512]{2,1,0:T(8,128)(2,1)S(1)} %get-tuple-element.59), channel_id=1, source_target_pairs={{1,0},{2,1},{3,2},{4,3},{5,4},{6,5},{7,6},{0,7},{9,8},{10,9},{11,1... | collective-permute-start | bytes 393224 | tf_op jit(solution)/shard_map/ppermute | solution.py:491
  80.7 7.8 %collective-permute-start.10 = (bf16[6,32,512]{2,1,0:T(8,128)(2,1)S(1)}, bf16[6,32,512]{2,1,0:T(8,128)(2,1)S(1)}, u32[]{:S(2)}, u32[]{:S(2)}) collective-permute-start(bf16[6,32,512]{2,1,0:T(8,128)(2,1)S(1)} %get-tuple-element.60.edge_in), channel_id=1, source_target_pairs={{8,0},{16,8},{24,16},{0,24},{9,1},{17,9},{25,17},{1,25},{10,2},{18... | collective-permute-start | bytes 589832 | tf_op jit(solution)/shard_map/ppermute | solution.py:492
  82.8 4.1 %collective-permute-start.11 = (bf16[6,8,512]{2,1,0:T(8,128)(2,1)S(1)}, bf16[6,8,512]{2,1,0:T(8,128)(2,1)S(1)}, u32[]{:S(2)}, u32[]{:S(2)}) collective-permute-start(bf16[6,8,512]{2,1,0:T(8,128)(2,1)S(1)} %get-tuple-element.61), channel_id=1, source_target_pairs={{9,0},{10,1},{11,2},{12,3},{13,4},{14,5},{15,6},{8,7},{17,8},{18,9... | collective-permute-start | bytes 147464 | tf_op jit(solution)/shard_map/ppermute | solution.py:493

commit v4 on v1

--- a/solution.py
+++ b/solution.py
@@ -14,6 +14,8 @@
 SHIFT = 2 * HALO
 EDGE = 8
 TILE = 16
+PIECES = 4
+SPARE = 4
 WORK = 5000
 VMEM_LIMIT = 24 * 1024 * 1024
 PACK_LIMIT = 58 * 1024 * 1024
@@ -106,8 +108,31 @@
 
 
 def assim_kernel(
-    cap, step, got_ref, proj_ref, back_ref, edge_ref, inner_ref, lon_ref, corner_ref, wide_ref
+    cap,
+    step,
+    got_hbm,
+    proj_ref,
+    back_ref,
+    edge_ref,
+    left_ref,
+    right_ref,
+    lon_ref,
+    corner_ref,
+    got_ref,
+    wide_ref,
+    sems,
 ):
+    piece = got_ref.shape[0] // PIECES
+    copies = [
+        pltpu.make_async_copy(
+            got_hbm.at[k * piece : (k + 1) * piece],
+            got_ref.at[k * piece : (k + 1) * piece],
+            sems.at[k],
+        )
+        for k in range(PIECES)
+    ]
+    for copy in copies:
+        copy.start()
     devices, depth, _ = got_ref.shape
     rows, cols, chans = back_ref.shape
     cells = rows * cols
@@ -118,6 +143,8 @@
     cell = lax.broadcasted_iota(jnp.int32, (cells, LANES), 0)
     total = jnp.zeros((cells, feats), F32)
     for pair in range(0, devices // per, 2):
+        if pair * per % piece == 0:
+            copies[pair * per // piece].wait()
         maps = []
         blocks = []
         for chunk in (pair, pair + 1):
@@ -153,7 +180,8 @@
         wide_ref[g] = state[:, cols - EDGE :, lanes_of(g)].reshape(rows * EDGE, LANES)
     state = state.astype(BF16)
     edge_ref[...] = state[rows - SHIFT :]
-    inner_ref[...] = state[: rows - SHIFT]
+    left_ref[...] = state[: rows - SHIFT, :TILE]
+    right_ref[...] = state[: rows - SHIFT, TILE:]
     for x in range(SHIFT):
         for g in range(chans // LANES):
             column = wide_ref[g, pl.ds(EDGE - SHIFT + x, rows, stride=EDGE), :]
@@ -195,20 +223,25 @@
         spread_ref[p, first : first + count, :, lanes] = total
 
 
-def finish(taps_in, spread_ref, mix_ref, out_ref, layer, first, count):
+def finish(taps_in, spread_ref, mix_ref, out_ref, layer, first, count, stacked=1):
     chans = mix_ref.shape[1]
     ones = jnp.ones((chans, LANES), BF16)
-    for p in range(2):
-        spread = spread_ref[p, first : first + count].reshape(count * TILE, chans)
-        power = jnp.dot(spread * spread, ones, preferred_element_type=F32)
-        scale = 0.5 * lax.rsqrt(power * (1.0 / chans) + 1e-05)
-        mixed = jnp.dot(spread, mix_ref[layer], preferred_element_type=F32)
-        for g in range(chans // LANES):
-            moved = gelu(mixed[:, g * LANES : (g + 1) * LANES] * scale)
+    step = TILE // stacked
+    spread = spread_ref[:, first : first + count].reshape(2 * count * TILE, chans)
+    power = jnp.dot(spread * spread, ones, preferred_element_type=F32)
+    scale = 0.5 * lax.rsqrt(power * (1.0 / chans) + 1e-05)
+    mixed = jnp.dot(spread, mix_ref[layer], preferred_element_type=F32)
+    for g in range(chans // LANES):
+        moved = gelu(mixed[:, lanes_of(g)] * scale).reshape(2, count, TILE, LANES)
+        for p in range(2):
             center = taps_in[g, p + HALO, first + HALO : first + HALO + count].astype(F32)
-            fresh = center + moved.reshape(count, TILE, LANES)
+            fresh = center + moved[p]
             for k in range(count):
-                out_ref[g, first + k, pl.ds(p, TILE, stride=2), :] = fresh[k]
+                for h in range(stacked):
+                    row = first * stacked + h * count + k
+                    out_ref[g, row, pl.ds(p, step, stride=2), :] = fresh[
+                        k, h * step : (h + 1) * step
+                    ]
 
 
 def row_of(out_ref, y):
@@ -228,95 +261,92 @@
     return lax.axis_index("lat") == lax.axis_size("lat") - 1
 
 
-def inner_kernel(
-    shrink,
-    layer,
-    edge_in,
-    inner_in,
-    lon_in,
-    taps_ref,
-    mix_ref,
-    inner_ref,
-    lon_ref,
-    near_ref,
-    wide_ref,
-    taps_in,
-    tap_ref,
-    spread_ref,
-    out_ref,
-):
+def block_kernel(shrink, lead, layer, edge_in, left_in, right_in, *refs):
+    if lead:
+        taps_ref, mix_ref, block_ref, *scratch = refs
+    else:
+        lon_in, taps_ref, mix_ref, block_ref, lon_ref, near_ref, *scratch = refs
+    wide_ref, taps_in, tap_ref, spread_ref, out_ref = scratch
     cols = edge_in.shape[1]
     groups = wide_ref.shape[0]
     width = wide_ref.shape[2]
-    own = inner_in.shape[0] - (HALO if shrink else 0)
+    own = left_in.shape[0] - (SPARE if shrink else 0)
     rows = own + SHIFT
-    count = rows - SHIFT
     main = 0 if shrink else EDGE
     base = 0 if shrink else EDGE - SHIFT
-    side = cols if shrink else base
-
-    for g in range(groups):
-        for x in range(SHIFT):
-            column = lon_in[x, 0:rows, lanes_of(g)].astype(F32)
-            flat(wide_ref)[g, pl.ds(side + x, rows, stride=width), :] = column
-
-    def load(ref, place, y):
-        put(wide_ref, place, main, ref[y].astype(F32))
-        shifted(wide_ref, taps_in, base, place, place)
+    start = base + (0 if lead == shrink else TILE)
+
+    if not lead:
+        side = cols if shrink else base
+        for g in range(groups):
+            for x in range(SHIFT):
+                column = lon_in[x, 0:rows, lanes_of(g)].astype(F32)
+                flat(wide_ref)[g, pl.ds(side + x, rows, stride=width), :] = column
 
     @pl.loop(0, SHIFT, unroll=2)
     def _(y):
-        load(edge_in, y if shrink else own + y, y)
+        put(wide_ref, y if shrink else own + y, main, edge_in[y].astype(F32))
 
     @pl.loop(0, own, unroll=2)
     def _(y):
-        load(inner_in, y + SHIFT if shrink else y, y)
-
-    near = rows - SHIFT if shrink else 0
-    near_ref[...] = taps_in[:, :, near : near + SHIFT]
-
-    @pl.loop(0, groups)
-    def _(g):
-        convolve(taps_in, taps_ref, tap_ref, spread_ref, layer, g, 0, count)
-
-    finish(taps_in, spread_ref, mix_ref, out_ref, layer, 0, count)
-    edge = cols - SHIFT if shrink else 0
-    above = 0 if shrink else SHIFT
-    for g in range(groups):
-        for x in range(SHIFT):
-            column = flat(out_ref)[g, pl.ds(edge + x, count, stride=cols), :]
-            lon_ref[g, x, above : above + count, :] = column
-
-    @pl.loop(0, count, unroll=2)
-    def _(y):
-        inner_ref[y] = row_of(out_ref, y).astype(BF16)
-
+        place = y + SHIFT if shrink else y
+        put(wide_ref, place, main, left_in[y].astype(F32))
+        put(wide_ref, place, main + TILE, right_in[y].astype(F32))
+
+    def stage(top, high):
+        @pl.loop(0, high + TAPS - 1)
+        def _(y):
+            for g in range(groups):
+                for r in range(TAPS + 1):
+                    both = [
+                        wide_ref[g, top + y + h, pl.ds(start + r, TILE // 2, stride=2), :]
+                        for h in (0, high)
+                    ]
+                    taps_in[g, r, y] = jnp.concatenate(both, axis=0).astype(BF16)
+
+        @pl.loop(0, groups)
+        def _(g):
+            convolve(taps_in, taps_ref, tap_ref, spread_ref, layer, g, 0, high)
+
+        finish(taps_in, spread_ref, mix_ref, out_ref, layer, 0, high, 2)
+
+        @pl.loop(0, 2 * high, unroll=2)
+        def _(y):
+            block_ref[top + y] = row_of(out_ref, y).astype(BF16)
+
+    stage(0, own // 2)
+    if not lead:
+        edge = TILE - SHIFT if shrink else 0
+        above = 0 if shrink else SHIFT
+        near = rows - SHIFT if shrink else 0
+        for g in range(groups):
+            for x in range(SHIFT):
+                column = flat(out_ref)[g, pl.ds(edge + x, own, stride=TILE), :]
+                lon_ref[g, x, above : above + own, :] = column
+            for r in range(TAPS + 1):
+                for k in range(SHIFT):
+                    columns = pl.ds(base + r, TILE, stride=2)
+                    near_ref[g, r, k] = wide_ref[g, near + k, columns, :].astype(BF16)
     if not shrink:
 
         @pl.when(at_last())
         def _():
-            taps_in[:, :, rows:] = jnp.zeros((groups, TAPS + 1, HALO, TILE, LANES), BF16)
-
-            @pl.loop(0, groups)
-            def _(g):
-                convolve(taps_in, taps_ref, tap_ref, spread_ref, layer, g, count, HALO)
-
-            finish(taps_in, spread_ref, mix_ref, out_ref, layer, count, HALO)
-
-        for k in range(HALO):
-            inner_ref[count + k] = row_of(out_ref, count + k).astype(BF16)
+            wide_ref[:, rows:] = jnp.zeros((groups, SPARE, width, LANES), F32)
+            stage(own, SPARE // 2)
 
 
 def edge_kernel(
     shrink,
     final,
     layer,
-    inner_in,
+    left_in,
+    right_in,
     lon_in,
     lat_in,
     corner_in,
     near_ref,
-    inner_new,
+    left_new,
+    right_new,
     lon_new,
     taps_ref,
     mix_ref,
@@ -345,8 +375,9 @@
         if not shrink:
             value, beside = jnp.where(top, 0.0, value), jnp.where(top, 0.0, beside)
         elif k < HALO:
-            kept = inner_in.shape[0] - HALO
-            value = jnp.where(last, inner_in[kept + k].astype(F32), value)
+            kept = left_in.shape[0] - SPARE + k
+            inner = jnp.concatenate([left_in[kept], right_in[kept]], axis=0)
+            value = jnp.where(last, inner.astype(F32), value)
             beside = beside[:SHIFT]
             extra = [spare_ref[g, pl.ds(k, SHIFT, stride=HALO), :] for g in range(groups)]
             beside = jnp.where(last, jnp.concatenate(extra, axis=1), beside)
@@ -362,11 +393,12 @@
         convolve(taps_in, taps_ref, tap_ref, spread_ref, layer, g, 0, SHIFT)
 
     finish(taps_in, spread_ref, mix_ref, out_ref, layer, 0, SHIFT)
-    kept = inner_new.shape[0]
+    kept = left_new.shape[0]
     if final:
         for k in range(SHIFT):
             state_ref[kept + k] = row_of(out_ref, k).astype(BF16)
-        state_ref[0:kept] = inner_new[...]
+        state_ref[0:kept, 0:TILE, :] = left_new[...]
+        state_ref[0:kept, TILE:cols, :] = right_new[...]
         return
 
     for k in range(SHIFT):
@@ -388,7 +420,7 @@
             lon_ref[x, :, lanes_of(g)] = mix_lon[g, x].astype(BF16)
     if not shrink:
         for k in range(HALO):
-            value = inner_new[kept - HALO + k, 0:TILE, :].astype(F32)
+            value = left_new[kept - SPARE + k].astype(F32)
             for g in range(groups):
                 spare_ref[g, pl.ds(k, SHIFT, stride=HALO), :] = value[:SHIFT, lanes_of(g)]
         for g in range(groups):
@@ -427,24 +459,40 @@
 
 
 def layer(state, lon_out, corner_out, taps, mix, number, shrink, final):
-    edge, inner = state
+    edge, left, right = state
     lat_in, lon_in, corner_in = exchange((edge, lon_out, corner_out), not shrink)
     cols, chans = edge.shape[1:]
     groups = chans // LANES
-    rows = inner.shape[0] + SHIFT - (HALO if shrink else 0)
-    spare = 0 if shrink else HALO
-    made = rows - SHIFT + spare
-    inner_new, lon_new, near = call(
-        functools.partial(inner_kernel, shrink, number),
+    own = left.shape[0] - (SPARE if shrink else 0)
+    rows = own + SHIFT
+    spare = 0 if shrink else SPARE
+    made = own + spare
+    block = held(made, TILE, chans)
+    scratch = (
+        pltpu.VMEM((groups, rows + spare, cols + EDGE, LANES), F32),
+        pltpu.VMEM((groups, TAPS + 1, own // 2 + TAPS - 1, TILE, LANES), BF16),
+        pltpu.VMEM((TAPS * TAPS, TILE, LANES), BF16),
+        pltpu.VMEM((2, own // 2, TILE, chans), BF16),
+        pltpu.VMEM((groups, own, TILE, LANES), F32),
+    )
+    lead = call(
+        functools.partial(block_kernel, shrink, True, number),
+        block,
+        (edge, left, right, taps, mix),
+        scratch,
+    )
+    trail, lon_new, near = call(
+        functools.partial(block_kernel, shrink, False, number),
         (
-            held(made, cols, chans),
+            block,
             jax.ShapeDtypeStruct((groups, SHIFT, rows, LANES), F32),
             held(groups, TAPS + 1, SHIFT, TILE, LANES),
         ),
-        (edge, inner, lon_in, taps, mix),
-        scratch_of(groups, rows + spare, made, cols, chans),
+        (edge, left, right, lon_in, taps, mix),
+        scratch,
         work=made * cols * chans * WORK,
     )
+    new = (lead, trail) if shrink else (trail, lead)
     if final:
         outs = held(made + SHIFT, cols, chans)
     else:
@@ -456,7 +504,7 @@
     outs = call(
         functools.partial(edge_kernel, shrink, final, number),
         outs,
-        (inner, lon_in, lat_in, corner_in, near, inner_new, lon_new, taps, mix),
+        (left, right, lon_in, lat_in, corner_in, near, *new, lon_new, taps, mix),
         scratch_of(groups, 2 * SHIFT, SHIFT, cols, chans)
         + (
             pltpu.VMEM((groups, 2 * TILE, LANES), F32),
@@ -467,7 +515,7 @@
     if final:
         return outs
     edge, lon_out, corner_out = outs
-    return (edge, inner_new), lon_out, corner_out
+    return (edge, *new), lon_out, corner_out
 
 
 def exchange(pieces, forward):
@@ -522,18 +570,24 @@
         space=(pltpu.HBM, pltpu.HBM),
     )
     got, mix, proj, back = lax.optimization_barrier((got, mix, proj, back))
-    edge, inner, lon_out, corner_out = call(
+    edge, left, right, lon_out, corner_out = call(
         functools.partial(assim_kernel, cap, cols + 1),
         (
             held(SHIFT, cols, chans),
-            held(rows - SHIFT, cols, chans),
+            held(rows - SHIFT, TILE, chans),
+            held(rows - SHIFT, TILE, chans),
             held(SHIFT, rows, chans),
             held(SHIFT, EDGE, chans),
         ),
         (got, proj, back),
-        (pltpu.VMEM((chans // LANES, rows * EDGE, LANES), F32),),
-    )
-    state = (edge, inner)
+        (
+            pltpu.VMEM((devices, depth, LANES), BF16),
+            pltpu.VMEM((chans // LANES, rows * EDGE, LANES), F32),
+            pltpu.SemaphoreType.DMA((PIECES,)),
+        ),
+        space=(pltpu.HBM, pltpu.VMEM, pltpu.VMEM),
+    )
+    state = (edge, left, right)
     for n in range(layers - 1):
         state, lon_out, corner_out = layer(
             state, lon_out, corner_out, taps, mix, n, n % 2 == 1, False

time: 90.3 us -> 90.6 us (level)
  waiting for transfers between devices: 40.8 us -> 37.9 us
  Pallas kernels: 30.6 us -> 32.5 us
  starting transfers between devices: 16.2 us -> 17.6 us
    ppermute x4, waiting for transfers between devices: 10.4 us -> 5.5 us  [exchange(): lon = lax.ppermute(lon, 'lon', around)]
    ppermute x4, waiting for transfers between devices: 1.92 us -> 5.64 us  [exchange(): corner = lax.ppermute(corner, ('lat', 'lon'), across)]
    pallas_call x11 -> x15, Pallas kernels: 30.6 us -> 32.5 us  [call(): pl.pallas_call(kernel, out_shape=out_shape, in_specs=[pl.BlockSpec(memory...]
    ppermute x4, waiting for transfers between devices: 1.81 us -> 0.01 us  [exchange(): lat = lax.ppermute(lat, 'lat', along)]
  transfers between devices with their start and end apart: 13 -> 13, of which waited for: 8 -> 7; matrix products, arithmetic and copies ran while one was open for 2% -> 2% of each run, Pallas kernels for 15% -> 17%
where the time goes in v4:
time: 90.6 us; the launch traced here: 90.3 us
  waiting for transfers between devices  37.9 us (42%)
  Pallas kernels  32.5 us (36%)
  starting transfers between devices  17.6 us (19%)
  other arithmetic  2.11 us (2%)
    pallas_call x15, Pallas kernels, call(): pl.pallas_call(kernel, out_shape=out_shape, in_specs=[pl.BlockSpec(memory...  32.5 us
    all_to_all x1, waiting for transfers between devices, body(): lax.all_to_all(send, ('lat', 'lon'), split_axis=0, concat_axis=0, tiled=T...  26.7 us
    all_to_all x1, starting transfers between devices, body(): lax.all_to_all(send, ('lat', 'lon'), split_axis=0, concat_axis=0, tiled=T...  7.42 us
    ppermute x4, starting transfers between devices, exchange(): lat = lax.ppermute(lat, 'lat', along)  5.68 us
    ppermute x4, waiting for transfers between devices, exchange(): corner = lax.ppermute(corner, ('lat', 'lon'), across)  5.64 us
    ppermute x4, waiting for transfers between devices, exchange(): lon = lax.ppermute(lon, 'lon', around)  5.5 us
    ppermute x4, starting transfers between devices, exchange(): lon = lax.ppermute(lon, 'lon', around)  3.38 us
    convert_element_type x1, other arithmetic, body(): mix = (gains[:, :, None] * point_w.astype(F32)).astype(BF16)  2.11 us
  transfers between devices with their start and end apart: 13, of which 7 were waited for; matrix products, arithmetic and copies ran while one was open for 2% of the time, Pallas kernels for 17%

profile of v4, /device:TPU:0, one launch (start us, length us, event | category | flops | bytes accessed | tf_op | source)
XLA Modules:
  0.0 90.3 jit_solution(12176705415460216205)
XLA Ops:
  0.0 4.8 %shard_map.91 = bf16[32,136,128]{2,1,0:T(8,128)(2,1)} custom-call(s32[1,1024]{1,0:T(1,128)} %bitcast.20, s32[4,1024]{1,0:T(4,128)} %bitcast.18, bf16[4,1024]{1,0:T(4,128)(2,1)} %bitcast.19, bf16[1024,256]{1,0:T(8,128)(2,1)} %obs_hbm.1), custom_call_target="tpu_custom_call" | custom-call | tf_op jit(solution)/shard_map/pallas_call | solution.py:436
  4.8 7.4 %all-to-all-start = ((bf16[32,136,128]{2,1,0:T(8,128)(2,1)}), bf16[32,136,128]{2,1,0:T(8,128)(2,1)}, u32[]{:S(2)}, u32[]{:S(2)}) async-start(bf16[32,136,128]{2,1,0:T(8,128)(2,1)} %shard_map.91), calls=%async_computation | async-start | bytes 2228224 | tf_op jit(solution)/shard_map/all_to_all | solution.py:561
  12.3 2.1 %multiply_convert_fusion.refs_2_.refs_1_.mix_ref = bf16[4,512,512]{2,1,0:T(8,128)(2,1)S(1)} fusion(bf16[4,512,512]{2,1,0:T(8,128)(2,1)} %param.16, f32[4,512]{1,0:T(4,128)S(1)} %copy-done.3), kind=kLoop, calls=%fused_computation | loop fusion | flops 3145728 | bytes 4202496 | tf_op jit(solution)/shard_map/convert_element_type | solution.py:564
  14.5 26.7 %all-to-all-done.got_hbm = bf16[32,136,128]{2,1,0:T(8,128)(2,1)} async-done(((bf16[32,136,128]{2,1,0:T(8,128)(2,1)}), bf16[32,136,128]{2,1,0:T(8,128)(2,1)}, u32[]{:S(2)}, u32[]{:S(2)}) %all-to-all-start) | async-done | bytes 1114144 | tf_op jit(solution)/shard_map/all_to_all | solution.py:561
  41.2 3.3 %shard_map.93 = (bf16[6,32,512]{2,1,0:T(8,128)(2,1)S(1)}, bf16[10,16,512]{2,1,0:T(8,128)(2,1)S(1)}, bf16[10,16,512]{2,1,0:T(8,128)(2,1)S(1)}, bf16[6,16,512]{2,1,0:T(8,128)(2,1)S(1)}, bf16[6,8,512]{2,1,0:T(8,128)(2,1)S(1)}) custom-call(bf16[32,136,128]{2,1,0:T(8,128)(2,1)} %all-to-all-done.got_hbm, bf16[256,512]{1,0:T(8,128)(2,1)S(1)} %get-tuple-element.40.proj_ref, ...), custom_call_target="tpu_custom_call" | custom-call | tf_op jit(solution)/shard_map/pallas_call | solution.py:436
  46.3 1.8 %shard_map.95.right_new.right_in = bf16[14,16,512]{2,1,0:T(8,128)(2,1)S(1)} custom-call(bf16[6,32,512]{2,1,0:T(8,128)(2,1)S(1)} %get-tuple-element.42.edge_in, bf16[10,16,512]{2,1,0:T(8,128)(2,1)S(1)} %get-tuple-element.43.left_in, bf16[10,16,512]{2,1,0:T(8,128)(2,1)S(1)} %get-tuple-element.44.right_in, f32[49,4,512]{2,1,0:T(4,128)S(1)} %bitcast.6, ...), custom_call_target="tpu_custom_call" | custom-call | tf_op jit(solution)/shard_map/pallas_call | solution.py:436
  48.2 2.3 %collective-permute-done.refs_0_.lon_in = bf16[6,16,512]{2,1,0:T(8,128)(2,1)S(1)} collective-permute-done((bf16[6,16,512]{2,1,0:T(8,128)(2,1)S(1)}, bf16[6,16,512]{2,1,0:T(8,128)(2,1)S(1)}, u32[]{:S(2)}, u32[]{:S(2)}) %collective-permute-start) | collective-permute-done | bytes 98336 | tf_op jit(solution)/shard_map/ppermute | solution.py:532
  50.4 2.0 %shard_map.94 = (bf16[14,16,512]{2,1,0:T(8,128)(2,1)S(1)}, f32[4,6,16,128]{3,2,1,0:T(8,128)S(1)}, bf16[4,8,6,16,128]{4,3,2,1,0:T(8,128)(2,1)S(1)}) custom-call(bf16[6,32,512]{2,1,0:T(8,128)(2,1)S(1)} %get-tuple-element.42.edge_in, bf16[10,16,512]{2,1,0:T(8,128)(2,1)S(1)} %get-tuple-element.43.left_in, bf16[10,16,512]{2,1,0:T(8,128)(2,1)S(1)} %get-tuple-element.44.right_in, ...), custom_call_target="tpu_custom_call" | custom-call | flops 1146880000 | tf_op jit(solution)/shard_map/pallas_call | solution.py:436
  52.7 2.1 %shard_map.96 = (bf16[6,32,512]{2,1,0:T(8,128)(2,1)S(1)}, bf16[8,16,512]{2,1,0:T(8,128)(2,1)S(1)}, bf16[6,8,512]{2,1,0:T(8,128)(2,1)S(1)}) custom-call(bf16[10,16,512]{2,1,0:T(8,128)(2,1)S(1)} %get-tuple-element.43.left_in, bf16[10,16,512]{2,1,0:T(8,128)(2,1)S(1)} %get-tuple-element.44.right_in, bf16[6,16,512]{2,1,0:T(8,128)(2,1)S(1)} %collective-permute-done.refs_0_.lon_in, ...), custom_call_target="tpu_custom_call" | custom-call | flops 491520000 | tf_op jit(solution)/shard_map/pallas_call | solution.py:436
  56.2 3.2 %collective-permute-start.4 = (bf16[6,32,512]{2,1,0:T(8,128)(2,1)S(1)}, bf16[6,32,512]{2,1,0:T(8,128)(2,1)S(1)}, u32[]{:S(2)}, u32[]{:S(2)}) collective-permute-start(bf16[6,32,512]{2,1,0:T(8,128)(2,1)S(1)} %get-tuple-element.52.edge_in), channel_id=1, source_target_pairs={{8,0},{16,8},{24,16},{0,24},{9,1},{17,9},{25,17},{1,25},{10,2},{18... | collective-permute-start | bytes 589832 | tf_op jit(solution)/shard_map/ppermute | solution.py:533
  59.4 1.8 %shard_map.98.left_new.left_in = bf16[10,16,512]{2,1,0:T(8,128)(2,1)S(1)} custom-call(bf16[6,32,512]{2,1,0:T(8,128)(2,1)S(1)} %get-tuple-element.52.edge_in, bf16[14,16,512]{2,1,0:T(8,128)(2,1)S(1)} %get-tuple-element.47.left_new.left_in, bf16[14,16,512]{2,1,0:T(8,128)(2,1)S(1)} %shard_map.95.right_new.right_in, f32[49,4,512]{2,1,0:T(4,128)S(1)} %bitcast.9, ...), custom_call_target="tpu_custom_call" | custom-call | tf_op jit(solution)/shard_map/pallas_call | solution.py:436
  61.3 2.0 %shard_map.97 = (bf16[10,16,512]{2,1,0:T(8,128)(2,1)S(1)}, f32[4,6,16,128]{3,2,1,0:T(8,128)S(1)}, bf16[4,8,6,16,128]{4,3,2,1,0:T(8,128)(2,1)S(1)}) custom-call(bf16[6,32,512]{2,1,0:T(8,128)(2,1)S(1)} %get-tuple-element.52.edge_in, bf16[14,16,512]{2,1,0:T(8,128)(2,1)S(1)} %get-tuple-element.47.left_new.left_in, ...), custom_call_target="tpu_custom_call" | custom-call | flops 819200000 | tf_op jit(solution)/shard_map/pallas_call | solution.py:436
  63.3 1.5 %collective-permute-done.5.corner_in = bf16[6,8,512]{2,1,0:T(8,128)(2,1)S(1)} collective-permute-done((bf16[6,8,512]{2,1,0:T(8,128)(2,1)S(1)}, bf16[6,8,512]{2,1,0:T(8,128)(2,1)S(1)}, u32[]{:S(2)}, u32[]{:S(2)}) %collective-permute-start.5) | collective-permute-done | bytes 49184 | tf_op jit(solution)/shard_map/ppermute | solution.py:534
  64.8 2.1 %shard_map.99 = (bf16[6,32,512]{2,1,0:T(8,128)(2,1)S(1)}, bf16[6,16,512]{2,1,0:T(8,128)(2,1)S(1)}, bf16[6,8,512]{2,1,0:T(8,128)(2,1)S(1)}) custom-call(bf16[14,16,512]{2,1,0:T(8,128)(2,1)S(1)} %get-tuple-element.47.left_new.left_in, bf16[14,16,512]{2,1,0:T(8,128)(2,1)S(1)} %shard_map.95.right_new.right_in, ...), custom_call_target="tpu_custom_call" | custom-call | flops 491520000 | tf_op jit(solution)/shard_map/pallas_call | solution.py:436
  67.6 1.8 %shard_map.101.right_new.right_in = bf16[14,16,512]{2,1,0:T(8,128)(2,1)S(1)} custom-call(bf16[6,32,512]{2,1,0:T(8,128)(2,1)S(1)} %get-tuple-element.57.edge_in, bf16[10,16,512]{2,1,0:T(8,128)(2,1)S(1)} %shard_map.98.left_new.left_in, bf16[10,16,512]{2,1,0:T(8,128)(2,1)S(1)} %get-tuple-element.55.right_new.right_in, f32[49,4,512]{2,1,0:T(4,128)S(1)} %bitcast.12, ...), custom_call_target="tpu_custom_call" | custom-call | tf_op jit(solution)/shard_map/pallas_call | solution.py:436
  69.5 3.2 %collective-permute-done.6.refs_0_.lon_in = bf16[6,16,512]{2,1,0:T(8,128)(2,1)S(1)} collective-permute-done((bf16[6,16,512]{2,1,0:T(8,128)(2,1)S(1)}, bf16[6,16,512]{2,1,0:T(8,128)(2,1)S(1)}, u32[]{:S(2)}, u32[]{:S(2)}) %collective-permute-start.6) | collective-permute-done | bytes 98336 | tf_op jit(solution)/shard_map/ppermute | solution.py:532
  72.8 2.0 %shard_map.100 = (bf16[14,16,512]{2,1,0:T(8,128)(2,1)S(1)}, f32[4,6,16,128]{3,2,1,0:T(8,128)S(1)}, bf16[4,8,6,16,128]{4,3,2,1,0:T(8,128)(2,1)S(1)}) custom-call(bf16[6,32,512]{2,1,0:T(8,128)(2,1)S(1)} %get-tuple-element.57.edge_in, bf16[10,16,512]{2,1,0:T(8,128)(2,1)S(1)} %shard_map.98.left_new.left_in, ...), custom_call_target="tpu_custom_call" | custom-call | flops 1146880000 | tf_op jit(solution)/shard_map/pallas_call | solution.py:436
  74.8 2.4 %collective-permute-done.8.corner_in = bf16[6,8,512]{2,1,0:T(8,128)(2,1)S(1)} collective-permute-done((bf16[6,8,512]{2,1,0:T(8,128)(2,1)S(1)}, bf16[6,8,512]{2,1,0:T(8,128)(2,1)S(1)}, u32[]{:S(2)}, u32[]{:S(2)}) %collective-permute-start.8) | collective-permute-done | bytes 49184 | tf_op jit(solution)/shard_map/ppermute | solution.py:534
  77.2 2.1 %shard_map.102 = (bf16[6,32,512]{2,1,0:T(8,128)(2,1)S(1)}, bf16[8,16,512]{2,1,0:T(8,128)(2,1)S(1)}, bf16[6,8,512]{2,1,0:T(8,128)(2,1)S(1)}) custom-call(bf16[10,16,512]{2,1,0:T(8,128)(2,1)S(1)} %shard_map.98.left_new.left_in, bf16[10,16,512]{2,1,0:T(8,128)(2,1)S(1)} %get-tuple-element.55.right_new.right_in, ...), custom_call_target="tpu_custom_call" | custom-call | flops 491520000 | tf_op jit(solution)/shard_map/pallas_call | solution.py:436
  79.3 1.8 %collective-permute-start.9 = (bf16[8,16,512]{2,1,0:T(8,128)(2,1)S(1)}, bf16[8,16,512]{2,1,0:T(8,128)(2,1)S(1)}, u32[]{:S(2)}, u32[]{:S(2)}) collective-permute-start(bf16[8,16,512]{2,1,0:T(8,128)(2,1)S(1)} %get-tuple-element.63), channel_id=1, source_target_pairs={{1,0},{2,1},{3,2},{4,3},{5,4},{6,5},{7,6},{0,7},{9,8},{10,9},{11,1... | collective-permute-start | bytes 393224 | tf_op jit(solution)/shard_map/ppermute | solution.py:532
  82.1 1.8 %shard_map.104.left_new = bf16[10,16,512]{2,1,0:T(8,128)(2,1)S(1)} custom-call(bf16[6,32,512]{2,1,0:T(8,128)(2,1)S(1)} %get-tuple-element.64.edge_in, bf16[14,16,512]{2,1,0:T(8,128)(2,1)S(1)} %get-tuple-element.59.left_new.left_in, bf16[14,16,512]{2,1,0:T(8,128)(2,1)S(1)} %shard_map.101.right_new.right_in, f32[49,4,512]{2,1,0:T(4,128)S(1)} %bitcast.15, ...), custom_call_target="tpu_custom_call" | custom-call | tf_op jit(solution)/shard_map/pallas_call | solution.py:436
  84.0 2.0 %shard_map.103 = (bf16[10,16,512]{2,1,0:T(8,128)(2,1)S(1)}, f32[4,6,16,128]{3,2,1,0:T(8,128)S(1)}, bf16[4,8,6,16,128]{4,3,2,1,0:T(8,128)(2,1)S(1)}) custom-call(bf16[6,32,512]{2,1,0:T(8,128)(2,1)S(1)} %get-tuple-element.64.edge_in, bf16[14,16,512]{2,1,0:T(8,128)(2,1)S(1)} %get-tuple-element.59.left_new.left_in, ...), custom_call_target="tpu_custom_call" | custom-call | flops 819200000 | tf_op jit(solution)/shard_map/pallas_call | solution.py:436
  86.0 1.5 %collective-permute-done.11.corner_in = bf16[6,8,512]{2,1,0:T(8,128)(2,1)S(1)} collective-permute-done((bf16[6,8,512]{2,1,0:T(8,128)(2,1)S(1)}, bf16[6,8,512]{2,1,0:T(8,128)(2,1)S(1)}, u32[]{:S(2)}, u32[]{:S(2)}) %collective-permute-start.11) | collective-permute-done | bytes 49184 | tf_op jit(solution)/shard_map/ppermute | solution.py:534
  87.5 2.8 %shard_map.105 = bf16[16,32,512]{2,1,0:T(8,128)(2,1)} custom-call(bf16[14,16,512]{2,1,0:T(8,128)(2,1)S(1)} %get-tuple-element.59.left_new.left_in, bf16[14,16,512]{2,1,0:T(8,128)(2,1)S(1)} %shard_map.101.right_new.right_in, bf16[8,16,512]{2,1,0:T(8,128)(2,1)S(1)} %collective-permute-done.9.refs_0_.lon_in, ...), custom_call_target="tpu_custom_call" | custom-call | flops 491520000 | tf_op jit(solution)/shard_map/pallas_call | solution.py:436
  (26 shorter events, 5.5 us)
Async XLA Ops:
  0.0 12.2 %copy-start.2 = (bf16[256,512]{1,0:T(8,128)(2,1)S(1)}, bf16[256,512]{1,0:T(8,128)(2,1)}, u32[]{:S(2)}) copy-start(bf16[256,512]{1,0:T(8,128)(2,1)} %proj_hbm.1) | copy-start | bytes 786436
  0.0 12.2 %copy-start.1 = (bf16[16,32,512]{2,1,0:T(8,128)(2,1)S(1)}, bf16[16,32,512]{2,1,0:T(8,128)(2,1)}, u32[]{:S(2)}) copy-start(bf16[16,32,512]{2,1,0:T(8,128)(2,1)} %back_hbm.1) | copy-start | bytes 1572868
  0.0 12.3 %copy-start.3 = (f32[4,512]{1,0:T(4,128)S(1)}, f32[4,512]{1,0:T(4,128)}, u32[]{:S(2)}) copy-start(f32[4,512]{1,0:T(4,128)} %param.17) | copy-start | bytes 24580
  4.8 36.4 %all-to-all-start = ((bf16[32,136,128]{2,1,0:T(8,128)(2,1)}), bf16[32,136,128]{2,1,0:T(8,128)(2,1)}, u32[]{:S(2)}, u32[]{:S(2)}) async-start(bf16[32,136,128]{2,1,0:T(8,128)(2,1)} %shard_map.91), calls=%async_computation | async-start | bytes 2228224 | tf_op jit(solution)/shard_map/all_to_all | solution.py:561
  12.3 34.0 %copy-start = (f32[4,7,7,512]{3,0,2,1:T(4,128)S(1)}, f32[4,7,7,512]{3,0,2,1:T(4,128)}, u32[]{:S(2)}) copy-start(f32[4,7,7,512]{3,0,2,1:T(4,128)} %param.15) | copy-start | bytes 1204228
  44.5 5.9 %collective-permute-start = (bf16[6,16,512]{2,1,0:T(8,128)(2,1)S(1)}, bf16[6,16,512]{2,1,0:T(8,128)(2,1)S(1)}, u32[]{:S(2)}, u32[]{:S(2)}) collective-permute-start(bf16[6,16,512]{2,1,0:T(8,128)(2,1)S(1)} %get-tuple-element.45), channel_id=1, source_target_pairs={{0,1},{1,2},{2,3},{3,4},{4,5},{5,6},{6,7},{7,0},{8,9},{9,10},{10,1... | collective-permute-start | bytes 294920 | tf_op jit(solution)/shard_map/ppermute | solution.py:532
  44.6 8.1 %collective-permute-start.1 = (bf16[6,32,512]{2,1,0:T(8,128)(2,1)S(1)}, bf16[6,32,512]{2,1,0:T(8,128)(2,1)S(1)}, u32[]{:S(2)}, u32[]{:S(2)}) collective-permute-start(bf16[6,32,512]{2,1,0:T(8,128)(2,1)S(1)} %get-tuple-element.42.edge_in), channel_id=1, source_target_pairs={{0,8},{8,16},{16,24},{24,0},{1,9},{9,17},{17,25},{25,1},{2,10},{10... | collective-permute-start | bytes 589832 | tf_op jit(solution)/shard_map/ppermute | solution.py:533
  45.5 7.2 %collective-permute-start.2 = (bf16[6,8,512]{2,1,0:T(8,128)(2,1)S(1)}, bf16[6,8,512]{2,1,0:T(8,128)(2,1)S(1)}, u32[]{:S(2)}, u32[]{:S(2)}) collective-permute-start(bf16[6,8,512]{2,1,0:T(8,128)(2,1)S(1)} %get-tuple-element.48), channel_id=1, source_target_pairs={{0,9},{1,10},{2,11},{3,12},{4,13},{5,14},{6,15},{7,8},{8,17},{9,18... | collective-permute-start | bytes 147464 | tf_op jit(solution)/shard_map/ppermute | solution.py:534
  54.7 6.5 %collective-permute-start.3 = (bf16[8,16,512]{2,1,0:T(8,128)(2,1)S(1)}, bf16[8,16,512]{2,1,0:T(8,128)(2,1)S(1)}, u32[]{:S(2)}, u32[]{:S(2)}) collective-permute-start(bf16[8,16,512]{2,1,0:T(8,128)(2,1)S(1)} %get-tuple-element.51), channel_id=1, source_target_pairs={{1,0},{2,1},{3,2},{4,3},{5,4},{6,5},{7,6},{0,7},{9,8},{10,9},{11,1... | collective-permute-start | bytes 393224 | tf_op jit(solution)/shard_map/ppermute | solution.py:532
  56.2 8.6 %collective-permute-start.4 = (bf16[6,32,512]{2,1,0:T(8,128)(2,1)S(1)}, bf16[6,32,512]{2,1,0:T(8,128)(2,1)S(1)}, u32[]{:S(2)}, u32[]{:S(2)}) collective-permute-start(bf16[6,32,512]{2,1,0:T(8,128)(2,1)S(1)} %get-tuple-element.52.edge_in), channel_id=1, source_target_pairs={{8,0},{16,8},{24,16},{0,24},{9,1},{17,9},{25,17},{1,25},{10,2},{18... | collective-permute-start | bytes 589832 | tf_op jit(solution)/shard_map/ppermute | solution.py:533
  61.2 3.6 %collective-permute-start.5 = (bf16[6,8,512]{2,1,0:T(8,128)(2,1)S(1)}, bf16[6,8,512]{2,1,0:T(8,128)(2,1)S(1)}, u32[]{:S(2)}, u32[]{:S(2)}) collective-permute-start(bf16[6,8,512]{2,1,0:T(8,128)(2,1)S(1)} %get-tuple-element.53), channel_id=1, source_target_pairs={{9,0},{10,1},{11,2},{12,3},{13,4},{14,5},{15,6},{8,7},{17,8},{18,9... | collective-permute-start | bytes 147464 | tf_op jit(solution)/shard_map/ppermute | solution.py:534
  66.9 5.9 %collective-permute-start.6 = (bf16[6,16,512]{2,1,0:T(8,128)(2,1)S(1)}, bf16[6,16,512]{2,1,0:T(8,128)(2,1)S(1)}, u32[]{:S(2)}, u32[]{:S(2)}) collective-permute-start(bf16[6,16,512]{2,1,0:T(8,128)(2,1)S(1)} %get-tuple-element.58), channel_id=1, source_target_pairs={{0,1},{1,2},{2,3},{3,4},{4,5},{5,6},{6,7},{7,0},{8,9},{9,10},{10,1... | collective-permute-start | bytes 294920 | tf_op jit(solution)/shard_map/ppermute | solution.py:532
  66.9 10.3 %collective-permute-start.7 = (bf16[6,32,512]{2,1,0:T(8,128)(2,1)S(1)}, bf16[6,32,512]{2,1,0:T(8,128)(2,1)S(1)}, u32[]{:S(2)}, u32[]{:S(2)}) collective-permute-start(bf16[6,32,512]{2,1,0:T(8,128)(2,1)S(1)} %get-tuple-element.57.edge_in), channel_id=1, source_target_pairs={{0,8},{8,16},{16,24},{24,0},{1,9},{9,17},{17,25},{25,1},{2,10},{10... | collective-permute-start | bytes 589832 | tf_op jit(solution)/shard_map/ppermute | solution.py:533
  69.4 7.8 %collective-permute-start.8 = (bf16[6,8,512]{2,1,0:T(8,128)(2,1)S(1)}, bf16[6,8,512]{2,1,0:T(8,128)(2,1)S(1)}, u32[]{:S(2)}, u32[]{:S(2)}) collective-permute-start(bf16[6,8,512]{2,1,0:T(8,128)(2,1)S(1)} %get-tuple-element.60), channel_id=1, source_target_pairs={{0,9},{1,10},{2,11},{3,12},{4,13},{5,14},{6,15},{7,8},{8,17},{9,18... | collective-permute-start | bytes 147464 | tf_op jit(solution)/shard_map/ppermute | solution.py:534
  79.3 4.7 %collective-permute-start.9 = (bf16[8,16,512]{2,1,0:T(8,128)(2,1)S(1)}, bf16[8,16,512]{2,1,0:T(8,128)(2,1)S(1)}, u32[]{:S(2)}, u32[]{:S(2)}) collective-permute-start(bf16[8,16,512]{2,1,0:T(8,128)(2,1)S(1)} %get-tuple-element.63), channel_id=1, source_target_pairs={{1,0},{2,1},{3,2},{4,3},{5,4},{6,5},{7,6},{0,7},{9,8},{10,9},{11,1... | collective-permute-start | bytes 393224 | tf_op jit(solution)/shard_map/ppermute | solution.py:532
  81.1 6.4 %collective-permute-start.10 = (bf16[6,32,512]{2,1,0:T(8,128)(2,1)S(1)}, bf16[6,32,512]{2,1,0:T(8,128)(2,1)S(1)}, u32[]{:S(2)}, u32[]{:S(2)}) collective-permute-start(bf16[6,32,512]{2,1,0:T(8,128)(2,1)S(1)} %get-tuple-element.64.edge_in), channel_id=1, source_target_pairs={{8,0},{16,8},{24,16},{0,24},{9,1},{17,9},{25,17},{1,25},{10,2},{18... | collective-permute-start | bytes 589832 | tf_op jit(solution)/shard_map/ppermute | solution.py:533
  83.9 3.6 %collective-permute-start.11 = (bf16[6,8,512]{2,1,0:T(8,128)(2,1)S(1)}, bf16[6,8,512]{2,1,0:T(8,128)(2,1)S(1)}, u32[]{:S(2)}, u32[]{:S(2)}) collective-permute-start(bf16[6,8,512]{2,1,0:T(8,128)(2,1)S(1)} %get-tuple-element.65), channel_id=1, source_target_pairs={{9,0},{10,1},{11,2},{12,3},{13,4},{14,5},{15,6},{8,7},{17,8},{18,9... | collective-permute-start | bytes 147464 | tf_op jit(solution)/shard_map/ppermute | solution.py:534

commit v5 on v4

--- a/solution.py
+++ b/solution.py
@@ -480,6 +480,7 @@
         block,
         (edge, left, right, taps, mix),
         scratch,
+        work=made * TILE * chans * WORK,
     )
     trail, lon_new, near = call(
         functools.partial(block_kernel, shrink, False, number),
@@ -490,7 +491,7 @@
         ),
         (edge, left, right, lon_in, taps, mix),
         scratch,
-        work=made * cols * chans * WORK,
+        work=made * TILE * chans * WORK * 7 // 5,
     )
     new = (lead, trail) if shrink else (trail, lead)
     if final:

time: 90.6 us -> 88 us (0.971)
  waiting for transfers between devices: 37.9 us -> 33.7 us
  starting transfers between devices: 17.6 us -> 19.2 us
    ppermute x4, waiting for transfers between devices: 5.64 us -> 0.83 us  [exchange(): corner = lax.ppermute(corner, ('lat', 'lon'), across)]
    ppermute x4, starting transfers between devices: 1.1 us -> 2.71 us  [exchange(): corner = lax.ppermute(corner, ('lat', 'lon'), across)]
    ppermute x4, starting transfers between devices: 3.38 us -> 1.82 us  [exchange(): lon = lax.ppermute(lon, 'lon', around)]
    ppermute x4, starting transfers between devices: 5.68 us -> 7.21 us  [exchange(): lat = lax.ppermute(lat, 'lat', along)]
  transfers between devices with their start and end apart: 13 -> 13, of which waited for: 7 -> 6; matrix products, arithmetic and copies ran while one was open for 2% -> 2% of each run, Pallas kernels for 17% -> 18%
where the time goes in v5:
time: 88 us; the launch traced here: 87.8 us
  waiting for transfers between devices  33.7 us (38%)
  Pallas kernels  32.6 us (37%)
  starting transfers between devices  19.2 us (22%)
  other arithmetic  2.11 us (2%)
    pallas_call x15, Pallas kernels, call(): pl.pallas_call(kernel, out_shape=out_shape, in_specs=[pl.BlockSpec(memory...  32.6 us
    all_to_all x1, waiting for transfers between devices, body(): lax.all_to_all(send, ('lat', 'lon'), split_axis=0, concat_axis=0, tiled=T...  26.7 us
    all_to_all x1, starting transfers between devices, body(): lax.all_to_all(send, ('lat', 'lon'), split_axis=0, concat_axis=0, tiled=T...  7.42 us
    ppermute x4, starting transfers between devices, exchange(): lat = lax.ppermute(lat, 'lat', along)  7.21 us
    ppermute x4, waiting for transfers between devices, exchange(): lon = lax.ppermute(lon, 'lon', around)  6.14 us
    ppermute x4, starting transfers between devices, exchange(): corner = lax.ppermute(corner, ('lat', 'lon'), across)  2.71 us
    convert_element_type x1, other arithmetic, body(): mix = (gains[:, :, None] * point_w.astype(F32)).astype(BF16)  2.11 us
    ppermute x4, starting transfers between devices, exchange(): lon = lax.ppermute(lon, 'lon', around)  1.82 us
  transfers between devices with their start and end apart: 13, of which 6 were waited for; matrix products, arithmetic and copies ran while one was open for 2% of the time, Pallas kernels for 18%

profile of v5, /device:TPU:0, one launch (start us, length us, event | category | flops | bytes accessed | tf_op | source)
XLA Modules:
  0.0 87.8 jit_solution(4442753143529972194)
XLA Ops:
  0.0 4.8 %shard_map.91 = bf16[32,136,128]{2,1,0:T(8,128)(2,1)} custom-call(s32[1,1024]{1,0:T(1,128)} %bitcast.20, s32[4,1024]{1,0:T(4,128)} %bitcast.18, bf16[4,1024]{1,0:T(4,128)(2,1)} %bitcast.19, bf16[1024,256]{1,0:T(8,128)(2,1)} %obs_hbm.1), custom_call_target="tpu_custom_call" | custom-call | tf_op jit(solution)/shard_map/pallas_call | solution.py:436
  4.8 7.4 %all-to-all-start = ((bf16[32,136,128]{2,1,0:T(8,128)(2,1)}), bf16[32,136,128]{2,1,0:T(8,128)(2,1)}, u32[]{:S(2)}, u32[]{:S(2)}) async-start(bf16[32,136,128]{2,1,0:T(8,128)(2,1)} %shard_map.91), calls=%async_computation | async-start | bytes 2228224 | tf_op jit(solution)/shard_map/all_to_all | solution.py:562
  12.3 2.1 %multiply_convert_fusion.refs_2_.refs_1_.mix_ref = bf16[4,512,512]{2,1,0:T(8,128)(2,1)S(1)} fusion(bf16[4,512,512]{2,1,0:T(8,128)(2,1)} %param.16, f32[4,512]{1,0:T(4,128)S(1)} %copy-done.3), kind=kLoop, calls=%fused_computation | loop fusion | flops 3145728 | bytes 4202496 | tf_op jit(solution)/shard_map/convert_element_type | solution.py:565
  14.5 26.7 %all-to-all-done.got_hbm = bf16[32,136,128]{2,1,0:T(8,128)(2,1)} async-done(((bf16[32,136,128]{2,1,0:T(8,128)(2,1)}), bf16[32,136,128]{2,1,0:T(8,128)(2,1)}, u32[]{:S(2)}, u32[]{:S(2)}) %all-to-all-start) | async-done | bytes 1114144 | tf_op jit(solution)/shard_map/all_to_all | solution.py:562
  41.2 3.3 %shard_map.93 = (bf16[6,32,512]{2,1,0:T(8,128)(2,1)S(1)}, bf16[10,16,512]{2,1,0:T(8,128)(2,1)S(1)}, bf16[10,16,512]{2,1,0:T(8,128)(2,1)S(1)}, bf16[6,16,512]{2,1,0:T(8,128)(2,1)S(1)}, bf16[6,8,512]{2,1,0:T(8,128)(2,1)S(1)}) custom-call(bf16[32,136,128]{2,1,0:T(8,128)(2,1)} %all-to-all-done.got_hbm, bf16[256,512]{1,0:T(8,128)(2,1)S(1)} %get-tuple-element.40.proj_ref, ...), custom_call_target="tpu_custom_call" | custom-call | tf_op jit(solution)/shard_map/pallas_call | solution.py:436
  45.2 1.1 %collective-permute-start.2 = (bf16[6,8,512]{2,1,0:T(8,128)(2,1)S(1)}, bf16[6,8,512]{2,1,0:T(8,128)(2,1)S(1)}, u32[]{:S(2)}, u32[]{:S(2)}) collective-permute-start(bf16[6,8,512]{2,1,0:T(8,128)(2,1)S(1)} %get-tuple-element.48), channel_id=1, source_target_pairs={{0,9},{1,10},{2,11},{3,12},{4,13},{5,14},{6,15},{7,8},{8,17},{9,18... | collective-permute-start | bytes 147464 | tf_op jit(solution)/shard_map/ppermute | solution.py:535
  46.2 1.8 %shard_map.95.right_new.right_in = bf16[14,16,512]{2,1,0:T(8,128)(2,1)S(1)} custom-call(bf16[6,32,512]{2,1,0:T(8,128)(2,1)S(1)} %get-tuple-element.42.edge_in, bf16[10,16,512]{2,1,0:T(8,128)(2,1)S(1)} %get-tuple-element.43.left_in, bf16[10,16,512]{2,1,0:T(8,128)(2,1)S(1)} %get-tuple-element.44.right_in, f32[49,4,512]{2,1,0:T(4,128)S(1)} %bitcast.6, ...), custom_call_target="tpu_custom_call" | custom-call | flops 573440000 | tf_op jit(solution)/shard_map/pallas_call | solution.py:436
  48.1 2.4 %collective-permute-done.refs_0_.lon_in = bf16[6,16,512]{2,1,0:T(8,128)(2,1)S(1)} collective-permute-done((bf16[6,16,512]{2,1,0:T(8,128)(2,1)S(1)}, bf16[6,16,512]{2,1,0:T(8,128)(2,1)S(1)}, u32[]{:S(2)}, u32[]{:S(2)}) %collective-permute-start) | collective-permute-done | bytes 98336 | tf_op jit(solution)/shard_map/ppermute | solution.py:533
  50.5 2.0 %shard_map.94 = (bf16[14,16,512]{2,1,0:T(8,128)(2,1)S(1)}, f32[4,6,16,128]{3,2,1,0:T(8,128)S(1)}, bf16[4,8,6,16,128]{4,3,2,1,0:T(8,128)(2,1)S(1)}) custom-call(bf16[6,32,512]{2,1,0:T(8,128)(2,1)S(1)} %get-tuple-element.42.edge_in, bf16[10,16,512]{2,1,0:T(8,128)(2,1)S(1)} %get-tuple-element.43.left_in, bf16[10,16,512]{2,1,0:T(8,128)(2,1)S(1)} %get-tuple-element.44.right_in, ...), custom_call_target="tpu_custom_call" | custom-call | flops 802816000 | tf_op jit(solution)/shard_map/pallas_call | solution.py:436
  53.3 2.1 %shard_map.96 = (bf16[6,32,512]{2,1,0:T(8,128)(2,1)S(1)}, bf16[8,16,512]{2,1,0:T(8,128)(2,1)S(1)}, bf16[6,8,512]{2,1,0:T(8,128)(2,1)S(1)}) custom-call(bf16[10,16,512]{2,1,0:T(8,128)(2,1)S(1)} %get-tuple-element.43.left_in, bf16[10,16,512]{2,1,0:T(8,128)(2,1)S(1)} %get-tuple-element.44.right_in, bf16[6,16,512]{2,1,0:T(8,128)(2,1)S(1)} %collective-permute-done.refs_0_.lon_in, ...), custom_call_target="tpu_custom_call" | custom-call | flops 491520000 | tf_op jit(solution)/shard_map/pallas_call | solution.py:436
  55.4 3.1 %collective-permute-start.4 = (bf16[6,32,512]{2,1,0:T(8,128)(2,1)S(1)}, bf16[6,32,512]{2,1,0:T(8,128)(2,1)S(1)}, u32[]{:S(2)}, u32[]{:S(2)}) collective-permute-start(bf16[6,32,512]{2,1,0:T(8,128)(2,1)S(1)} %get-tuple-element.52.edge_in), channel_id=1, source_target_pairs={{8,0},{16,8},{24,16},{0,24},{9,1},{17,9},{25,17},{1,25},{10,2},{18... | collective-permute-start | bytes 589832 | tf_op jit(solution)/shard_map/ppermute | solution.py:534
  58.8 1.8 %shard_map.98.left_new.left_in = bf16[10,16,512]{2,1,0:T(8,128)(2,1)S(1)} custom-call(bf16[6,32,512]{2,1,0:T(8,128)(2,1)S(1)} %get-tuple-element.52.edge_in, bf16[14,16,512]{2,1,0:T(8,128)(2,1)S(1)} %get-tuple-element.47.left_new.left_in, bf16[14,16,512]{2,1,0:T(8,128)(2,1)S(1)} %shard_map.95.right_new.right_in, f32[49,4,512]{2,1,0:T(4,128)S(1)} %bitcast.9, ...), custom_call_target="tpu_custom_call" | custom-call | flops 409600000 | tf_op jit(solution)/shard_map/pallas_call | solution.py:436
  61.3 2.0 %shard_map.97 = (bf16[10,16,512]{2,1,0:T(8,128)(2,1)S(1)}, f32[4,6,16,128]{3,2,1,0:T(8,128)S(1)}, bf16[4,8,6,16,128]{4,3,2,1,0:T(8,128)(2,1)S(1)}) custom-call(bf16[6,32,512]{2,1,0:T(8,128)(2,1)S(1)} %get-tuple-element.52.edge_in, bf16[14,16,512]{2,1,0:T(8,128)(2,1)S(1)} %get-tuple-element.47.left_new.left_in, ...), custom_call_target="tpu_custom_call" | custom-call | flops 573440000 | tf_op jit(solution)/shard_map/pallas_call | solution.py:436
  63.4 2.1 %shard_map.99 = (bf16[6,32,512]{2,1,0:T(8,128)(2,1)S(1)}, bf16[6,16,512]{2,1,0:T(8,128)(2,1)S(1)}, bf16[6,8,512]{2,1,0:T(8,128)(2,1)S(1)}) custom-call(bf16[14,16,512]{2,1,0:T(8,128)(2,1)S(1)} %get-tuple-element.47.left_new.left_in, bf16[14,16,512]{2,1,0:T(8,128)(2,1)S(1)} %shard_map.95.right_new.right_in, ...), custom_call_target="tpu_custom_call" | custom-call | flops 491520000 | tf_op jit(solution)/shard_map/pallas_call | solution.py:436
  65.5 1.3 %collective-permute-start.7 = (bf16[6,32,512]{2,1,0:T(8,128)(2,1)S(1)}, bf16[6,32,512]{2,1,0:T(8,128)(2,1)S(1)}, u32[]{:S(2)}, u32[]{:S(2)}) collective-permute-start(bf16[6,32,512]{2,1,0:T(8,128)(2,1)S(1)} %get-tuple-element.57.edge_in), channel_id=1, source_target_pairs={{0,8},{8,16},{16,24},{24,0},{1,9},{9,17},{17,25},{25,1},{2,10},{10... | collective-permute-start | bytes 589832 | tf_op jit(solution)/shard_map/ppermute | solution.py:534
  66.8 1.2 %collective-permute-start.8 = (bf16[6,8,512]{2,1,0:T(8,128)(2,1)S(1)}, bf16[6,8,512]{2,1,0:T(8,128)(2,1)S(1)}, u32[]{:S(2)}, u32[]{:S(2)}) collective-permute-start(bf16[6,8,512]{2,1,0:T(8,128)(2,1)S(1)} %get-tuple-element.60), channel_id=1, source_target_pairs={{0,9},{1,10},{2,11},{3,12},{4,13},{5,14},{6,15},{7,8},{8,17},{9,18... | collective-permute-start | bytes 147464 | tf_op jit(solution)/shard_map/ppermute | solution.py:535
  67.9 1.8 %shard_map.101.right_new.right_in = bf16[14,16,512]{2,1,0:T(8,128)(2,1)S(1)} custom-call(bf16[6,32,512]{2,1,0:T(8,128)(2,1)S(1)} %get-tuple-element.57.edge_in, bf16[10,16,512]{2,1,0:T(8,128)(2,1)S(1)} %shard_map.98.left_new.left_in, bf16[10,16,512]{2,1,0:T(8,128)(2,1)S(1)} %get-tuple-element.55.right_new.right_in, f32[49,4,512]{2,1,0:T(4,128)S(1)} %bitcast.12, ...), custom_call_target="tpu_custom_call" | custom-call | flops 573440000 | tf_op jit(solution)/shard_map/pallas_call | solution.py:436
  69.8 2.8 %collective-permute-done.6.refs_0_.lon_in = bf16[6,16,512]{2,1,0:T(8,128)(2,1)S(1)} collective-permute-done((bf16[6,16,512]{2,1,0:T(8,128)(2,1)S(1)}, bf16[6,16,512]{2,1,0:T(8,128)(2,1)S(1)}, u32[]{:S(2)}, u32[]{:S(2)}) %collective-permute-start.6) | collective-permute-done | bytes 98336 | tf_op jit(solution)/shard_map/ppermute | solution.py:533
  72.6 2.0 %shard_map.100 = (bf16[14,16,512]{2,1,0:T(8,128)(2,1)S(1)}, f32[4,6,16,128]{3,2,1,0:T(8,128)S(1)}, bf16[4,8,6,16,128]{4,3,2,1,0:T(8,128)(2,1)S(1)}) custom-call(bf16[6,32,512]{2,1,0:T(8,128)(2,1)S(1)} %get-tuple-element.57.edge_in, bf16[10,16,512]{2,1,0:T(8,128)(2,1)S(1)} %shard_map.98.left_new.left_in, ...), custom_call_target="tpu_custom_call" | custom-call | flops 802816000 | tf_op jit(solution)/shard_map/pallas_call | solution.py:436
  74.6 2.1 %shard_map.102 = (bf16[6,32,512]{2,1,0:T(8,128)(2,1)S(1)}, bf16[8,16,512]{2,1,0:T(8,128)(2,1)S(1)}, bf16[6,8,512]{2,1,0:T(8,128)(2,1)S(1)}) custom-call(bf16[10,16,512]{2,1,0:T(8,128)(2,1)S(1)} %shard_map.98.left_new.left_in, bf16[10,16,512]{2,1,0:T(8,128)(2,1)S(1)} %get-tuple-element.55.right_new.right_in, ...), custom_call_target="tpu_custom_call" | custom-call | flops 491520000 | tf_op jit(solution)/shard_map/pallas_call | solution.py:436
  76.7 2.7 %collective-permute-start.10 = (bf16[6,32,512]{2,1,0:T(8,128)(2,1)S(1)}, bf16[6,32,512]{2,1,0:T(8,128)(2,1)S(1)}, u32[]{:S(2)}, u32[]{:S(2)}) collective-permute-start(bf16[6,32,512]{2,1,0:T(8,128)(2,1)S(1)} %get-tuple-element.64.edge_in), channel_id=1, source_target_pairs={{8,0},{16,8},{24,16},{0,24},{9,1},{17,9},{25,17},{1,25},{10,2},{18... | collective-permute-start | bytes 589832 | tf_op jit(solution)/shard_map/ppermute | solution.py:534
  80.8 1.8 %shard_map.104.left_new = bf16[10,16,512]{2,1,0:T(8,128)(2,1)S(1)} custom-call(bf16[6,32,512]{2,1,0:T(8,128)(2,1)S(1)} %get-tuple-element.64.edge_in, bf16[14,16,512]{2,1,0:T(8,128)(2,1)S(1)} %get-tuple-element.59.left_new.left_in, bf16[14,16,512]{2,1,0:T(8,128)(2,1)S(1)} %shard_map.101.right_new.right_in, f32[49,4,512]{2,1,0:T(4,128)S(1)} %bitcast.15, ...), custom_call_target="tpu_custom_call" | custom-call | flops 409600000 | tf_op jit(solution)/shard_map/pallas_call | solution.py:436
  82.9 2.0 %shard_map.103 = (bf16[10,16,512]{2,1,0:T(8,128)(2,1)S(1)}, f32[4,6,16,128]{3,2,1,0:T(8,128)S(1)}, bf16[4,8,6,16,128]{4,3,2,1,0:T(8,128)(2,1)S(1)}) custom-call(bf16[6,32,512]{2,1,0:T(8,128)(2,1)S(1)} %get-tuple-element.64.edge_in, bf16[14,16,512]{2,1,0:T(8,128)(2,1)S(1)} %get-tuple-element.59.left_new.left_in, ...), custom_call_target="tpu_custom_call" | custom-call | flops 573440000 | tf_op jit(solution)/shard_map/pallas_call | solution.py:436
  84.9 2.8 %shard_map.105 = bf16[16,32,512]{2,1,0:T(8,128)(2,1)} custom-call(bf16[14,16,512]{2,1,0:T(8,128)(2,1)S(1)} %get-tuple-element.59.left_new.left_in, bf16[14,16,512]{2,1,0:T(8,128)(2,1)S(1)} %shard_map.101.right_new.right_in, bf16[8,16,512]{2,1,0:T(8,128)(2,1)S(1)} %collective-permute-done.9.refs_0_.lon_in, ...), custom_call_target="tpu_custom_call" | custom-call | flops 491520000 | tf_op jit(solution)/shard_map/pallas_call | solution.py:436
  (26 shorter events, 4.2 us)
Async XLA Ops:
  0.0 12.2 %copy-start.2 = (bf16[256,512]{1,0:T(8,128)(2,1)S(1)}, bf16[256,512]{1,0:T(8,128)(2,1)}, u32[]{:S(2)}) copy-start(bf16[256,512]{1,0:T(8,128)(2,1)} %proj_hbm.1) | copy-start | bytes 786436
  0.0 12.2 %copy-start.1 = (bf16[16,32,512]{2,1,0:T(8,128)(2,1)S(1)}, bf16[16,32,512]{2,1,0:T(8,128)(2,1)}, u32[]{:S(2)}) copy-start(bf16[16,32,512]{2,1,0:T(8,128)(2,1)} %back_hbm.1) | copy-start | bytes 1572868
  0.0 12.3 %copy-start.3 = (f32[4,512]{1,0:T(4,128)S(1)}, f32[4,512]{1,0:T(4,128)}, u32[]{:S(2)}) copy-start(f32[4,512]{1,0:T(4,128)} %param.17) | copy-start | bytes 24580
  4.8 36.4 %all-to-all-start = ((bf16[32,136,128]{2,1,0:T(8,128)(2,1)}), bf16[32,136,128]{2,1,0:T(8,128)(2,1)}, u32[]{:S(2)}, u32[]{:S(2)}) async-start(bf16[32,136,128]{2,1,0:T(8,128)(2,1)} %shard_map.91), calls=%async_computation | async-start | bytes 2228224 | tf_op jit(solution)/shard_map/all_to_all | solution.py:562
  12.3 33.9 %copy-start = (f32[4,7,7,512]{3,0,2,1:T(4,128)S(1)}, f32[4,7,7,512]{3,0,2,1:T(4,128)}, u32[]{:S(2)}) copy-start(f32[4,7,7,512]{3,0,2,1:T(4,128)} %param.15) | copy-start | bytes 1204228
  44.5 8.8 %collective-permute-start.1 = (bf16[6,32,512]{2,1,0:T(8,128)(2,1)S(1)}, bf16[6,32,512]{2,1,0:T(8,128)(2,1)S(1)}, u32[]{:S(2)}, u32[]{:S(2)}) collective-permute-start(bf16[6,32,512]{2,1,0:T(8,128)(2,1)S(1)} %get-tuple-element.42.edge_in), channel_id=1, source_target_pairs={{0,8},{8,16},{16,24},{24,0},{1,9},{9,17},{17,25},{25,1},{2,10},{10... | collective-permute-start | bytes 589832 | tf_op jit(solution)/shard_map/ppermute | solution.py:534
  44.6 5.9 %collective-permute-start = (bf16[6,16,512]{2,1,0:T(8,128)(2,1)S(1)}, bf16[6,16,512]{2,1,0:T(8,128)(2,1)S(1)}, u32[]{:S(2)}, u32[]{:S(2)}) collective-permute-start(bf16[6,16,512]{2,1,0:T(8,128)(2,1)S(1)} %get-tuple-element.45), channel_id=1, source_target_pairs={{0,1},{1,2},{2,3},{3,4},{4,5},{5,6},{6,7},{7,0},{8,9},{9,10},{10,1... | collective-permute-start | bytes 294920 | tf_op jit(solution)/shard_map/ppermute | solution.py:533
  45.2 8.1 %collective-permute-start.2 = (bf16[6,8,512]{2,1,0:T(8,128)(2,1)S(1)}, bf16[6,8,512]{2,1,0:T(8,128)(2,1)S(1)}, u32[]{:S(2)}, u32[]{:S(2)}) collective-permute-start(bf16[6,8,512]{2,1,0:T(8,128)(2,1)S(1)} %get-tuple-element.48), channel_id=1, source_target_pairs={{0,9},{1,10},{2,11},{3,12},{4,13},{5,14},{6,15},{7,8},{8,17},{9,18... | collective-permute-start | bytes 147464 | tf_op jit(solution)/shard_map/ppermute | solution.py:535
  55.4 8.0 %collective-permute-start.4 = (bf16[6,32,512]{2,1,0:T(8,128)(2,1)S(1)}, bf16[6,32,512]{2,1,0:T(8,128)(2,1)S(1)}, u32[]{:S(2)}, u32[]{:S(2)}) collective-permute-start(bf16[6,32,512]{2,1,0:T(8,128)(2,1)S(1)} %get-tuple-element.52.edge_in), channel_id=1, source_target_pairs={{8,0},{16,8},{24,16},{0,24},{9,1},{17,9},{25,17},{1,25},{10,2},{18... | collective-permute-start | bytes 589832 | tf_op jit(solution)/shard_map/ppermute | solution.py:534
  58.5 2.8 %collective-permute-start.3 = (bf16[8,16,512]{2,1,0:T(8,128)(2,1)S(1)}, bf16[8,16,512]{2,1,0:T(8,128)(2,1)S(1)}, u32[]{:S(2)}, u32[]{:S(2)}) collective-permute-start(bf16[8,16,512]{2,1,0:T(8,128)(2,1)S(1)} %get-tuple-element.51), channel_id=1, source_target_pairs={{1,0},{2,1},{3,2},{4,3},{5,4},{6,5},{7,6},{0,7},{9,8},{10,9},{11,1... | collective-permute-start | bytes 393224 | tf_op jit(solution)/shard_map/ppermute | solution.py:533
  58.8 4.5 %collective-permute-start.5 = (bf16[6,8,512]{2,1,0:T(8,128)(2,1)S(1)}, bf16[6,8,512]{2,1,0:T(8,128)(2,1)S(1)}, u32[]{:S(2)}, u32[]{:S(2)}) collective-permute-start(bf16[6,8,512]{2,1,0:T(8,128)(2,1)S(1)} %get-tuple-element.53), channel_id=1, source_target_pairs={{9,0},{10,1},{11,2},{12,3},{13,4},{14,5},{15,6},{8,7},{17,8},{18,9... | collective-permute-start | bytes 147464 | tf_op jit(solution)/shard_map/ppermute | solution.py:535
  65.5 9.1 %collective-permute-start.7 = (bf16[6,32,512]{2,1,0:T(8,128)(2,1)S(1)}, bf16[6,32,512]{2,1,0:T(8,128)(2,1)S(1)}, u32[]{:S(2)}, u32[]{:S(2)}) collective-permute-start(bf16[6,32,512]{2,1,0:T(8,128)(2,1)S(1)} %get-tuple-element.57.edge_in), channel_id=1, source_target_pairs={{0,8},{8,16},{16,24},{24,0},{1,9},{9,17},{17,25},{25,1},{2,10},{10... | collective-permute-start | bytes 589832 | tf_op jit(solution)/shard_map/ppermute | solution.py:534
  66.7 5.8 %collective-permute-start.6 = (bf16[6,16,512]{2,1,0:T(8,128)(2,1)S(1)}, bf16[6,16,512]{2,1,0:T(8,128)(2,1)S(1)}, u32[]{:S(2)}, u32[]{:S(2)}) collective-permute-start(bf16[6,16,512]{2,1,0:T(8,128)(2,1)S(1)} %get-tuple-element.58), channel_id=1, source_target_pairs={{0,1},{1,2},{2,3},{3,4},{4,5},{5,6},{6,7},{7,0},{8,9},{9,10},{10,1... | collective-permute-start | bytes 294920 | tf_op jit(solution)/shard_map/ppermute | solution.py:533
  66.8 7.8 %collective-permute-start.8 = (bf16[6,8,512]{2,1,0:T(8,128)(2,1)S(1)}, bf16[6,8,512]{2,1,0:T(8,128)(2,1)S(1)}, u32[]{:S(2)}, u32[]{:S(2)}) collective-permute-start(bf16[6,8,512]{2,1,0:T(8,128)(2,1)S(1)} %get-tuple-element.60), channel_id=1, source_target_pairs={{0,9},{1,10},{2,11},{3,12},{4,13},{5,14},{6,15},{7,8},{8,17},{9,18... | collective-permute-start | bytes 147464 | tf_op jit(solution)/shard_map/ppermute | solution.py:535
  76.7 8.2 %collective-permute-start.10 = (bf16[6,32,512]{2,1,0:T(8,128)(2,1)S(1)}, bf16[6,32,512]{2,1,0:T(8,128)(2,1)S(1)}, u32[]{:S(2)}, u32[]{:S(2)}) collective-permute-start(bf16[6,32,512]{2,1,0:T(8,128)(2,1)S(1)} %get-tuple-element.64.edge_in), channel_id=1, source_target_pairs={{8,0},{16,8},{24,16},{0,24},{9,1},{17,9},{25,17},{1,25},{10,2},{18... | collective-permute-start | bytes 589832 | tf_op jit(solution)/shard_map/ppermute | solution.py:534
  79.4 3.5 %collective-permute-start.9 = (bf16[8,16,512]{2,1,0:T(8,128)(2,1)S(1)}, bf16[8,16,512]{2,1,0:T(8,128)(2,1)S(1)}, u32[]{:S(2)}, u32[]{:S(2)}) collective-permute-start(bf16[8,16,512]{2,1,0:T(8,128)(2,1)S(1)} %get-tuple-element.63), channel_id=1, source_target_pairs={{1,0},{2,1},{3,2},{4,3},{5,4},{6,5},{7,6},{0,7},{9,8},{10,9},{11,1... | collective-permute-start | bytes 393224 | tf_op jit(solution)/shard_map/ppermute | solution.py:533
  80.4 4.5 %collective-permute-start.11 = (bf16[6,8,512]{2,1,0:T(8,128)(2,1)S(1)}, bf16[6,8,512]{2,1,0:T(8,128)(2,1)S(1)}, u32[]{:S(2)}, u32[]{:S(2)}) collective-permute-start(bf16[6,8,512]{2,1,0:T(8,128)(2,1)S(1)} %get-tuple-element.65), channel_id=1, source_target_pairs={{9,0},{10,1},{11,2},{12,3},{13,4},{14,5},{15,6},{8,7},{17,8},{18,9... | collective-permute-start | bytes 147464 | tf_op jit(solution)/shard_map/ppermute | solution.py:535

commit v6 on v5

--- a/solution.py
+++ b/solution.py
@@ -109,7 +109,6 @@
 
 def assim_kernel(
     cap,
-    step,
     got_hbm,
     proj_ref,
     back_ref,
@@ -140,7 +139,8 @@
     per = LANES // cap
     halves = feats // LANES
     lane = lax.broadcasted_iota(jnp.int32, (META, LANES), 1)
-    cell = lax.broadcasted_iota(jnp.int32, (cells, LANES), 0)
+    every_row = lax.broadcasted_iota(jnp.int32, (rows, LANES), 0).astype(F32)
+    every_column = lax.broadcasted_iota(jnp.int32, (cols, LANES), 0).astype(F32)
     total = jnp.zeros((cells, feats), F32)
     for pair in range(0, devices // per, 2):
         if pair * per % piece == 0:
@@ -152,12 +152,23 @@
             for group in range(1, per):
                 other = got_ref[chunk * per + group, depth - META :, :].astype(F32)
                 meta = jnp.where(lane // cap == group, other, meta)
-            start = (meta[0:1] * cols + meta[1:2]).astype(jnp.int32)
-            away = cell - start
-            away = jnp.where(away < 0, away + cells, away)
-            amount = jnp.zeros((cells, LANES), F32)
+            row, column = meta[0:1], meta[1:2]
+            amount = jnp.zeros((rows, LANES), F32)
+            place = jnp.full((rows, LANES), -1.0, F32)
             for entry in range(4):
-                amount = jnp.where(away == entry * step, meta[2 + entry : 3 + entry], amount)
+                at = column + entry
+                over = at >= cols
+                below = row + entry + jnp.where(over, 1.0, 0.0)
+                hit = every_row == jnp.where(below >= rows, below - rows, below)
+                place = jnp.where(hit, jnp.where(over, at - cols, at), place)
+                amount = jnp.where(hit, meta[2 + entry : 3 + entry], amount)
+            amount = jnp.concatenate(
+                [
+                    jnp.where(every_column == place[y : y + 1], amount[y : y + 1], 0.0)
+                    for y in range(rows)
+                ],
+                axis=0,
+            )
             maps.append(amount.astype(BF16))
             block = got_ref[chunk * per : (chunk + 1) * per]
             blocks.append(
@@ -293,13 +304,13 @@
         put(wide_ref, place, main, left_in[y].astype(F32))
         put(wide_ref, place, main + TILE, right_in[y].astype(F32))
 
-    def stage(top, high):
+    def stage(high):
         @pl.loop(0, high + TAPS - 1)
         def _(y):
             for g in range(groups):
                 for r in range(TAPS + 1):
                     both = [
-                        wide_ref[g, top + y + h, pl.ds(start + r, TILE // 2, stride=2), :]
+                        wide_ref[g, y + h, pl.ds(start + r, TILE // 2, stride=2), :]
                         for h in (0, high)
                     ]
                     taps_in[g, r, y] = jnp.concatenate(both, axis=0).astype(BF16)
@@ -312,9 +323,21 @@
 
         @pl.loop(0, 2 * high, unroll=2)
         def _(y):
-            block_ref[top + y] = row_of(out_ref, y).astype(BF16)
-
-    stage(0, own // 2)
+            block_ref[y] = row_of(out_ref, y).astype(BF16)
+
+    if shrink:
+        stage(own // 2)
+    else:
+
+        @pl.when(at_last())
+        def _():
+            wide_ref[:, rows:] = jnp.zeros((groups, SPARE, width, LANES), F32)
+            stage((own + SPARE) // 2)
+
+        @pl.when(jnp.logical_not(at_last()))
+        def _():
+            stage(own // 2)
+
     if not lead:
         edge = TILE - SHIFT if shrink else 0
         above = 0 if shrink else SHIFT
@@ -327,13 +350,6 @@
                 for k in range(SHIFT):
                     columns = pl.ds(base + r, TILE, stride=2)
                     near_ref[g, r, k] = wide_ref[g, near + k, columns, :].astype(BF16)
-    if not shrink:
-
-        @pl.when(at_last())
-        def _():
-            wide_ref[:, rows:] = jnp.zeros((groups, SPARE, width, LANES), F32)
-            stage(own, SPARE // 2)
-
 
 def edge_kernel(
     shrink,
@@ -353,7 +369,18 @@
     *refs,
 ):
     if final:
-        state_ref, wide_ref, taps_in, tap_ref, spread_ref, out_ref, spare_ref, mix_lon = refs
+        state_ref, wide_ref, taps_in, tap_ref, spread_ref, out_ref, spare_ref, mix_lon = refs[:8]
+        rows_ref, sems = refs[8:]
+        kept, width = left_new.shape[:2]
+        copies = [
+            pltpu.make_async_copy(left_new, state_ref.at[0:kept, 0:width], sems.at[0]),
+            pltpu.make_async_copy(
+                right_new, state_ref.at[0:kept, width : 2 * width], sems.at[1]
+            ),
+            pltpu.make_async_copy(rows_ref, state_ref.at[kept : kept + SHIFT], sems.at[2]),
+        ]
+        copies[0].start()
+        copies[1].start()
     else:
         edge_ref, lon_ref, corner_ref = refs[:3]
         wide_ref, taps_in, tap_ref, spread_ref, out_ref, spare_ref, mix_lon = refs[3:]
@@ -396,9 +423,10 @@
     kept = left_new.shape[0]
     if final:
         for k in range(SHIFT):
-            state_ref[kept + k] = row_of(out_ref, k).astype(BF16)
-        state_ref[0:kept, 0:TILE, :] = left_new[...]
-        state_ref[0:kept, TILE:cols, :] = right_new[...]
+            rows_ref[k] = row_of(out_ref, k).astype(BF16)
+        copies[2].start()
+        for copy in copies:
+            copy.wait()
         return
 
     for k in range(SHIFT):
@@ -429,8 +457,8 @@
                 lon_ref[SHIFT + k, :, lanes_of(g)] = spare.astype(BF16)
 
 
-def call(kernel, out_shape, inputs, scratch=(), limit=VMEM_LIMIT, space=None, work=0):
-    whole = pl.BlockSpec(memory_space=pltpu.VMEM)
+def call(kernel, out_shape, inputs, scratch=(), limit=VMEM_LIMIT, space=None, work=0, out_space=pltpu.VMEM):
+    whole = pl.BlockSpec(memory_space=out_space)
     single = isinstance(out_shape, jax.ShapeDtypeStruct)
     spaces = space or (pltpu.VMEM,) * len(inputs)
     return pl.pallas_call(
@@ -470,10 +498,10 @@
     block = held(made, TILE, chans)
     scratch = (
         pltpu.VMEM((groups, rows + spare, cols + EDGE, LANES), F32),
-        pltpu.VMEM((groups, TAPS + 1, own // 2 + TAPS - 1, TILE, LANES), BF16),
+        pltpu.VMEM((groups, TAPS + 1, made // 2 + TAPS - 1, TILE, LANES), BF16),
         pltpu.VMEM((TAPS * TAPS, TILE, LANES), BF16),
-        pltpu.VMEM((2, own // 2, TILE, chans), BF16),
-        pltpu.VMEM((groups, own, TILE, LANES), F32),
+        pltpu.VMEM((2, made // 2, TILE, chans), BF16),
+        pltpu.VMEM((groups, made, TILE, LANES), F32),
     )
     lead = call(
         functools.partial(block_kernel, shrink, True, number),
@@ -494,8 +522,10 @@
         work=made * TILE * chans * WORK * 7 // 5,
     )
     new = (lead, trail) if shrink else (trail, lead)
+    last_scratch = ()
     if final:
         outs = held(made + SHIFT, cols, chans)
+        last_scratch = (pltpu.VMEM((SHIFT, cols, chans), BF16), pltpu.SemaphoreType.DMA((3,)))
     else:
         outs = (
             held(SHIFT, cols, chans),
@@ -510,7 +540,9 @@
         + (
             pltpu.VMEM((groups, 2 * TILE, LANES), F32),
             pltpu.VMEM((groups, SHIFT, rows, LANES), F32),
-        ),
+        )
+        + last_scratch,
+        out_space=pltpu.HBM if final else pltpu.VMEM,
         work=SHIFT * cols * chans * WORK,
     )
     if final:
@@ -572,7 +604,7 @@
     )
     got, mix, proj, back = lax.optimization_barrier((got, mix, proj, back))
     edge, left, right, lon_out, corner_out = call(
-        functools.partial(assim_kernel, cap, cols + 1),
+        functools.partial(assim_kernel, cap),
         (
             held(SHIFT, cols, chans),
             held(rows - SHIFT, TILE, chans),

time: 88 us -> 86.4 us (0.982)
  no operation moved by 1% of the time
where the time goes in v6:
time: 86.4 us; the launch traced here: 86.2 us
  waiting for transfers between devices  32.9 us (38%)
  Pallas kernels  31.9 us (37%)
  starting transfers between devices  18.9 us (22%)
  other arithmetic  2.11 us (2%)
    pallas_call x15, Pallas kernels, call(): pl.pallas_call(kernel, out_shape=out_shape, in_specs=[pl.BlockSpec(memory...  31.9 us
    all_to_all x1, waiting for transfers between devices, body(): lax.all_to_all(send, ('lat', 'lon'), split_axis=0, concat_axis=0, tiled=T...  26.7 us
    all_to_all x1, starting transfers between devices, body(): lax.all_to_all(send, ('lat', 'lon'), split_axis=0, concat_axis=0, tiled=T...  7.42 us
    ppermute x4, starting transfers between devices, exchange(): lat = lax.ppermute(lat, 'lat', along)  6.53 us
    ppermute x4, waiting for transfers between devices, exchange(): lon = lax.ppermute(lon, 'lon', around)  5.33 us
    ppermute x4, starting transfers between devices, exchange(): corner = lax.ppermute(corner, ('lat', 'lon'), across)  3.37 us
    convert_element_type x1, other arithmetic, body(): mix = (gains[:, :, None] * point_w.astype(F32)).astype(BF16)  2.11 us
  transfers between devices with their start and end apart: 13, of which 6 were waited for; matrix products, arithmetic and copies ran while one was open for 2% of the time, Pallas kernels for 18%

profile of v6, /device:TPU:0, one launch (start us, length us, event | category | flops | bytes accessed | tf_op | source)
XLA Modules:
  0.0 86.2 jit_solution(5538347620713642076)
XLA Ops:
  0.0 4.8 %shard_map.91 = bf16[32,136,128]{2,1,0:T(8,128)(2,1)} custom-call(s32[1,1024]{1,0:T(1,128)} %bitcast.20, s32[4,1024]{1,0:T(4,128)} %bitcast.18, bf16[4,1024]{1,0:T(4,128)(2,1)} %bitcast.19, bf16[1024,256]{1,0:T(8,128)(2,1)} %obs_hbm.1), custom_call_target="tpu_custom_call" | custom-call | tf_op jit(solution)/shard_map/pallas_call | solution.py:464
  4.8 7.4 %all-to-all-start = ((bf16[32,136,128]{2,1,0:T(8,128)(2,1)}), bf16[32,136,128]{2,1,0:T(8,128)(2,1)}, u32[]{:S(2)}, u32[]{:S(2)}) async-start(bf16[32,136,128]{2,1,0:T(8,128)(2,1)} %shard_map.91), calls=%async_computation | async-start | bytes 2228224 | tf_op jit(solution)/shard_map/all_to_all | solution.py:594
  12.3 2.1 %multiply_convert_fusion.refs_2_.refs_1_.mix_ref = bf16[4,512,512]{2,1,0:T(8,128)(2,1)S(1)} fusion(bf16[4,512,512]{2,1,0:T(8,128)(2,1)} %param.16, f32[4,512]{1,0:T(4,128)S(1)} %copy-done.3), kind=kLoop, calls=%fused_computation | loop fusion | flops 3145728 | bytes 4202496 | tf_op jit(solution)/shard_map/convert_element_type | solution.py:597
  14.5 26.7 %all-to-all-done.got_hbm = bf16[32,136,128]{2,1,0:T(8,128)(2,1)} async-done(((bf16[32,136,128]{2,1,0:T(8,128)(2,1)}), bf16[32,136,128]{2,1,0:T(8,128)(2,1)}, u32[]{:S(2)}, u32[]{:S(2)}) %all-to-all-start) | async-done | bytes 1114144 | tf_op jit(solution)/shard_map/all_to_all | solution.py:594
  41.2 2.6 %shard_map.93 = (bf16[6,32,512]{2,1,0:T(8,128)(2,1)S(1)}, bf16[10,16,512]{2,1,0:T(8,128)(2,1)S(1)}, bf16[10,16,512]{2,1,0:T(8,128)(2,1)S(1)}, bf16[6,16,512]{2,1,0:T(8,128)(2,1)S(1)}, bf16[6,8,512]{2,1,0:T(8,128)(2,1)S(1)}) custom-call(bf16[32,136,128]{2,1,0:T(8,128)(2,1)} %all-to-all-done.got_hbm, bf16[256,512]{1,0:T(8,128)(2,1)S(1)} %get-tuple-element.40.proj_ref, ...), custom_call_target="tpu_custom_call" | custom-call | tf_op jit(solution)/shard_map/pallas_call | solution.py:464
  44.4 1.1 %collective-permute-start.2 = (bf16[6,8,512]{2,1,0:T(8,128)(2,1)S(1)}, bf16[6,8,512]{2,1,0:T(8,128)(2,1)S(1)}, u32[]{:S(2)}, u32[]{:S(2)}) collective-permute-start(bf16[6,8,512]{2,1,0:T(8,128)(2,1)S(1)} %get-tuple-element.48), channel_id=1, source_target_pairs={{0,9},{1,10},{2,11},{3,12},{4,13},{5,14},{6,15},{7,8},{8,17},{9,18... | collective-permute-start | bytes 147464 | tf_op jit(solution)/shard_map/ppermute | solution.py:567
  45.5 1.8 %shard_map.95.right_new.right_in = bf16[14,16,512]{2,1,0:T(8,128)(2,1)S(1)} custom-call(bf16[6,32,512]{2,1,0:T(8,128)(2,1)S(1)} %get-tuple-element.42.edge_in, bf16[10,16,512]{2,1,0:T(8,128)(2,1)S(1)} %get-tuple-element.43.left_in, bf16[10,16,512]{2,1,0:T(8,128)(2,1)S(1)} %get-tuple-element.44.right_in, f32[49,4,512]{2,1,0:T(4,128)S(1)} %bitcast.6, ...), custom_call_target="tpu_custom_call" | custom-call | flops 573440000 | tf_op jit(solution)/shard_map/pallas_call | solution.py:464
  47.4 2.4 %collective-permute-done.refs_0_.lon_in = bf16[6,16,512]{2,1,0:T(8,128)(2,1)S(1)} collective-permute-done((bf16[6,16,512]{2,1,0:T(8,128)(2,1)S(1)}, bf16[6,16,512]{2,1,0:T(8,128)(2,1)S(1)}, u32[]{:S(2)}, u32[]{:S(2)}) %collective-permute-start) | collective-permute-done | bytes 98336 | tf_op jit(solution)/shard_map/ppermute | solution.py:565
  49.8 2.0 %shard_map.94 = (bf16[14,16,512]{2,1,0:T(8,128)(2,1)S(1)}, f32[4,6,16,128]{3,2,1,0:T(8,128)S(1)}, bf16[4,8,6,16,128]{4,3,2,1,0:T(8,128)(2,1)S(1)}) custom-call(bf16[6,32,512]{2,1,0:T(8,128)(2,1)S(1)} %get-tuple-element.42.edge_in, bf16[10,16,512]{2,1,0:T(8,128)(2,1)S(1)} %get-tuple-element.43.left_in, bf16[10,16,512]{2,1,0:T(8,128)(2,1)S(1)} %get-tuple-element.44.right_in, ...), custom_call_target="tpu_custom_call" | custom-call | flops 802816000 | tf_op jit(solution)/shard_map/pallas_call | solution.py:464
  52.6 2.1 %shard_map.96 = (bf16[6,32,512]{2,1,0:T(8,128)(2,1)S(1)}, bf16[8,16,512]{2,1,0:T(8,128)(2,1)S(1)}, bf16[6,8,512]{2,1,0:T(8,128)(2,1)S(1)}) custom-call(bf16[10,16,512]{2,1,0:T(8,128)(2,1)S(1)} %get-tuple-element.43.left_in, bf16[10,16,512]{2,1,0:T(8,128)(2,1)S(1)} %get-tuple-element.44.right_in, bf16[6,16,512]{2,1,0:T(8,128)(2,1)S(1)} %collective-permute-done.refs_0_.lon_in, ...), custom_call_target="tpu_custom_call" | custom-call | flops 491520000 | tf_op jit(solution)/shard_map/pallas_call | solution.py:464
  54.7 2.8 %collective-permute-start.4 = (bf16[6,32,512]{2,1,0:T(8,128)(2,1)S(1)}, bf16[6,32,512]{2,1,0:T(8,128)(2,1)S(1)}, u32[]{:S(2)}, u32[]{:S(2)}) collective-permute-start(bf16[6,32,512]{2,1,0:T(8,128)(2,1)S(1)} %get-tuple-element.52.edge_in), channel_id=1, source_target_pairs={{8,0},{16,8},{24,16},{0,24},{9,1},{17,9},{25,17},{1,25},{10,2},{18... | collective-permute-start | bytes 589832 | tf_op jit(solution)/shard_map/ppermute | solution.py:566
  57.9 1.8 %shard_map.98.left_new.left_in = bf16[10,16,512]{2,1,0:T(8,128)(2,1)S(1)} custom-call(bf16[6,32,512]{2,1,0:T(8,128)(2,1)S(1)} %get-tuple-element.52.edge_in, bf16[14,16,512]{2,1,0:T(8,128)(2,1)S(1)} %get-tuple-element.47.left_new.left_in, bf16[14,16,512]{2,1,0:T(8,128)(2,1)S(1)} %shard_map.95.right_new.right_in, f32[49,4,512]{2,1,0:T(4,128)S(1)} %bitcast.9, ...), custom_call_target="tpu_custom_call" | custom-call | flops 409600000 | tf_op jit(solution)/shard_map/pallas_call | solution.py:464
  60.0 2.0 %shard_map.97 = (bf16[10,16,512]{2,1,0:T(8,128)(2,1)S(1)}, f32[4,6,16,128]{3,2,1,0:T(8,128)S(1)}, bf16[4,8,6,16,128]{4,3,2,1,0:T(8,128)(2,1)S(1)}) custom-call(bf16[6,32,512]{2,1,0:T(8,128)(2,1)S(1)} %get-tuple-element.52.edge_in, bf16[14,16,512]{2,1,0:T(8,128)(2,1)S(1)} %get-tuple-element.47.left_new.left_in, ...), custom_call_target="tpu_custom_call" | custom-call | flops 573440000 | tf_op jit(solution)/shard_map/pallas_call | solution.py:464
  62.0 2.1 %shard_map.99 = (bf16[6,32,512]{2,1,0:T(8,128)(2,1)S(1)}, bf16[6,16,512]{2,1,0:T(8,128)(2,1)S(1)}, bf16[6,8,512]{2,1,0:T(8,128)(2,1)S(1)}) custom-call(bf16[14,16,512]{2,1,0:T(8,128)(2,1)S(1)} %get-tuple-element.47.left_new.left_in, bf16[14,16,512]{2,1,0:T(8,128)(2,1)S(1)} %shard_map.95.right_new.right_in, ...), custom_call_target="tpu_custom_call" | custom-call | flops 491520000 | tf_op jit(solution)/shard_map/pallas_call | solution.py:464
  64.1 1.6 %collective-permute-start.7 = (bf16[6,32,512]{2,1,0:T(8,128)(2,1)S(1)}, bf16[6,32,512]{2,1,0:T(8,128)(2,1)S(1)}, u32[]{:S(2)}, u32[]{:S(2)}) collective-permute-start(bf16[6,32,512]{2,1,0:T(8,128)(2,1)S(1)} %get-tuple-element.57.edge_in), channel_id=1, source_target_pairs={{0,8},{8,16},{16,24},{24,0},{1,9},{9,17},{17,25},{25,1},{2,10},{10... | collective-permute-start | bytes 589832 | tf_op jit(solution)/shard_map/ppermute | solution.py:566
  65.6 1.3 %collective-permute-start.8 = (bf16[6,8,512]{2,1,0:T(8,128)(2,1)S(1)}, bf16[6,8,512]{2,1,0:T(8,128)(2,1)S(1)}, u32[]{:S(2)}, u32[]{:S(2)}) collective-permute-start(bf16[6,8,512]{2,1,0:T(8,128)(2,1)S(1)} %get-tuple-element.60), channel_id=1, source_target_pairs={{0,9},{1,10},{2,11},{3,12},{4,13},{5,14},{6,15},{7,8},{8,17},{9,18... | collective-permute-start | bytes 147464 | tf_op jit(solution)/shard_map/ppermute | solution.py:567
  67.0 2.0 %shard_map.101.right_new.right_in = bf16[14,16,512]{2,1,0:T(8,128)(2,1)S(1)} custom-call(bf16[6,32,512]{2,1,0:T(8,128)(2,1)S(1)} %get-tuple-element.57.edge_in, bf16[10,16,512]{2,1,0:T(8,128)(2,1)S(1)} %shard_map.98.left_new.left_in, bf16[10,16,512]{2,1,0:T(8,128)(2,1)S(1)} %get-tuple-element.55.right_new.right_in, f32[49,4,512]{2,1,0:T(4,128)S(1)} %bitcast.12, ...), custom_call_target="tpu_custom_call" | custom-call | flops 573440000 | tf_op jit(solution)/shard_map/pallas_call | solution.py:464
  69.0 2.5 %collective-permute-done.6.refs_0_.lon_in = bf16[6,16,512]{2,1,0:T(8,128)(2,1)S(1)} collective-permute-done((bf16[6,16,512]{2,1,0:T(8,128)(2,1)S(1)}, bf16[6,16,512]{2,1,0:T(8,128)(2,1)S(1)}, u32[]{:S(2)}, u32[]{:S(2)}) %collective-permute-start.6) | collective-permute-done | bytes 98336 | tf_op jit(solution)/shard_map/ppermute | solution.py:565
  71.5 2.0 %shard_map.100 = (bf16[14,16,512]{2,1,0:T(8,128)(2,1)S(1)}, f32[4,6,16,128]{3,2,1,0:T(8,128)S(1)}, bf16[4,8,6,16,128]{4,3,2,1,0:T(8,128)(2,1)S(1)}) custom-call(bf16[6,32,512]{2,1,0:T(8,128)(2,1)S(1)} %get-tuple-element.57.edge_in, bf16[10,16,512]{2,1,0:T(8,128)(2,1)S(1)} %shard_map.98.left_new.left_in, ...), custom_call_target="tpu_custom_call" | custom-call | flops 802816000 | tf_op jit(solution)/shard_map/pallas_call | solution.py:464
  73.5 2.1 %shard_map.102 = (bf16[6,32,512]{2,1,0:T(8,128)(2,1)S(1)}, bf16[8,16,512]{2,1,0:T(8,128)(2,1)S(1)}, bf16[6,8,512]{2,1,0:T(8,128)(2,1)S(1)}) custom-call(bf16[10,16,512]{2,1,0:T(8,128)(2,1)S(1)} %shard_map.98.left_new.left_in, bf16[10,16,512]{2,1,0:T(8,128)(2,1)S(1)} %get-tuple-element.55.right_new.right_in, ...), custom_call_target="tpu_custom_call" | custom-call | flops 491520000 | tf_op jit(solution)/shard_map/pallas_call | solution.py:464
  75.6 2.1 %collective-permute-start.10 = (bf16[6,32,512]{2,1,0:T(8,128)(2,1)S(1)}, bf16[6,32,512]{2,1,0:T(8,128)(2,1)S(1)}, u32[]{:S(2)}, u32[]{:S(2)}) collective-permute-start(bf16[6,32,512]{2,1,0:T(8,128)(2,1)S(1)} %get-tuple-element.64.edge_in), channel_id=1, source_target_pairs={{8,0},{16,8},{24,16},{0,24},{9,1},{17,9},{25,17},{1,25},{10,2},{18... | collective-permute-start | bytes 589832 | tf_op jit(solution)/shard_map/ppermute | solution.py:566
  79.2 1.8 %shard_map.104.left_new = bf16[10,16,512]{2,1,0:T(8,128)(2,1)S(1)} custom-call(bf16[6,32,512]{2,1,0:T(8,128)(2,1)S(1)} %get-tuple-element.64.edge_in, bf16[14,16,512]{2,1,0:T(8,128)(2,1)S(1)} %get-tuple-element.59.left_new.left_in, bf16[14,16,512]{2,1,0:T(8,128)(2,1)S(1)} %shard_map.101.right_new.right_in, f32[49,4,512]{2,1,0:T(4,128)S(1)} %bitcast.15, ...), custom_call_target="tpu_custom_call" | custom-call | flops 409600000 | tf_op jit(solution)/shard_map/pallas_call | solution.py:464
  81.3 2.0 %shard_map.103 = (bf16[10,16,512]{2,1,0:T(8,128)(2,1)S(1)}, f32[4,6,16,128]{3,2,1,0:T(8,128)S(1)}, bf16[4,8,6,16,128]{4,3,2,1,0:T(8,128)(2,1)S(1)}) custom-call(bf16[6,32,512]{2,1,0:T(8,128)(2,1)S(1)} %get-tuple-element.64.edge_in, bf16[14,16,512]{2,1,0:T(8,128)(2,1)S(1)} %get-tuple-element.59.left_new.left_in, ...), custom_call_target="tpu_custom_call" | custom-call | flops 573440000 | tf_op jit(solution)/shard_map/pallas_call | solution.py:464
  83.3 2.7 %shard_map.105 = bf16[16,32,512]{2,1,0:T(8,128)(2,1)} custom-call(bf16[14,16,512]{2,1,0:T(8,128)(2,1)S(1)} %get-tuple-element.59.left_new.left_in, bf16[14,16,512]{2,1,0:T(8,128)(2,1)S(1)} %shard_map.101.right_new.right_in, bf16[8,16,512]{2,1,0:T(8,128)(2,1)S(1)} %collective-permute-done.9.refs_0_.lon_in, ...), custom_call_target="tpu_custom_call" | custom-call | flops 491520000 | tf_op jit(solution)/shard_map/pallas_call | solution.py:464
  (26 shorter events, 4.0 us)
Async XLA Ops:
  0.0 12.2 %copy-start.2 = (bf16[256,512]{1,0:T(8,128)(2,1)S(1)}, bf16[256,512]{1,0:T(8,128)(2,1)}, u32[]{:S(2)}) copy-start(bf16[256,512]{1,0:T(8,128)(2,1)} %proj_hbm.1) | copy-start | bytes 786436
  0.0 12.2 %copy-start.1 = (bf16[16,32,512]{2,1,0:T(8,128)(2,1)S(1)}, bf16[16,32,512]{2,1,0:T(8,128)(2,1)}, u32[]{:S(2)}) copy-start(bf16[16,32,512]{2,1,0:T(8,128)(2,1)} %back_hbm.1) | copy-start | bytes 1572868
  0.0 12.3 %copy-start.3 = (f32[4,512]{1,0:T(4,128)S(1)}, f32[4,512]{1,0:T(4,128)}, u32[]{:S(2)}) copy-start(f32[4,512]{1,0:T(4,128)} %param.17) | copy-start | bytes 24580
  4.8 36.4 %all-to-all-start = ((bf16[32,136,128]{2,1,0:T(8,128)(2,1)}), bf16[32,136,128]{2,1,0:T(8,128)(2,1)}, u32[]{:S(2)}, u32[]{:S(2)}) async-start(bf16[32,136,128]{2,1,0:T(8,128)(2,1)} %shard_map.91), calls=%async_computation | async-start | bytes 2228224 | tf_op jit(solution)/shard_map/all_to_all | solution.py:594
  12.3 33.2 %copy-start = (f32[4,7,7,512]{3,0,2,1:T(4,128)S(1)}, f32[4,7,7,512]{3,0,2,1:T(4,128)}, u32[]{:S(2)}) copy-start(f32[4,7,7,512]{3,0,2,1:T(4,128)} %param.15) | copy-start | bytes 1204228
  43.8 8.8 %collective-permute-start.1 = (bf16[6,32,512]{2,1,0:T(8,128)(2,1)S(1)}, bf16[6,32,512]{2,1,0:T(8,128)(2,1)S(1)}, u32[]{:S(2)}, u32[]{:S(2)}) collective-permute-start(bf16[6,32,512]{2,1,0:T(8,128)(2,1)S(1)} %get-tuple-element.42.edge_in), channel_id=1, source_target_pairs={{0,8},{8,16},{16,24},{24,0},{1,9},{9,17},{17,25},{25,1},{2,10},{10... | collective-permute-start | bytes 589832 | tf_op jit(solution)/shard_map/ppermute | solution.py:566
  43.9 5.9 %collective-permute-start = (bf16[6,16,512]{2,1,0:T(8,128)(2,1)S(1)}, bf16[6,16,512]{2,1,0:T(8,128)(2,1)S(1)}, u32[]{:S(2)}, u32[]{:S(2)}) collective-permute-start(bf16[6,16,512]{2,1,0:T(8,128)(2,1)S(1)} %get-tuple-element.45), channel_id=1, source_target_pairs={{0,1},{1,2},{2,3},{3,4},{4,5},{5,6},{6,7},{7,0},{8,9},{9,10},{10,1... | collective-permute-start | bytes 294920 | tf_op jit(solution)/shard_map/ppermute | solution.py:565
  44.4 8.1 %collective-permute-start.2 = (bf16[6,8,512]{2,1,0:T(8,128)(2,1)S(1)}, bf16[6,8,512]{2,1,0:T(8,128)(2,1)S(1)}, u32[]{:S(2)}, u32[]{:S(2)}) collective-permute-start(bf16[6,8,512]{2,1,0:T(8,128)(2,1)S(1)} %get-tuple-element.48), channel_id=1, source_target_pairs={{0,9},{1,10},{2,11},{3,12},{4,13},{5,14},{6,15},{7,8},{8,17},{9,18... | collective-permute-start | bytes 147464 | tf_op jit(solution)/shard_map/ppermute | solution.py:567
  54.7 7.3 %collective-permute-start.4 = (bf16[6,32,512]{2,1,0:T(8,128)(2,1)S(1)}, bf16[6,32,512]{2,1,0:T(8,128)(2,1)S(1)}, u32[]{:S(2)}, u32[]{:S(2)}) collective-permute-start(bf16[6,32,512]{2,1,0:T(8,128)(2,1)S(1)} %get-tuple-element.52.edge_in), channel_id=1, source_target_pairs={{8,0},{16,8},{24,16},{0,24},{9,1},{17,9},{25,17},{1,25},{10,2},{18... | collective-permute-start | bytes 589832 | tf_op jit(solution)/shard_map/ppermute | solution.py:566
  57.4 2.5 %collective-permute-start.3 = (bf16[8,16,512]{2,1,0:T(8,128)(2,1)S(1)}, bf16[8,16,512]{2,1,0:T(8,128)(2,1)S(1)}, u32[]{:S(2)}, u32[]{:S(2)}) collective-permute-start(bf16[8,16,512]{2,1,0:T(8,128)(2,1)S(1)} %get-tuple-element.51), channel_id=1, source_target_pairs={{1,0},{2,1},{3,2},{4,3},{5,4},{6,5},{7,6},{0,7},{9,8},{10,9},{11,1... | collective-permute-start | bytes 393224 | tf_op jit(solution)/shard_map/ppermute | solution.py:565
  57.4 4.5 %collective-permute-start.5 = (bf16[6,8,512]{2,1,0:T(8,128)(2,1)S(1)}, bf16[6,8,512]{2,1,0:T(8,128)(2,1)S(1)}, u32[]{:S(2)}, u32[]{:S(2)}) collective-permute-start(bf16[6,8,512]{2,1,0:T(8,128)(2,1)S(1)} %get-tuple-element.53), channel_id=1, source_target_pairs={{9,0},{10,1},{11,2},{12,3},{13,4},{14,5},{15,6},{8,7},{17,8},{18,9... | collective-permute-start | bytes 147464 | tf_op jit(solution)/shard_map/ppermute | solution.py:567
  64.1 9.4 %collective-permute-start.7 = (bf16[6,32,512]{2,1,0:T(8,128)(2,1)S(1)}, bf16[6,32,512]{2,1,0:T(8,128)(2,1)S(1)}, u32[]{:S(2)}, u32[]{:S(2)}) collective-permute-start(bf16[6,32,512]{2,1,0:T(8,128)(2,1)S(1)} %get-tuple-element.57.edge_in), channel_id=1, source_target_pairs={{0,8},{8,16},{16,24},{24,0},{1,9},{9,17},{17,25},{25,1},{2,10},{10... | collective-permute-start | bytes 589832 | tf_op jit(solution)/shard_map/ppermute | solution.py:566
  65.6 5.8 %collective-permute-start.6 = (bf16[6,16,512]{2,1,0:T(8,128)(2,1)S(1)}, bf16[6,16,512]{2,1,0:T(8,128)(2,1)S(1)}, u32[]{:S(2)}, u32[]{:S(2)}) collective-permute-start(bf16[6,16,512]{2,1,0:T(8,128)(2,1)S(1)} %get-tuple-element.58), channel_id=1, source_target_pairs={{0,1},{1,2},{2,3},{3,4},{4,5},{5,6},{6,7},{7,0},{8,9},{9,10},{10,1... | collective-permute-start | bytes 294920 | tf_op jit(solution)/shard_map/ppermute | solution.py:565
  65.6 7.8 %collective-permute-start.8 = (bf16[6,8,512]{2,1,0:T(8,128)(2,1)S(1)}, bf16[6,8,512]{2,1,0:T(8,128)(2,1)S(1)}, u32[]{:S(2)}, u32[]{:S(2)}) collective-permute-start(bf16[6,8,512]{2,1,0:T(8,128)(2,1)S(1)} %get-tuple-element.60), channel_id=1, source_target_pairs={{0,9},{1,10},{2,11},{3,12},{4,13},{5,14},{6,15},{7,8},{8,17},{9,18... | collective-permute-start | bytes 147464 | tf_op jit(solution)/shard_map/ppermute | solution.py:567
  75.6 7.7 %collective-permute-start.10 = (bf16[6,32,512]{2,1,0:T(8,128)(2,1)S(1)}, bf16[6,32,512]{2,1,0:T(8,128)(2,1)S(1)}, u32[]{:S(2)}, u32[]{:S(2)}) collective-permute-start(bf16[6,32,512]{2,1,0:T(8,128)(2,1)S(1)} %get-tuple-element.64.edge_in), channel_id=1, source_target_pairs={{8,0},{16,8},{24,16},{0,24},{9,1},{17,9},{25,17},{1,25},{10,2},{18... | collective-permute-start | bytes 589832 | tf_op jit(solution)/shard_map/ppermute | solution.py:566
  77.7 3.5 %collective-permute-start.9 = (bf16[8,16,512]{2,1,0:T(8,128)(2,1)S(1)}, bf16[8,16,512]{2,1,0:T(8,128)(2,1)S(1)}, u32[]{:S(2)}, u32[]{:S(2)}) collective-permute-start(bf16[8,16,512]{2,1,0:T(8,128)(2,1)S(1)} %get-tuple-element.63), channel_id=1, source_target_pairs={{1,0},{2,1},{3,2},{4,3},{5,4},{6,5},{7,6},{0,7},{9,8},{10,9},{11,1... | collective-permute-start | bytes 393224 | tf_op jit(solution)/shard_map/ppermute | solution.py:565
  78.7 4.5 %collective-permute-start.11 = (bf16[6,8,512]{2,1,0:T(8,128)(2,1)S(1)}, bf16[6,8,512]{2,1,0:T(8,128)(2,1)S(1)}, u32[]{:S(2)}, u32[]{:S(2)}) collective-permute-start(bf16[6,8,512]{2,1,0:T(8,128)(2,1)S(1)} %get-tuple-element.65), channel_id=1, source_target_pairs={{9,0},{10,1},{11,2},{12,3},{13,4},{14,5},{15,6},{8,7},{17,8},{18,9... | collective-permute-start | bytes 147464 | tf_op jit(solution)/shard_map/ppermute | solution.py:567

commit v7 on v6

--- a/solution.py
+++ b/solution.py
@@ -16,7 +16,7 @@
 TILE = 16
 PIECES = 4
 SPARE = 4
-WORK = 5000
+WORK = 1000
 VMEM_LIMIT = 24 * 1024 * 1024
 PACK_LIMIT = 58 * 1024 * 1024
 BF16 = jnp.bfloat16
@@ -508,7 +508,7 @@
         block,
         (edge, left, right, taps, mix),
         scratch,
-        work=made * TILE * chans * WORK,
+        work=made * TILE * chans * WORK * (5 if shrink else 3),
     )
     trail, lon_new, near = call(
         functools.partial(block_kernel, shrink, False, number),
@@ -519,7 +519,7 @@
         ),
         (edge, left, right, lon_in, taps, mix),
         scratch,
-        work=made * TILE * chans * WORK * 7 // 5,
+        work=made * TILE * chans * WORK * (7 if shrink else 11),
     )
     new = (lead, trail) if shrink else (trail, lead)
     last_scratch = ()
@@ -543,7 +543,7 @@
         )
         + last_scratch,
         out_space=pltpu.HBM if final else pltpu.VMEM,
-        work=SHIFT * cols * chans * WORK,
+        work=SHIFT * cols * chans * WORK * 5,
     )
     if final:
         return outs

time: 86.4 us -> 87 us (level)
    ppermute x4, starting transfers between devices: 1.58 us -> 5.29 us  [exchange(): lon = lax.ppermute(lon, 'lon', around)]
    ppermute x4, starting transfers between devices: 6.53 us -> 4.54 us  [exchange(): lat = lax.ppermute(lat, 'lat', along)]
    ppermute x4, starting transfers between devices: 3.37 us -> 2.18 us  [exchange(): corner = lax.ppermute(corner, ('lat', 'lon'), across)]
where the time goes in v7:
time: 87 us; the launch traced here: 86.5 us
  waiting for transfers between devices  32.7 us (38%)
  Pallas kernels  31.9 us (37%)
  starting transfers between devices  19.4 us (22%)
  other arithmetic  2.11 us (2%)
    pallas_call x15, Pallas kernels, call(): pl.pallas_call(kernel, out_shape=out_shape, in_specs=[pl.BlockSpec(memory...  31.9 us
    all_to_all x1, waiting for transfers between devices, body(): lax.all_to_all(send, ('lat', 'lon'), split_axis=0, concat_axis=0, tiled=T...  26.7 us
    all_to_all x1, starting transfers between devices, body(): lax.all_to_all(send, ('lat', 'lon'), split_axis=0, concat_axis=0, tiled=T...  7.42 us
    ppermute x4, starting transfers between devices, exchange(): lon = lax.ppermute(lon, 'lon', around)  5.29 us
    ppermute x4, waiting for transfers between devices, exchange(): lon = lax.ppermute(lon, 'lon', around)  4.97 us
    ppermute x4, starting transfers between devices, exchange(): lat = lax.ppermute(lat, 'lat', along)  4.54 us
    ppermute x4, starting transfers between devices, exchange(): corner = lax.ppermute(corner, ('lat', 'lon'), across)  2.18 us
    convert_element_type x1, other arithmetic, body(): mix = (gains[:, :, None] * point_w.astype(F32)).astype(BF16)  2.11 us
  transfers between devices with their start and end apart: 13, of which 6 were waited for; matrix products, arithmetic and copies ran while one was open for 2% of the time, Pallas kernels for 18%

profile of v7, /device:TPU:0, one launch (start us, length us, event | category | flops | bytes accessed | tf_op | source)
XLA Modules:
  0.0 86.5 jit_solution(6093023075539712611)
XLA Ops:
  0.0 4.8 %shard_map.91 = bf16[32,136,128]{2,1,0:T(8,128)(2,1)} custom-call(s32[1,1024]{1,0:T(1,128)} %bitcast.20, s32[4,1024]{1,0:T(4,128)} %bitcast.18, bf16[4,1024]{1,0:T(4,128)(2,1)} %bitcast.19, bf16[1024,256]{1,0:T(8,128)(2,1)} %obs_hbm.1), custom_call_target="tpu_custom_call" | custom-call | tf_op jit(solution)/shard_map/pallas_call | solution.py:464
  4.8 7.4 %all-to-all-start = ((bf16[32,136,128]{2,1,0:T(8,128)(2,1)}), bf16[32,136,128]{2,1,0:T(8,128)(2,1)}, u32[]{:S(2)}, u32[]{:S(2)}) async-start(bf16[32,136,128]{2,1,0:T(8,128)(2,1)} %shard_map.91), calls=%async_computation | async-start | bytes 2228224 | tf_op jit(solution)/shard_map/all_to_all | solution.py:594
  12.3 2.1 %multiply_convert_fusion.refs_2_.refs_1_.mix_ref = bf16[4,512,512]{2,1,0:T(8,128)(2,1)S(1)} fusion(bf16[4,512,512]{2,1,0:T(8,128)(2,1)} %param.16, f32[4,512]{1,0:T(4,128)S(1)} %copy-done.3), kind=kLoop, calls=%fused_computation | loop fusion | flops 3145728 | bytes 4202496 | tf_op jit(solution)/shard_map/convert_element_type | solution.py:597
  14.5 26.7 %all-to-all-done.got_hbm = bf16[32,136,128]{2,1,0:T(8,128)(2,1)} async-done(((bf16[32,136,128]{2,1,0:T(8,128)(2,1)}), bf16[32,136,128]{2,1,0:T(8,128)(2,1)}, u32[]{:S(2)}, u32[]{:S(2)}) %all-to-all-start) | async-done | bytes 1114144 | tf_op jit(solution)/shard_map/all_to_all | solution.py:594
  41.2 2.6 %shard_map.93 = (bf16[6,32,512]{2,1,0:T(8,128)(2,1)S(1)}, bf16[10,16,512]{2,1,0:T(8,128)(2,1)S(1)}, bf16[10,16,512]{2,1,0:T(8,128)(2,1)S(1)}, bf16[6,16,512]{2,1,0:T(8,128)(2,1)S(1)}, bf16[6,8,512]{2,1,0:T(8,128)(2,1)S(1)}) custom-call(bf16[32,136,128]{2,1,0:T(8,128)(2,1)} %all-to-all-done.got_hbm, bf16[256,512]{1,0:T(8,128)(2,1)S(1)} %get-tuple-element.40.proj_ref, ...), custom_call_target="tpu_custom_call" | custom-call | tf_op jit(solution)/shard_map/pallas_call | solution.py:464
  45.6 1.8 %shard_map.95.right_new.right_in = bf16[14,16,512]{2,1,0:T(8,128)(2,1)S(1)} custom-call(bf16[6,32,512]{2,1,0:T(8,128)(2,1)S(1)} %get-tuple-element.42.edge_in, bf16[10,16,512]{2,1,0:T(8,128)(2,1)S(1)} %get-tuple-element.43.left_in, bf16[10,16,512]{2,1,0:T(8,128)(2,1)S(1)} %get-tuple-element.44.right_in, f32[49,4,512]{2,1,0:T(4,128)S(1)} %bitcast.6, ...), custom_call_target="tpu_custom_call" | custom-call | flops 344064000 | tf_op jit(solution)/shard_map/pallas_call | solution.py:464
  47.4 2.3 %collective-permute-done.refs_0_.lon_in = bf16[6,16,512]{2,1,0:T(8,128)(2,1)S(1)} collective-permute-done((bf16[6,16,512]{2,1,0:T(8,128)(2,1)S(1)}, bf16[6,16,512]{2,1,0:T(8,128)(2,1)S(1)}, u32[]{:S(2)}, u32[]{:S(2)}) %collective-permute-start) | collective-permute-done | bytes 98336 | tf_op jit(solution)/shard_map/ppermute | solution.py:565
  49.7 2.0 %shard_map.94 = (bf16[14,16,512]{2,1,0:T(8,128)(2,1)S(1)}, f32[4,6,16,128]{3,2,1,0:T(8,128)S(1)}, bf16[4,8,6,16,128]{4,3,2,1,0:T(8,128)(2,1)S(1)}) custom-call(bf16[6,32,512]{2,1,0:T(8,128)(2,1)S(1)} %get-tuple-element.42.edge_in, bf16[10,16,512]{2,1,0:T(8,128)(2,1)S(1)} %get-tuple-element.43.left_in, bf16[10,16,512]{2,1,0:T(8,128)(2,1)S(1)} %get-tuple-element.44.right_in, ...), custom_call_target="tpu_custom_call" | custom-call | flops 1261568000 | tf_op jit(solution)/shard_map/pallas_call | solution.py:464
  51.9 2.1 %shard_map.96 = (bf16[6,32,512]{2,1,0:T(8,128)(2,1)S(1)}, bf16[8,16,512]{2,1,0:T(8,128)(2,1)S(1)}, bf16[6,8,512]{2,1,0:T(8,128)(2,1)S(1)}) custom-call(bf16[10,16,512]{2,1,0:T(8,128)(2,1)S(1)} %get-tuple-element.43.left_in, bf16[10,16,512]{2,1,0:T(8,128)(2,1)S(1)} %get-tuple-element.44.right_in, bf16[6,16,512]{2,1,0:T(8,128)(2,1)S(1)} %collective-permute-done.refs_0_.lon_in, ...), custom_call_target="tpu_custom_call" | custom-call | flops 491520000 | tf_op jit(solution)/shard_map/pallas_call | solution.py:464
  54.0 1.2 %collective-permute-start.4 = (bf16[6,32,512]{2,1,0:T(8,128)(2,1)S(1)}, bf16[6,32,512]{2,1,0:T(8,128)(2,1)S(1)}, u32[]{:S(2)}, u32[]{:S(2)}) collective-permute-start(bf16[6,32,512]{2,1,0:T(8,128)(2,1)S(1)} %get-tuple-element.52.edge_in), channel_id=1, source_target_pairs={{8,0},{16,8},{24,16},{0,24},{9,1},{17,9},{25,17},{1,25},{10,2},{18... | collective-permute-start | bytes 589832 | tf_op jit(solution)/shard_map/ppermute | solution.py:566
  55.2 2.4 %collective-permute-start.3 = (bf16[8,16,512]{2,1,0:T(8,128)(2,1)S(1)}, bf16[8,16,512]{2,1,0:T(8,128)(2,1)S(1)}, u32[]{:S(2)}, u32[]{:S(2)}) collective-permute-start(bf16[8,16,512]{2,1,0:T(8,128)(2,1)S(1)} %get-tuple-element.51), channel_id=1, source_target_pairs={{1,0},{2,1},{3,2},{4,3},{5,4},{6,5},{7,6},{0,7},{9,8},{10,9},{11,1... | collective-permute-start | bytes 393224 | tf_op jit(solution)/shard_map/ppermute | solution.py:565
  57.7 1.8 %shard_map.98.left_new.left_in = bf16[10,16,512]{2,1,0:T(8,128)(2,1)S(1)} custom-call(bf16[6,32,512]{2,1,0:T(8,128)(2,1)S(1)} %get-tuple-element.52.edge_in, bf16[14,16,512]{2,1,0:T(8,128)(2,1)S(1)} %get-tuple-element.47.left_new.left_in, bf16[14,16,512]{2,1,0:T(8,128)(2,1)S(1)} %shard_map.95.right_new.right_in, f32[49,4,512]{2,1,0:T(4,128)S(1)} %bitcast.9, ...), custom_call_target="tpu_custom_call" | custom-call | flops 409600000 | tf_op jit(solution)/shard_map/pallas_call | solution.py:464
  60.2 2.0 %shard_map.97 = (bf16[10,16,512]{2,1,0:T(8,128)(2,1)S(1)}, f32[4,6,16,128]{3,2,1,0:T(8,128)S(1)}, bf16[4,8,6,16,128]{4,3,2,1,0:T(8,128)(2,1)S(1)}) custom-call(bf16[6,32,512]{2,1,0:T(8,128)(2,1)S(1)} %get-tuple-element.52.edge_in, bf16[14,16,512]{2,1,0:T(8,128)(2,1)S(1)} %get-tuple-element.47.left_new.left_in, ...), custom_call_target="tpu_custom_call" | custom-call | flops 573440000 | tf_op jit(solution)/shard_map/pallas_call | solution.py:464
  62.2 2.1 %shard_map.99 = (bf16[6,32,512]{2,1,0:T(8,128)(2,1)S(1)}, bf16[6,16,512]{2,1,0:T(8,128)(2,1)S(1)}, bf16[6,8,512]{2,1,0:T(8,128)(2,1)S(1)}) custom-call(bf16[14,16,512]{2,1,0:T(8,128)(2,1)S(1)} %get-tuple-element.47.left_new.left_in, bf16[14,16,512]{2,1,0:T(8,128)(2,1)S(1)} %shard_map.95.right_new.right_in, ...), custom_call_target="tpu_custom_call" | custom-call | flops 491520000 | tf_op jit(solution)/shard_map/pallas_call | solution.py:464
  64.4 1.4 %collective-permute-start.7 = (bf16[6,32,512]{2,1,0:T(8,128)(2,1)S(1)}, bf16[6,32,512]{2,1,0:T(8,128)(2,1)S(1)}, u32[]{:S(2)}, u32[]{:S(2)}) collective-permute-start(bf16[6,32,512]{2,1,0:T(8,128)(2,1)S(1)} %get-tuple-element.57.edge_in), channel_id=1, source_target_pairs={{0,8},{8,16},{16,24},{24,0},{1,9},{9,17},{17,25},{25,1},{2,10},{10... | collective-permute-start | bytes 589832 | tf_op jit(solution)/shard_map/ppermute | solution.py:566
  66.3 2.0 %shard_map.101.right_new.right_in = bf16[14,16,512]{2,1,0:T(8,128)(2,1)S(1)} custom-call(bf16[6,32,512]{2,1,0:T(8,128)(2,1)S(1)} %get-tuple-element.57.edge_in, bf16[10,16,512]{2,1,0:T(8,128)(2,1)S(1)} %shard_map.98.left_new.left_in, bf16[10,16,512]{2,1,0:T(8,128)(2,1)S(1)} %get-tuple-element.55.right_new.right_in, f32[49,4,512]{2,1,0:T(4,128)S(1)} %bitcast.12, ...), custom_call_target="tpu_custom_call" | custom-call | flops 344064000 | tf_op jit(solution)/shard_map/pallas_call | solution.py:464
  68.3 2.0 %collective-permute-done.6.refs_0_.lon_in = bf16[6,16,512]{2,1,0:T(8,128)(2,1)S(1)} collective-permute-done((bf16[6,16,512]{2,1,0:T(8,128)(2,1)S(1)}, bf16[6,16,512]{2,1,0:T(8,128)(2,1)S(1)}, u32[]{:S(2)}, u32[]{:S(2)}) %collective-permute-start.6) | collective-permute-done | bytes 98336 | tf_op jit(solution)/shard_map/ppermute | solution.py:565
  70.3 2.0 %shard_map.100 = (bf16[14,16,512]{2,1,0:T(8,128)(2,1)S(1)}, f32[4,6,16,128]{3,2,1,0:T(8,128)S(1)}, bf16[4,8,6,16,128]{4,3,2,1,0:T(8,128)(2,1)S(1)}) custom-call(bf16[6,32,512]{2,1,0:T(8,128)(2,1)S(1)} %get-tuple-element.57.edge_in, bf16[10,16,512]{2,1,0:T(8,128)(2,1)S(1)} %shard_map.98.left_new.left_in, ...), custom_call_target="tpu_custom_call" | custom-call | flops 1261568000 | tf_op jit(solution)/shard_map/pallas_call | solution.py:464
  73.0 2.1 %shard_map.102 = (bf16[6,32,512]{2,1,0:T(8,128)(2,1)S(1)}, bf16[8,16,512]{2,1,0:T(8,128)(2,1)S(1)}, bf16[6,8,512]{2,1,0:T(8,128)(2,1)S(1)}) custom-call(bf16[10,16,512]{2,1,0:T(8,128)(2,1)S(1)} %shard_map.98.left_new.left_in, bf16[10,16,512]{2,1,0:T(8,128)(2,1)S(1)} %get-tuple-element.55.right_new.right_in, ...), custom_call_target="tpu_custom_call" | custom-call | flops 491520000 | tf_op jit(solution)/shard_map/pallas_call | solution.py:464
  75.1 1.1 %collective-permute-start.10 = (bf16[6,32,512]{2,1,0:T(8,128)(2,1)S(1)}, bf16[6,32,512]{2,1,0:T(8,128)(2,1)S(1)}, u32[]{:S(2)}, u32[]{:S(2)}) collective-permute-start(bf16[6,32,512]{2,1,0:T(8,128)(2,1)S(1)} %get-tuple-element.64.edge_in), channel_id=1, source_target_pairs={{8,0},{16,8},{24,16},{0,24},{9,1},{17,9},{25,17},{1,25},{10,2},{18... | collective-permute-start | bytes 589832 | tf_op jit(solution)/shard_map/ppermute | solution.py:566
  76.1 2.7 %collective-permute-start.9 = (bf16[8,16,512]{2,1,0:T(8,128)(2,1)S(1)}, bf16[8,16,512]{2,1,0:T(8,128)(2,1)S(1)}, u32[]{:S(2)}, u32[]{:S(2)}) collective-permute-start(bf16[8,16,512]{2,1,0:T(8,128)(2,1)S(1)} %get-tuple-element.63), channel_id=1, source_target_pairs={{1,0},{2,1},{3,2},{4,3},{5,4},{6,5},{7,6},{0,7},{9,8},{10,9},{11,1... | collective-permute-start | bytes 393224 | tf_op jit(solution)/shard_map/ppermute | solution.py:565
  79.7 1.8 %shard_map.104.left_new = bf16[10,16,512]{2,1,0:T(8,128)(2,1)S(1)} custom-call(bf16[6,32,512]{2,1,0:T(8,128)(2,1)S(1)} %get-tuple-element.64.edge_in, bf16[14,16,512]{2,1,0:T(8,128)(2,1)S(1)} %get-tuple-element.59.left_new.left_in, bf16[14,16,512]{2,1,0:T(8,128)(2,1)S(1)} %shard_map.101.right_new.right_in, f32[49,4,512]{2,1,0:T(4,128)S(1)} %bitcast.15, ...), custom_call_target="tpu_custom_call" | custom-call | flops 409600000 | tf_op jit(solution)/shard_map/pallas_call | solution.py:464
  81.5 2.0 %shard_map.103 = (bf16[10,16,512]{2,1,0:T(8,128)(2,1)S(1)}, f32[4,6,16,128]{3,2,1,0:T(8,128)S(1)}, bf16[4,8,6,16,128]{4,3,2,1,0:T(8,128)(2,1)S(1)}) custom-call(bf16[6,32,512]{2,1,0:T(8,128)(2,1)S(1)} %get-tuple-element.64.edge_in, bf16[14,16,512]{2,1,0:T(8,128)(2,1)S(1)} %get-tuple-element.59.left_new.left_in, ...), custom_call_target="tpu_custom_call" | custom-call | flops 573440000 | tf_op jit(solution)/shard_map/pallas_call | solution.py:464
  83.6 2.7 %shard_map.105 = bf16[16,32,512]{2,1,0:T(8,128)(2,1)} custom-call(bf16[14,16,512]{2,1,0:T(8,128)(2,1)S(1)} %get-tuple-element.59.left_new.left_in, bf16[14,16,512]{2,1,0:T(8,128)(2,1)S(1)} %shard_map.101.right_new.right_in, bf16[8,16,512]{2,1,0:T(8,128)(2,1)S(1)} %collective-permute-done.9.refs_0_.lon_in, ...), custom_call_target="tpu_custom_call" | custom-call | flops 491520000 | tf_op jit(solution)/shard_map/pallas_call | solution.py:464
  (26 shorter events, 4.9 us)
Async XLA Ops:
  0.0 12.2 %copy-start.2 = (bf16[256,512]{1,0:T(8,128)(2,1)S(1)}, bf16[256,512]{1,0:T(8,128)(2,1)}, u32[]{:S(2)}) copy-start(bf16[256,512]{1,0:T(8,128)(2,1)} %proj_hbm.1) | copy-start | bytes 786436
  0.0 12.2 %copy-start.1 = (bf16[16,32,512]{2,1,0:T(8,128)(2,1)S(1)}, bf16[16,32,512]{2,1,0:T(8,128)(2,1)}, u32[]{:S(2)}) copy-start(bf16[16,32,512]{2,1,0:T(8,128)(2,1)} %back_hbm.1) | copy-start | bytes 1572868
  0.0 12.3 %copy-start.3 = (f32[4,512]{1,0:T(4,128)S(1)}, f32[4,512]{1,0:T(4,128)}, u32[]{:S(2)}) copy-start(f32[4,512]{1,0:T(4,128)} %param.17) | copy-start | bytes 24580
  4.8 36.4 %all-to-all-start = ((bf16[32,136,128]{2,1,0:T(8,128)(2,1)}), bf16[32,136,128]{2,1,0:T(8,128)(2,1)}, u32[]{:S(2)}, u32[]{:S(2)}) async-start(bf16[32,136,128]{2,1,0:T(8,128)(2,1)} %shard_map.91), calls=%async_computation | async-start | bytes 2228224 | tf_op jit(solution)/shard_map/all_to_all | solution.py:594
  12.3 33.2 %copy-start = (f32[4,7,7,512]{3,0,2,1:T(4,128)S(1)}, f32[4,7,7,512]{3,0,2,1:T(4,128)}, u32[]{:S(2)}) copy-start(f32[4,7,7,512]{3,0,2,1:T(4,128)} %param.15) | copy-start | bytes 1204228
  43.8 5.9 %collective-permute-start = (bf16[6,16,512]{2,1,0:T(8,128)(2,1)S(1)}, bf16[6,16,512]{2,1,0:T(8,128)(2,1)S(1)}, u32[]{:S(2)}, u32[]{:S(2)}) collective-permute-start(bf16[6,16,512]{2,1,0:T(8,128)(2,1)S(1)} %get-tuple-element.45), channel_id=1, source_target_pairs={{0,1},{1,2},{2,3},{3,4},{4,5},{5,6},{6,7},{7,0},{8,9},{9,10},{10,1... | collective-permute-start | bytes 294920 | tf_op jit(solution)/shard_map/ppermute | solution.py:565
  43.9 8.1 %collective-permute-start.1 = (bf16[6,32,512]{2,1,0:T(8,128)(2,1)S(1)}, bf16[6,32,512]{2,1,0:T(8,128)(2,1)S(1)}, u32[]{:S(2)}, u32[]{:S(2)}) collective-permute-start(bf16[6,32,512]{2,1,0:T(8,128)(2,1)S(1)} %get-tuple-element.42.edge_in), channel_id=1, source_target_pairs={{0,8},{8,16},{16,24},{24,0},{1,9},{9,17},{17,25},{25,1},{2,10},{10... | collective-permute-start | bytes 589832 | tf_op jit(solution)/shard_map/ppermute | solution.py:566
  44.7 7.2 %collective-permute-start.2 = (bf16[6,8,512]{2,1,0:T(8,128)(2,1)S(1)}, bf16[6,8,512]{2,1,0:T(8,128)(2,1)S(1)}, u32[]{:S(2)}, u32[]{:S(2)}) collective-permute-start(bf16[6,8,512]{2,1,0:T(8,128)(2,1)S(1)} %get-tuple-element.48), channel_id=1, source_target_pairs={{0,9},{1,10},{2,11},{3,12},{4,13},{5,14},{6,15},{7,8},{8,17},{9,18... | collective-permute-start | bytes 147464 | tf_op jit(solution)/shard_map/ppermute | solution.py:567
  54.0 8.2 %collective-permute-start.4 = (bf16[6,32,512]{2,1,0:T(8,128)(2,1)S(1)}, bf16[6,32,512]{2,1,0:T(8,128)(2,1)S(1)}, u32[]{:S(2)}, u32[]{:S(2)}) collective-permute-start(bf16[6,32,512]{2,1,0:T(8,128)(2,1)S(1)} %get-tuple-element.52.edge_in), channel_id=1, source_target_pairs={{8,0},{16,8},{24,16},{0,24},{9,1},{17,9},{25,17},{1,25},{10,2},{18... | collective-permute-start | bytes 589832 | tf_op jit(solution)/shard_map/ppermute | solution.py:566
  55.2 5.0 %collective-permute-start.3 = (bf16[8,16,512]{2,1,0:T(8,128)(2,1)S(1)}, bf16[8,16,512]{2,1,0:T(8,128)(2,1)S(1)}, u32[]{:S(2)}, u32[]{:S(2)}) collective-permute-start(bf16[8,16,512]{2,1,0:T(8,128)(2,1)S(1)} %get-tuple-element.51), channel_id=1, source_target_pairs={{1,0},{2,1},{3,2},{4,3},{5,4},{6,5},{7,6},{0,7},{9,8},{10,9},{11,1... | collective-permute-start | bytes 393224 | tf_op jit(solution)/shard_map/ppermute | solution.py:565
  57.6 4.5 %collective-permute-start.5 = (bf16[6,8,512]{2,1,0:T(8,128)(2,1)S(1)}, bf16[6,8,512]{2,1,0:T(8,128)(2,1)S(1)}, u32[]{:S(2)}, u32[]{:S(2)}) collective-permute-start(bf16[6,8,512]{2,1,0:T(8,128)(2,1)S(1)} %get-tuple-element.53), channel_id=1, source_target_pairs={{9,0},{10,1},{11,2},{12,3},{13,4},{14,5},{15,6},{8,7},{17,8},{18,9... | collective-permute-start | bytes 147464 | tf_op jit(solution)/shard_map/ppermute | solution.py:567
  64.3 6.0 %collective-permute-start.6 = (bf16[6,16,512]{2,1,0:T(8,128)(2,1)S(1)}, bf16[6,16,512]{2,1,0:T(8,128)(2,1)S(1)}, u32[]{:S(2)}, u32[]{:S(2)}) collective-permute-start(bf16[6,16,512]{2,1,0:T(8,128)(2,1)S(1)} %get-tuple-element.58), channel_id=1, source_target_pairs={{0,1},{1,2},{2,3},{3,4},{4,5},{5,6},{6,7},{7,0},{8,9},{9,10},{10,1... | collective-permute-start | bytes 294920 | tf_op jit(solution)/shard_map/ppermute | solution.py:565
  64.4 8.7 %collective-permute-start.7 = (bf16[6,32,512]{2,1,0:T(8,128)(2,1)S(1)}, bf16[6,32,512]{2,1,0:T(8,128)(2,1)S(1)}, u32[]{:S(2)}, u32[]{:S(2)}) collective-permute-start(bf16[6,32,512]{2,1,0:T(8,128)(2,1)S(1)} %get-tuple-element.57.edge_in), channel_id=1, source_target_pairs={{0,8},{8,16},{16,24},{24,0},{1,9},{9,17},{17,25},{25,1},{2,10},{10... | collective-permute-start | bytes 589832 | tf_op jit(solution)/shard_map/ppermute | solution.py:566
  65.8 7.2 %collective-permute-start.8 = (bf16[6,8,512]{2,1,0:T(8,128)(2,1)S(1)}, bf16[6,8,512]{2,1,0:T(8,128)(2,1)S(1)}, u32[]{:S(2)}, u32[]{:S(2)}) collective-permute-start(bf16[6,8,512]{2,1,0:T(8,128)(2,1)S(1)} %get-tuple-element.60), channel_id=1, source_target_pairs={{0,9},{1,10},{2,11},{3,12},{4,13},{5,14},{6,15},{7,8},{8,17},{9,18... | collective-permute-start | bytes 147464 | tf_op jit(solution)/shard_map/ppermute | solution.py:567
  75.1 8.5 %collective-permute-start.10 = (bf16[6,32,512]{2,1,0:T(8,128)(2,1)S(1)}, bf16[6,32,512]{2,1,0:T(8,128)(2,1)S(1)}, u32[]{:S(2)}, u32[]{:S(2)}) collective-permute-start(bf16[6,32,512]{2,1,0:T(8,128)(2,1)S(1)} %get-tuple-element.64.edge_in), channel_id=1, source_target_pairs={{8,0},{16,8},{24,16},{0,24},{9,1},{17,9},{25,17},{1,25},{10,2},{18... | collective-permute-start | bytes 589832 | tf_op jit(solution)/shard_map/ppermute | solution.py:566
  76.1 5.4 %collective-permute-start.9 = (bf16[8,16,512]{2,1,0:T(8,128)(2,1)S(1)}, bf16[8,16,512]{2,1,0:T(8,128)(2,1)S(1)}, u32[]{:S(2)}, u32[]{:S(2)}) collective-permute-start(bf16[8,16,512]{2,1,0:T(8,128)(2,1)S(1)} %get-tuple-element.63), channel_id=1, source_target_pairs={{1,0},{2,1},{3,2},{4,3},{5,4},{6,5},{7,6},{0,7},{9,8},{10,9},{11,1... | collective-permute-start | bytes 393224 | tf_op jit(solution)/shard_map/ppermute | solution.py:565
  78.9 4.7 %collective-permute-start.11 = (bf16[6,8,512]{2,1,0:T(8,128)(2,1)S(1)}, bf16[6,8,512]{2,1,0:T(8,128)(2,1)S(1)}, u32[]{:S(2)}, u32[]{:S(2)}) collective-permute-start(bf16[6,8,512]{2,1,0:T(8,128)(2,1)S(1)} %get-tuple-element.65), channel_id=1, source_target_pairs={{9,0},{10,1},{11,2},{12,3},{13,4},{14,5},{15,6},{8,7},{17,8},{18,9... | collective-permute-start | bytes 147464 | tf_op jit(solution)/shard_map/ppermute | solution.py:567

commit v8 on v7

--- a/solution.py
+++ b/solution.py
@@ -217,7 +217,7 @@
             taps_in[g, r, target] = wide_ref[g, row, columns, :].astype(BF16)
 
 
-def convolve(taps_in, taps_ref, tap_ref, spread_ref, layer, g, first, count):
+def convolve(shifts, taps_ref, tap_ref, spread_ref, layer, g, first, count):
     lanes = pl.ds(pl.multiple_of(g * LANES, LANES), LANES)
     for k in range(TAPS * TAPS):
         row = taps_ref[k, layer : layer + 1, lanes]
@@ -225,7 +225,7 @@
     for p in range(2):
         total = None
         for b in range(TAPS):
-            seen = taps_in[g, p + b, first : first + count + TAPS - 1]
+            seen = shifts[p + b, first : first + count + TAPS - 1]
             part = None
             for a in range(TAPS):
                 term = seen[a : a + count] * tap_ref[a * TAPS + b]
@@ -234,7 +234,7 @@
         spread_ref[p, first : first + count, :, lanes] = total
 
 
-def finish(taps_in, spread_ref, mix_ref, out_ref, layer, first, count, stacked=1):
+def finish(center_ref, spread_ref, mix_ref, out_ref, layer, first, count, stacked=1):
     chans = mix_ref.shape[1]
     ones = jnp.ones((chans, LANES), BF16)
     step = TILE // stacked
@@ -245,7 +245,7 @@
     for g in range(chans // LANES):
         moved = gelu(mixed[:, lanes_of(g)] * scale).reshape(2, count, TILE, LANES)
         for p in range(2):
-            center = taps_in[g, p + HALO, first + HALO : first + HALO + count].astype(F32)
+            center = center_ref[g, p, first : first + count].astype(F32)
             fresh = center + moved[p]
             for k in range(count):
                 for h in range(stacked):
@@ -277,7 +277,7 @@
         taps_ref, mix_ref, block_ref, *scratch = refs
     else:
         lon_in, taps_ref, mix_ref, block_ref, lon_ref, near_ref, *scratch = refs
-    wide_ref, taps_in, tap_ref, spread_ref, out_ref = scratch
+    wide_ref, taps_in, center_ref, tap_ref, spread_ref, out_ref = scratch
     cols = edge_in.shape[1]
     groups = wide_ref.shape[0]
     width = wide_ref.shape[2]
@@ -305,21 +305,19 @@
         put(wide_ref, place, main + TILE, right_in[y].astype(F32))
 
     def stage(high):
-        @pl.loop(0, high + TAPS - 1)
-        def _(y):
-            for g in range(groups):
+        @pl.loop(0, groups)
+        def _(g):
+            for y in range(high + TAPS - 1):
                 for r in range(TAPS + 1):
                     both = [
                         wide_ref[g, y + h, pl.ds(start + r, TILE // 2, stride=2), :]
                         for h in (0, high)
                     ]
-                    taps_in[g, r, y] = jnp.concatenate(both, axis=0).astype(BF16)
-
-        @pl.loop(0, groups)
-        def _(g):
+                    taps_in[r, y] = jnp.concatenate(both, axis=0).astype(BF16)
+            center_ref[g, :, 0:high] = taps_in[HALO : HALO + 2, HALO : HALO + high]
             convolve(taps_in, taps_ref, tap_ref, spread_ref, layer, g, 0, high)
 
-        finish(taps_in, spread_ref, mix_ref, out_ref, layer, 0, high, 2)
+        finish(center_ref, spread_ref, mix_ref, out_ref, layer, 0, high, 2)
 
         @pl.loop(0, 2 * high, unroll=2)
         def _(y):
@@ -417,9 +415,10 @@
 
     @pl.loop(0, groups)
     def _(g):
-        convolve(taps_in, taps_ref, tap_ref, spread_ref, layer, g, 0, SHIFT)
-
-    finish(taps_in, spread_ref, mix_ref, out_ref, layer, 0, SHIFT)
+        convolve(taps_in.at[g], taps_ref, tap_ref, spread_ref, layer, g, 0, SHIFT)
+
+    center_ref = taps_in.at[:, HALO : HALO + 2, HALO : HALO + SHIFT]
+    finish(center_ref, spread_ref, mix_ref, out_ref, layer, 0, SHIFT)
     kept = left_new.shape[0]
     if final:
         for k in range(SHIFT):
@@ -498,7 +497,8 @@
     block = held(made, TILE, chans)
     scratch = (
         pltpu.VMEM((groups, rows + spare, cols + EDGE, LANES), F32),
-        pltpu.VMEM((groups, TAPS + 1, made // 2 + TAPS - 1, TILE, LANES), BF16),
+        pltpu.VMEM((TAPS + 1, made // 2 + TAPS - 1, TILE, LANES), BF16),
+        pltpu.VMEM((groups, 2, made // 2, TILE, LANES), BF16),
         pltpu.VMEM((TAPS * TAPS, TILE, LANES), BF16),
         pltpu.VMEM((2, made // 2, TILE, chans), BF16),
         pltpu.VMEM((groups, made, TILE, LANES), F32),

time: 87 us -> 86.7 us (level)
  transfers between devices with their start and end apart: 13 -> 13, of which waited for: 6 -> 8; matrix products, arithmetic and copies ran while one was open for 2% -> 2% of each run, Pallas kernels for 18% -> 17%
where the time goes in v8:
time: 86.7 us; the launch traced here: 86.2 us
  waiting for transfers between devices  33.2 us (38%)
  Pallas kernels  31.1 us (36%)
  starting transfers between devices  19.3 us (22%)
  other arithmetic  2.11 us (2%)
    pallas_call x15, Pallas kernels, call(): pl.pallas_call(kernel, out_shape=out_shape, in_specs=[pl.BlockSpec(memory...  31.1 us
    all_to_all x1, waiting for transfers between devices, body(): lax.all_to_all(send, ('lat', 'lon'), split_axis=0, concat_axis=0, tiled=T...  26.7 us
    all_to_all x1, starting transfers between devices, body(): lax.all_to_all(send, ('lat', 'lon'), split_axis=0, concat_axis=0, tiled=T...  7.42 us
    ppermute x4, waiting for transfers between devices, exchange(): lon = lax.ppermute(lon, 'lon', around)  5.01 us
    ppermute x4, starting transfers between devices, exchange(): lon = lax.ppermute(lon, 'lon', around)  4.89 us
    ppermute x4, starting transfers between devices, exchange(): lat = lax.ppermute(lat, 'lat', along)  4.43 us
    ppermute x4, starting transfers between devices, exchange(): corner = lax.ppermute(corner, ('lat', 'lon'), across)  2.59 us
    convert_element_type x1, other arithmetic, body(): mix = (gains[:, :, None] * point_w.astype(F32)).astype(BF16)  2.11 us
  transfers between devices with their start and end apart: 13, of which 8 were waited for; matrix products, arithmetic and copies ran while one was open for 2% of the time, Pallas kernels for 17%

profile of v8, /device:TPU:0, one launch (start us, length us, event | category | flops | bytes accessed | tf_op | source)
XLA Modules:
  0.0 86.2 jit_solution(12426636763452145561)
XLA Ops:
  0.0 4.8 %shard_map.91 = bf16[32,136,128]{2,1,0:T(8,128)(2,1)} custom-call(s32[1,1024]{1,0:T(1,128)} %bitcast.20, s32[4,1024]{1,0:T(4,128)} %bitcast.18, bf16[4,1024]{1,0:T(4,128)(2,1)} %bitcast.19, bf16[1024,256]{1,0:T(8,128)(2,1)} %obs_hbm.1), custom_call_target="tpu_custom_call" | custom-call | tf_op jit(solution)/shard_map/pallas_call | solution.py:463
  4.8 7.4 %all-to-all-start = ((bf16[32,136,128]{2,1,0:T(8,128)(2,1)}), bf16[32,136,128]{2,1,0:T(8,128)(2,1)}, u32[]{:S(2)}, u32[]{:S(2)}) async-start(bf16[32,136,128]{2,1,0:T(8,128)(2,1)} %shard_map.91), calls=%async_computation | async-start | bytes 2228224 | tf_op jit(solution)/shard_map/all_to_all | solution.py:594
  12.3 2.1 %multiply_convert_fusion.refs_2_.refs_1_.mix_ref = bf16[4,512,512]{2,1,0:T(8,128)(2,1)S(1)} fusion(bf16[4,512,512]{2,1,0:T(8,128)(2,1)} %param.16, f32[4,512]{1,0:T(4,128)S(1)} %copy-done.3), kind=kLoop, calls=%fused_computation | loop fusion | flops 3145728 | bytes 4202496 | tf_op jit(solution)/shard_map/convert_element_type | solution.py:597
  14.5 26.7 %all-to-all-done.got_hbm = bf16[32,136,128]{2,1,0:T(8,128)(2,1)} async-done(((bf16[32,136,128]{2,1,0:T(8,128)(2,1)}), bf16[32,136,128]{2,1,0:T(8,128)(2,1)}, u32[]{:S(2)}, u32[]{:S(2)}) %all-to-all-start) | async-done | bytes 1114144 | tf_op jit(solution)/shard_map/all_to_all | solution.py:594
  41.2 2.6 %shard_map.93 = (bf16[6,32,512]{2,1,0:T(8,128)(2,1)S(1)}, bf16[10,16,512]{2,1,0:T(8,128)(2,1)S(1)}, bf16[10,16,512]{2,1,0:T(8,128)(2,1)S(1)}, bf16[6,16,512]{2,1,0:T(8,128)(2,1)S(1)}, bf16[6,8,512]{2,1,0:T(8,128)(2,1)S(1)}) custom-call(bf16[32,136,128]{2,1,0:T(8,128)(2,1)} %all-to-all-done.got_hbm, bf16[256,512]{1,0:T(8,128)(2,1)S(1)} %get-tuple-element.40.proj_ref, ...), custom_call_target="tpu_custom_call" | custom-call | tf_op jit(solution)/shard_map/pallas_call | solution.py:463
  45.6 1.7 %shard_map.95.right_new.right_in = bf16[14,16,512]{2,1,0:T(8,128)(2,1)S(1)} custom-call(bf16[6,32,512]{2,1,0:T(8,128)(2,1)S(1)} %get-tuple-element.42.edge_in, bf16[10,16,512]{2,1,0:T(8,128)(2,1)S(1)} %get-tuple-element.43.left_in, bf16[10,16,512]{2,1,0:T(8,128)(2,1)S(1)} %get-tuple-element.44.right_in, f32[49,4,512]{2,1,0:T(4,128)S(1)} %bitcast.6, ...), custom_call_target="tpu_custom_call" | custom-call | flops 344064000 | tf_op jit(solution)/shard_map/pallas_call | solution.py:463
  47.3 2.4 %collective-permute-done.refs_0_.lon_in = bf16[6,16,512]{2,1,0:T(8,128)(2,1)S(1)} collective-permute-done((bf16[6,16,512]{2,1,0:T(8,128)(2,1)S(1)}, bf16[6,16,512]{2,1,0:T(8,128)(2,1)S(1)}, u32[]{:S(2)}, u32[]{:S(2)}) %collective-permute-start) | collective-permute-done | bytes 98336 | tf_op jit(solution)/shard_map/ppermute | solution.py:565
  49.7 1.9 %shard_map.94 = (bf16[14,16,512]{2,1,0:T(8,128)(2,1)S(1)}, f32[4,6,16,128]{3,2,1,0:T(8,128)S(1)}, bf16[4,8,6,16,128]{4,3,2,1,0:T(8,128)(2,1)S(1)}) custom-call(bf16[6,32,512]{2,1,0:T(8,128)(2,1)S(1)} %get-tuple-element.42.edge_in, bf16[10,16,512]{2,1,0:T(8,128)(2,1)S(1)} %get-tuple-element.43.left_in, bf16[10,16,512]{2,1,0:T(8,128)(2,1)S(1)} %get-tuple-element.44.right_in, ...), custom_call_target="tpu_custom_call" | custom-call | flops 1261568000 | tf_op jit(solution)/shard_map/pallas_call | solution.py:463
  51.9 2.1 %shard_map.96 = (bf16[6,32,512]{2,1,0:T(8,128)(2,1)S(1)}, bf16[8,16,512]{2,1,0:T(8,128)(2,1)S(1)}, bf16[6,8,512]{2,1,0:T(8,128)(2,1)S(1)}) custom-call(bf16[10,16,512]{2,1,0:T(8,128)(2,1)S(1)} %get-tuple-element.43.left_in, bf16[10,16,512]{2,1,0:T(8,128)(2,1)S(1)} %get-tuple-element.44.right_in, bf16[6,16,512]{2,1,0:T(8,128)(2,1)S(1)} %collective-permute-done.refs_0_.lon_in, ...), custom_call_target="tpu_custom_call" | custom-call | flops 491520000 | tf_op jit(solution)/shard_map/pallas_call | solution.py:463
  54.0 1.2 %collective-permute-start.4 = (bf16[6,32,512]{2,1,0:T(8,128)(2,1)S(1)}, bf16[6,32,512]{2,1,0:T(8,128)(2,1)S(1)}, u32[]{:S(2)}, u32[]{:S(2)}) collective-permute-start(bf16[6,32,512]{2,1,0:T(8,128)(2,1)S(1)} %get-tuple-element.52.edge_in), channel_id=1, source_target_pairs={{8,0},{16,8},{24,16},{0,24},{9,1},{17,9},{25,17},{1,25},{10,2},{18... | collective-permute-start | bytes 589832 | tf_op jit(solution)/shard_map/ppermute | solution.py:566
  55.2 2.1 %collective-permute-start.3 = (bf16[8,16,512]{2,1,0:T(8,128)(2,1)S(1)}, bf16[8,16,512]{2,1,0:T(8,128)(2,1)S(1)}, u32[]{:S(2)}, u32[]{:S(2)}) collective-permute-start(bf16[8,16,512]{2,1,0:T(8,128)(2,1)S(1)} %get-tuple-element.51), channel_id=1, source_target_pairs={{1,0},{2,1},{3,2},{4,3},{5,4},{6,5},{7,6},{0,7},{9,8},{10,9},{11,1... | collective-permute-start | bytes 393224 | tf_op jit(solution)/shard_map/ppermute | solution.py:565
  57.5 1.7 %shard_map.98.left_new.left_in = bf16[10,16,512]{2,1,0:T(8,128)(2,1)S(1)} custom-call(bf16[6,32,512]{2,1,0:T(8,128)(2,1)S(1)} %get-tuple-element.52.edge_in, bf16[14,16,512]{2,1,0:T(8,128)(2,1)S(1)} %get-tuple-element.47.left_new.left_in, bf16[14,16,512]{2,1,0:T(8,128)(2,1)S(1)} %shard_map.95.right_new.right_in, f32[49,4,512]{2,1,0:T(4,128)S(1)} %bitcast.9, ...), custom_call_target="tpu_custom_call" | custom-call | flops 409600000 | tf_op jit(solution)/shard_map/pallas_call | solution.py:463
  59.9 1.9 %shard_map.97 = (bf16[10,16,512]{2,1,0:T(8,128)(2,1)S(1)}, f32[4,6,16,128]{3,2,1,0:T(8,128)S(1)}, bf16[4,8,6,16,128]{4,3,2,1,0:T(8,128)(2,1)S(1)}) custom-call(bf16[6,32,512]{2,1,0:T(8,128)(2,1)S(1)} %get-tuple-element.52.edge_in, bf16[14,16,512]{2,1,0:T(8,128)(2,1)S(1)} %get-tuple-element.47.left_new.left_in, ...), custom_call_target="tpu_custom_call" | custom-call | flops 573440000 | tf_op jit(solution)/shard_map/pallas_call | solution.py:463
  62.2 2.1 %shard_map.99 = (bf16[6,32,512]{2,1,0:T(8,128)(2,1)S(1)}, bf16[6,16,512]{2,1,0:T(8,128)(2,1)S(1)}, bf16[6,8,512]{2,1,0:T(8,128)(2,1)S(1)}) custom-call(bf16[14,16,512]{2,1,0:T(8,128)(2,1)S(1)} %get-tuple-element.47.left_new.left_in, bf16[14,16,512]{2,1,0:T(8,128)(2,1)S(1)} %shard_map.95.right_new.right_in, ...), custom_call_target="tpu_custom_call" | custom-call | flops 491520000 | tf_op jit(solution)/shard_map/pallas_call | solution.py:463
  64.3 1.3 %collective-permute-start.7 = (bf16[6,32,512]{2,1,0:T(8,128)(2,1)S(1)}, bf16[6,32,512]{2,1,0:T(8,128)(2,1)S(1)}, u32[]{:S(2)}, u32[]{:S(2)}) collective-permute-start(bf16[6,32,512]{2,1,0:T(8,128)(2,1)S(1)} %get-tuple-element.57.edge_in), channel_id=1, source_target_pairs={{0,8},{8,16},{16,24},{24,0},{1,9},{9,17},{17,25},{25,1},{2,10},{10... | collective-permute-start | bytes 589832 | tf_op jit(solution)/shard_map/ppermute | solution.py:566
  66.3 1.9 %shard_map.101.right_new.right_in = bf16[14,16,512]{2,1,0:T(8,128)(2,1)S(1)} custom-call(bf16[6,32,512]{2,1,0:T(8,128)(2,1)S(1)} %get-tuple-element.57.edge_in, bf16[10,16,512]{2,1,0:T(8,128)(2,1)S(1)} %shard_map.98.left_new.left_in, bf16[10,16,512]{2,1,0:T(8,128)(2,1)S(1)} %get-tuple-element.55.right_new.right_in, f32[49,4,512]{2,1,0:T(4,128)S(1)} %bitcast.12, ...), custom_call_target="tpu_custom_call" | custom-call | flops 344064000 | tf_op jit(solution)/shard_map/pallas_call | solution.py:463
  68.2 1.9 %collective-permute-done.6.refs_0_.lon_in = bf16[6,16,512]{2,1,0:T(8,128)(2,1)S(1)} collective-permute-done((bf16[6,16,512]{2,1,0:T(8,128)(2,1)S(1)}, bf16[6,16,512]{2,1,0:T(8,128)(2,1)S(1)}, u32[]{:S(2)}, u32[]{:S(2)}) %collective-permute-start.6) | collective-permute-done | bytes 98336 | tf_op jit(solution)/shard_map/ppermute | solution.py:565
  70.2 1.9 %shard_map.100 = (bf16[14,16,512]{2,1,0:T(8,128)(2,1)S(1)}, f32[4,6,16,128]{3,2,1,0:T(8,128)S(1)}, bf16[4,8,6,16,128]{4,3,2,1,0:T(8,128)(2,1)S(1)}) custom-call(bf16[6,32,512]{2,1,0:T(8,128)(2,1)S(1)} %get-tuple-element.57.edge_in, bf16[10,16,512]{2,1,0:T(8,128)(2,1)S(1)} %shard_map.98.left_new.left_in, ...), custom_call_target="tpu_custom_call" | custom-call | flops 1261568000 | tf_op jit(solution)/shard_map/pallas_call | solution.py:463
  72.8 2.1 %shard_map.102 = (bf16[6,32,512]{2,1,0:T(8,128)(2,1)S(1)}, bf16[8,16,512]{2,1,0:T(8,128)(2,1)S(1)}, bf16[6,8,512]{2,1,0:T(8,128)(2,1)S(1)}) custom-call(bf16[10,16,512]{2,1,0:T(8,128)(2,1)S(1)} %shard_map.98.left_new.left_in, bf16[10,16,512]{2,1,0:T(8,128)(2,1)S(1)} %get-tuple-element.55.right_new.right_in, ...), custom_call_target="tpu_custom_call" | custom-call | flops 491520000 | tf_op jit(solution)/shard_map/pallas_call | solution.py:463
  74.9 1.1 %collective-permute-start.10 = (bf16[6,32,512]{2,1,0:T(8,128)(2,1)S(1)}, bf16[6,32,512]{2,1,0:T(8,128)(2,1)S(1)}, u32[]{:S(2)}, u32[]{:S(2)}) collective-permute-start(bf16[6,32,512]{2,1,0:T(8,128)(2,1)S(1)} %get-tuple-element.64.edge_in), channel_id=1, source_target_pairs={{8,0},{16,8},{24,16},{0,24},{9,1},{17,9},{25,17},{1,25},{10,2},{18... | collective-permute-start | bytes 589832 | tf_op jit(solution)/shard_map/ppermute | solution.py:566
  76.0 2.6 %collective-permute-start.9 = (bf16[8,16,512]{2,1,0:T(8,128)(2,1)S(1)}, bf16[8,16,512]{2,1,0:T(8,128)(2,1)S(1)}, u32[]{:S(2)}, u32[]{:S(2)}) collective-permute-start(bf16[8,16,512]{2,1,0:T(8,128)(2,1)S(1)} %get-tuple-element.63), channel_id=1, source_target_pairs={{1,0},{2,1},{3,2},{4,3},{5,4},{6,5},{7,6},{0,7},{9,8},{10,9},{11,1... | collective-permute-start | bytes 393224 | tf_op jit(solution)/shard_map/ppermute | solution.py:565
  79.6 1.7 %shard_map.104.left_new = bf16[10,16,512]{2,1,0:T(8,128)(2,1)S(1)} custom-call(bf16[6,32,512]{2,1,0:T(8,128)(2,1)S(1)} %get-tuple-element.64.edge_in, bf16[14,16,512]{2,1,0:T(8,128)(2,1)S(1)} %get-tuple-element.59.left_new.left_in, bf16[14,16,512]{2,1,0:T(8,128)(2,1)S(1)} %shard_map.101.right_new.right_in, f32[49,4,512]{2,1,0:T(4,128)S(1)} %bitcast.15, ...), custom_call_target="tpu_custom_call" | custom-call | flops 409600000 | tf_op jit(solution)/shard_map/pallas_call | solution.py:463
  81.3 1.9 %shard_map.103 = (bf16[10,16,512]{2,1,0:T(8,128)(2,1)S(1)}, f32[4,6,16,128]{3,2,1,0:T(8,128)S(1)}, bf16[4,8,6,16,128]{4,3,2,1,0:T(8,128)(2,1)S(1)}) custom-call(bf16[6,32,512]{2,1,0:T(8,128)(2,1)S(1)} %get-tuple-element.64.edge_in, bf16[14,16,512]{2,1,0:T(8,128)(2,1)S(1)} %get-tuple-element.59.left_new.left_in, ...), custom_call_target="tpu_custom_call" | custom-call | flops 573440000 | tf_op jit(solution)/shard_map/pallas_call | solution.py:463
  83.3 2.7 %shard_map.105 = bf16[16,32,512]{2,1,0:T(8,128)(2,1)} custom-call(bf16[14,16,512]{2,1,0:T(8,128)(2,1)S(1)} %get-tuple-element.59.left_new.left_in, bf16[14,16,512]{2,1,0:T(8,128)(2,1)S(1)} %shard_map.101.right_new.right_in, bf16[8,16,512]{2,1,0:T(8,128)(2,1)S(1)} %collective-permute-done.9.refs_0_.lon_in, ...), custom_call_target="tpu_custom_call" | custom-call | flops 491520000 | tf_op jit(solution)/shard_map/pallas_call | solution.py:463
  (26 shorter events, 5.8 us)
Async XLA Ops:
  0.0 12.2 %copy-start.2 = (bf16[256,512]{1,0:T(8,128)(2,1)S(1)}, bf16[256,512]{1,0:T(8,128)(2,1)}, u32[]{:S(2)}) copy-start(bf16[256,512]{1,0:T(8,128)(2,1)} %proj_hbm.1) | copy-start | bytes 786436
  0.0 12.2 %copy-start.1 = (bf16[16,32,512]{2,1,0:T(8,128)(2,1)S(1)}, bf16[16,32,512]{2,1,0:T(8,128)(2,1)}, u32[]{:S(2)}) copy-start(bf16[16,32,512]{2,1,0:T(8,128)(2,1)} %back_hbm.1) | copy-start | bytes 1572868
  0.0 12.3 %copy-start.3 = (f32[4,512]{1,0:T(4,128)S(1)}, f32[4,512]{1,0:T(4,128)}, u32[]{:S(2)}) copy-start(f32[4,512]{1,0:T(4,128)} %param.17) | copy-start | bytes 24580
  4.8 36.4 %all-to-all-start = ((bf16[32,136,128]{2,1,0:T(8,128)(2,1)}), bf16[32,136,128]{2,1,0:T(8,128)(2,1)}, u32[]{:S(2)}, u32[]{:S(2)}) async-start(bf16[32,136,128]{2,1,0:T(8,128)(2,1)} %shard_map.91), calls=%async_computation | async-start | bytes 2228224 | tf_op jit(solution)/shard_map/all_to_all | solution.py:594
  12.3 33.2 %copy-start = (f32[4,7,7,512]{3,0,2,1:T(4,128)S(1)}, f32[4,7,7,512]{3,0,2,1:T(4,128)}, u32[]{:S(2)}) copy-start(f32[4,7,7,512]{3,0,2,1:T(4,128)} %param.15) | copy-start | bytes 1204228
  43.8 5.9 %collective-permute-start = (bf16[6,16,512]{2,1,0:T(8,128)(2,1)S(1)}, bf16[6,16,512]{2,1,0:T(8,128)(2,1)S(1)}, u32[]{:S(2)}, u32[]{:S(2)}) collective-permute-start(bf16[6,16,512]{2,1,0:T(8,128)(2,1)S(1)} %get-tuple-element.45), channel_id=1, source_target_pairs={{0,1},{1,2},{2,3},{3,4},{4,5},{5,6},{6,7},{7,0},{8,9},{9,10},{10,1... | collective-permute-start | bytes 294920 | tf_op jit(solution)/shard_map/ppermute | solution.py:565
  43.9 8.1 %collective-permute-start.1 = (bf16[6,32,512]{2,1,0:T(8,128)(2,1)S(1)}, bf16[6,32,512]{2,1,0:T(8,128)(2,1)S(1)}, u32[]{:S(2)}, u32[]{:S(2)}) collective-permute-start(bf16[6,32,512]{2,1,0:T(8,128)(2,1)S(1)} %get-tuple-element.42.edge_in), channel_id=1, source_target_pairs={{0,8},{8,16},{16,24},{24,0},{1,9},{9,17},{17,25},{25,1},{2,10},{10... | collective-permute-start | bytes 589832 | tf_op jit(solution)/shard_map/ppermute | solution.py:566
  44.7 7.2 %collective-permute-start.2 = (bf16[6,8,512]{2,1,0:T(8,128)(2,1)S(1)}, bf16[6,8,512]{2,1,0:T(8,128)(2,1)S(1)}, u32[]{:S(2)}, u32[]{:S(2)}) collective-permute-start(bf16[6,8,512]{2,1,0:T(8,128)(2,1)S(1)} %get-tuple-element.48), channel_id=1, source_target_pairs={{0,9},{1,10},{2,11},{3,12},{4,13},{5,14},{6,15},{7,8},{8,17},{9,18... | collective-permute-start | bytes 147464 | tf_op jit(solution)/shard_map/ppermute | solution.py:567
  54.0 8.1 %collective-permute-start.4 = (bf16[6,32,512]{2,1,0:T(8,128)(2,1)S(1)}, bf16[6,32,512]{2,1,0:T(8,128)(2,1)S(1)}, u32[]{:S(2)}, u32[]{:S(2)}) collective-permute-start(bf16[6,32,512]{2,1,0:T(8,128)(2,1)S(1)} %get-tuple-element.52.edge_in), channel_id=1, source_target_pairs={{8,0},{16,8},{24,16},{0,24},{9,1},{17,9},{25,17},{1,25},{10,2},{18... | collective-permute-start | bytes 589832 | tf_op jit(solution)/shard_map/ppermute | solution.py:566
  55.2 4.7 %collective-permute-start.3 = (bf16[8,16,512]{2,1,0:T(8,128)(2,1)S(1)}, bf16[8,16,512]{2,1,0:T(8,128)(2,1)S(1)}, u32[]{:S(2)}, u32[]{:S(2)}) collective-permute-start(bf16[8,16,512]{2,1,0:T(8,128)(2,1)S(1)} %get-tuple-element.51), channel_id=1, source_target_pairs={{1,0},{2,1},{3,2},{4,3},{5,4},{6,5},{7,6},{0,7},{9,8},{10,9},{11,1... | collective-permute-start | bytes 393224 | tf_op jit(solution)/shard_map/ppermute | solution.py:565
  57.4 4.6 %collective-permute-start.5 = (bf16[6,8,512]{2,1,0:T(8,128)(2,1)S(1)}, bf16[6,8,512]{2,1,0:T(8,128)(2,1)S(1)}, u32[]{:S(2)}, u32[]{:S(2)}) collective-permute-start(bf16[6,8,512]{2,1,0:T(8,128)(2,1)S(1)} %get-tuple-element.53), channel_id=1, source_target_pairs={{9,0},{10,1},{11,2},{12,3},{13,4},{14,5},{15,6},{8,7},{17,8},{18,9... | collective-permute-start | bytes 147464 | tf_op jit(solution)/shard_map/ppermute | solution.py:567
  64.3 5.9 %collective-permute-start.6 = (bf16[6,16,512]{2,1,0:T(8,128)(2,1)S(1)}, bf16[6,16,512]{2,1,0:T(8,128)(2,1)S(1)}, u32[]{:S(2)}, u32[]{:S(2)}) collective-permute-start(bf16[6,16,512]{2,1,0:T(8,128)(2,1)S(1)} %get-tuple-element.58), channel_id=1, source_target_pairs={{0,1},{1,2},{2,3},{3,4},{4,5},{5,6},{6,7},{7,0},{8,9},{9,10},{10,1... | collective-permute-start | bytes 294920 | tf_op jit(solution)/shard_map/ppermute | solution.py:565
  64.3 8.5 %collective-permute-start.7 = (bf16[6,32,512]{2,1,0:T(8,128)(2,1)S(1)}, bf16[6,32,512]{2,1,0:T(8,128)(2,1)S(1)}, u32[]{:S(2)}, u32[]{:S(2)}) collective-permute-start(bf16[6,32,512]{2,1,0:T(8,128)(2,1)S(1)} %get-tuple-element.57.edge_in), channel_id=1, source_target_pairs={{0,8},{8,16},{16,24},{24,0},{1,9},{9,17},{17,25},{25,1},{2,10},{10... | collective-permute-start | bytes 589832 | tf_op jit(solution)/shard_map/ppermute | solution.py:566
  65.6 7.2 %collective-permute-start.8 = (bf16[6,8,512]{2,1,0:T(8,128)(2,1)S(1)}, bf16[6,8,512]{2,1,0:T(8,128)(2,1)S(1)}, u32[]{:S(2)}, u32[]{:S(2)}) collective-permute-start(bf16[6,8,512]{2,1,0:T(8,128)(2,1)S(1)} %get-tuple-element.60), channel_id=1, source_target_pairs={{0,9},{1,10},{2,11},{3,12},{4,13},{5,14},{6,15},{7,8},{8,17},{9,18... | collective-permute-start | bytes 147464 | tf_op jit(solution)/shard_map/ppermute | solution.py:567
  74.9 8.3 %collective-permute-start.10 = (bf16[6,32,512]{2,1,0:T(8,128)(2,1)S(1)}, bf16[6,32,512]{2,1,0:T(8,128)(2,1)S(1)}, u32[]{:S(2)}, u32[]{:S(2)}) collective-permute-start(bf16[6,32,512]{2,1,0:T(8,128)(2,1)S(1)} %get-tuple-element.64.edge_in), channel_id=1, source_target_pairs={{8,0},{16,8},{24,16},{0,24},{9,1},{17,9},{25,17},{1,25},{10,2},{18... | collective-permute-start | bytes 589832 | tf_op jit(solution)/shard_map/ppermute | solution.py:566
  76.0 5.3 %collective-permute-start.9 = (bf16[8,16,512]{2,1,0:T(8,128)(2,1)S(1)}, bf16[8,16,512]{2,1,0:T(8,128)(2,1)S(1)}, u32[]{:S(2)}, u32[]{:S(2)}) collective-permute-start(bf16[8,16,512]{2,1,0:T(8,128)(2,1)S(1)} %get-tuple-element.63), channel_id=1, source_target_pairs={{1,0},{2,1},{3,2},{4,3},{5,4},{6,5},{7,6},{0,7},{9,8},{10,9},{11,1... | collective-permute-start | bytes 393224 | tf_op jit(solution)/shard_map/ppermute | solution.py:565
  78.6 4.6 %collective-permute-start.11 = (bf16[6,8,512]{2,1,0:T(8,128)(2,1)S(1)}, bf16[6,8,512]{2,1,0:T(8,128)(2,1)S(1)}, u32[]{:S(2)}, u32[]{:S(2)}) collective-permute-start(bf16[6,8,512]{2,1,0:T(8,128)(2,1)S(1)} %get-tuple-element.65), channel_id=1, source_target_pairs={{9,0},{10,1},{11,2},{12,3},{13,4},{14,5},{15,6},{8,7},{17,8},{18,9... | collective-permute-start | bytes 147464 | tf_op jit(solution)/shard_map/ppermute | solution.py:567

commit v9 on v8

--- a/solution.py
+++ b/solution.py
@@ -367,8 +367,8 @@
     *refs,
 ):
     if final:
-        state_ref, wide_ref, taps_in, tap_ref, spread_ref, out_ref, spare_ref, mix_lon = refs[:8]
-        rows_ref, sems = refs[8:]
+        state_ref, wide_ref, taps_in, center_ref, tap_ref, spread_ref, out_ref = refs[:7]
+        spare_ref, mix_lon, rows_ref, sems = refs[7:]
         kept, width = left_new.shape[:2]
         copies = [
             pltpu.make_async_copy(left_new, state_ref.at[0:kept, 0:width], sems.at[0]),
@@ -381,7 +381,7 @@
         copies[1].start()
     else:
         edge_ref, lon_ref, corner_ref = refs[:3]
-        wide_ref, taps_in, tap_ref, spread_ref, out_ref, spare_ref, mix_lon = refs[3:]
+        wide_ref, taps_in, center_ref, tap_ref, spread_ref, out_ref, spare_ref, mix_lon = refs[3:]
     cols = lat_in.shape[1]
     groups = wide_ref.shape[0]
     main = 0 if shrink else EDGE
@@ -410,14 +410,17 @@
             value, beside = jnp.where(last, 0.0, value), jnp.where(last, 0.0, beside)
         put(wide_ref, k, main, value)
         put(wide_ref, k, side, beside)
-        shifted(wide_ref, taps_in, base, k, k if not shrink else k + SHIFT)
-    taps_in[:, :, own : own + SHIFT] = near_ref[...]
 
     @pl.loop(0, groups)
     def _(g):
-        convolve(taps_in.at[g], taps_ref, tap_ref, spread_ref, layer, g, 0, SHIFT)
-
-    center_ref = taps_in.at[:, HALO : HALO + 2, HALO : HALO + SHIFT]
+        for k in range(SHIFT):
+            for r in range(TAPS + 1):
+                columns = pl.ds(base + r, TILE, stride=2)
+                taps_in[r, SHIFT - own + k] = wide_ref[g, k, columns, :].astype(BF16)
+        taps_in[:, own : own + SHIFT] = near_ref[g]
+        center_ref[g] = taps_in[HALO : HALO + 2, HALO : HALO + SHIFT]
+        convolve(taps_in, taps_ref, tap_ref, spread_ref, layer, g, 0, SHIFT)
+
     finish(center_ref, spread_ref, mix_ref, out_ref, layer, 0, SHIFT)
     kept = left_new.shape[0]
     if final:
@@ -478,7 +481,8 @@
 def scratch_of(groups, seen, made, cols, chans):
     return (
         pltpu.VMEM((groups, seen, cols + EDGE, LANES), F32),
-        pltpu.VMEM((groups, TAPS + 1, seen, TILE, LANES), BF16),
+        pltpu.VMEM((TAPS + 1, seen, TILE, LANES), BF16),
+        pltpu.VMEM((groups, 2, made, TILE, LANES), BF16),
         pltpu.VMEM((TAPS * TAPS, TILE, LANES), BF16),
         pltpu.VMEM((2, made, TILE, chans), BF16),
         pltpu.VMEM((groups, made, cols, LANES), F32),

time: 86.7 us -> 86.4 us (level)
  no operation moved by 1% of the time
where the time goes in v9:
time: 86.4 us; the launch traced here: 85.9 us
  waiting for transfers between devices  33.3 us (39%)
  Pallas kernels  30.8 us (36%)
  starting transfers between devices  19.3 us (22%)
  other arithmetic  2.11 us (2%)
    pallas_call x15, Pallas kernels, call(): pl.pallas_call(kernel, out_shape=out_shape, in_specs=[pl.BlockSpec(memory...  30.8 us
    all_to_all x1, waiting for transfers between devices, body(): lax.all_to_all(send, ('lat', 'lon'), split_axis=0, concat_axis=0, tiled=T...  26.7 us
    all_to_all x1, starting transfers between devices, body(): lax.all_to_all(send, ('lat', 'lon'), split_axis=0, concat_axis=0, tiled=T...  7.42 us
    ppermute x4, waiting for transfers between devices, exchange(): lon = lax.ppermute(lon, 'lon', around)  5.01 us
    ppermute x4, starting transfers between devices, exchange(): lon = lax.ppermute(lon, 'lon', around)  4.89 us
    ppermute x4, starting transfers between devices, exchange(): lat = lax.ppermute(lat, 'lat', along)  4.43 us
    ppermute x4, starting transfers between devices, exchange(): corner = lax.ppermute(corner, ('lat', 'lon'), across)  2.6 us
    convert_element_type x1, other arithmetic, body(): mix = (gains[:, :, None] * point_w.astype(F32)).astype(BF16)  2.11 us
  transfers between devices with their start and end apart: 13, of which 8 were waited for; matrix products, arithmetic and copies ran while one was open for 2% of the time, Pallas kernels for 17%

profile of v9, /device:TPU:0, one launch (start us, length us, event | category | flops | bytes accessed | tf_op | source)
XLA Modules:
  0.0 85.9 jit_solution(5231439395496504553)
XLA Ops:
  0.0 4.8 %shard_map.91 = bf16[32,136,128]{2,1,0:T(8,128)(2,1)} custom-call(s32[1,1024]{1,0:T(1,128)} %bitcast.20, s32[4,1024]{1,0:T(4,128)} %bitcast.18, bf16[4,1024]{1,0:T(4,128)(2,1)} %bitcast.19, bf16[1024,256]{1,0:T(8,128)(2,1)} %obs_hbm.1), custom_call_target="tpu_custom_call" | custom-call | tf_op jit(solution)/shard_map/pallas_call | solution.py:466
  4.8 7.4 %all-to-all-start = ((bf16[32,136,128]{2,1,0:T(8,128)(2,1)}), bf16[32,136,128]{2,1,0:T(8,128)(2,1)}, u32[]{:S(2)}, u32[]{:S(2)}) async-start(bf16[32,136,128]{2,1,0:T(8,128)(2,1)} %shard_map.91), calls=%async_computation | async-start | bytes 2228224 | tf_op jit(solution)/shard_map/all_to_all | solution.py:598
  12.3 2.1 %multiply_convert_fusion.refs_2_.refs_1_.mix_ref = bf16[4,512,512]{2,1,0:T(8,128)(2,1)S(1)} fusion(bf16[4,512,512]{2,1,0:T(8,128)(2,1)} %param.16, f32[4,512]{1,0:T(4,128)S(1)} %copy-done.3), kind=kLoop, calls=%fused_computation | loop fusion | flops 3145728 | bytes 4202496 | tf_op jit(solution)/shard_map/convert_element_type | solution.py:601
  14.5 26.7 %all-to-all-done.got_hbm = bf16[32,136,128]{2,1,0:T(8,128)(2,1)} async-done(((bf16[32,136,128]{2,1,0:T(8,128)(2,1)}), bf16[32,136,128]{2,1,0:T(8,128)(2,1)}, u32[]{:S(2)}, u32[]{:S(2)}) %all-to-all-start) | async-done | bytes 1114144 | tf_op jit(solution)/shard_map/all_to_all | solution.py:598
  41.2 2.6 %shard_map.93 = (bf16[6,32,512]{2,1,0:T(8,128)(2,1)S(1)}, bf16[10,16,512]{2,1,0:T(8,128)(2,1)S(1)}, bf16[10,16,512]{2,1,0:T(8,128)(2,1)S(1)}, bf16[6,16,512]{2,1,0:T(8,128)(2,1)S(1)}, bf16[6,8,512]{2,1,0:T(8,128)(2,1)S(1)}) custom-call(bf16[32,136,128]{2,1,0:T(8,128)(2,1)} %all-to-all-done.got_hbm, bf16[256,512]{1,0:T(8,128)(2,1)S(1)} %get-tuple-element.40.proj_ref, ...), custom_call_target="tpu_custom_call" | custom-call | tf_op jit(solution)/shard_map/pallas_call | solution.py:466
  45.6 1.7 %shard_map.95.right_new.right_in = bf16[14,16,512]{2,1,0:T(8,128)(2,1)S(1)} custom-call(bf16[6,32,512]{2,1,0:T(8,128)(2,1)S(1)} %get-tuple-element.42.edge_in, bf16[10,16,512]{2,1,0:T(8,128)(2,1)S(1)} %get-tuple-element.43.left_in, bf16[10,16,512]{2,1,0:T(8,128)(2,1)S(1)} %get-tuple-element.44.right_in, f32[49,4,512]{2,1,0:T(4,128)S(1)} %bitcast.6, ...), custom_call_target="tpu_custom_call" | custom-call | flops 344064000 | tf_op jit(solution)/shard_map/pallas_call | solution.py:466
  47.3 2.4 %collective-permute-done.refs_0_.lon_in = bf16[6,16,512]{2,1,0:T(8,128)(2,1)S(1)} collective-permute-done((bf16[6,16,512]{2,1,0:T(8,128)(2,1)S(1)}, bf16[6,16,512]{2,1,0:T(8,128)(2,1)S(1)}, u32[]{:S(2)}, u32[]{:S(2)}) %collective-permute-start) | collective-permute-done | bytes 98336 | tf_op jit(solution)/shard_map/ppermute | solution.py:569
  49.7 1.9 %shard_map.94 = (bf16[14,16,512]{2,1,0:T(8,128)(2,1)S(1)}, f32[4,6,16,128]{3,2,1,0:T(8,128)S(1)}, bf16[4,8,6,16,128]{4,3,2,1,0:T(8,128)(2,1)S(1)}) custom-call(bf16[6,32,512]{2,1,0:T(8,128)(2,1)S(1)} %get-tuple-element.42.edge_in, bf16[10,16,512]{2,1,0:T(8,128)(2,1)S(1)} %get-tuple-element.43.left_in, bf16[10,16,512]{2,1,0:T(8,128)(2,1)S(1)} %get-tuple-element.44.right_in, ...), custom_call_target="tpu_custom_call" | custom-call | flops 1261568000 | tf_op jit(solution)/shard_map/pallas_call | solution.py:466
  51.9 2.0 %shard_map.96 = (bf16[6,32,512]{2,1,0:T(8,128)(2,1)S(1)}, bf16[8,16,512]{2,1,0:T(8,128)(2,1)S(1)}, bf16[6,8,512]{2,1,0:T(8,128)(2,1)S(1)}) custom-call(bf16[10,16,512]{2,1,0:T(8,128)(2,1)S(1)} %get-tuple-element.43.left_in, bf16[10,16,512]{2,1,0:T(8,128)(2,1)S(1)} %get-tuple-element.44.right_in, bf16[6,16,512]{2,1,0:T(8,128)(2,1)S(1)} %collective-permute-done.refs_0_.lon_in, ...), custom_call_target="tpu_custom_call" | custom-call | flops 491520000 | tf_op jit(solution)/shard_map/pallas_call | solution.py:466
  53.9 1.2 %collective-permute-start.4 = (bf16[6,32,512]{2,1,0:T(8,128)(2,1)S(1)}, bf16[6,32,512]{2,1,0:T(8,128)(2,1)S(1)}, u32[]{:S(2)}, u32[]{:S(2)}) collective-permute-start(bf16[6,32,512]{2,1,0:T(8,128)(2,1)S(1)} %get-tuple-element.52.edge_in), channel_id=1, source_target_pairs={{8,0},{16,8},{24,16},{0,24},{9,1},{17,9},{25,17},{1,25},{10,2},{18... | collective-permute-start | bytes 589832 | tf_op jit(solution)/shard_map/ppermute | solution.py:570
  55.1 2.1 %collective-permute-start.3 = (bf16[8,16,512]{2,1,0:T(8,128)(2,1)S(1)}, bf16[8,16,512]{2,1,0:T(8,128)(2,1)S(1)}, u32[]{:S(2)}, u32[]{:S(2)}) collective-permute-start(bf16[8,16,512]{2,1,0:T(8,128)(2,1)S(1)} %get-tuple-element.51), channel_id=1, source_target_pairs={{1,0},{2,1},{3,2},{4,3},{5,4},{6,5},{7,6},{0,7},{9,8},{10,9},{11,1... | collective-permute-start | bytes 393224 | tf_op jit(solution)/shard_map/ppermute | solution.py:569
  57.4 1.7 %shard_map.98.left_new.left_in = bf16[10,16,512]{2,1,0:T(8,128)(2,1)S(1)} custom-call(bf16[6,32,512]{2,1,0:T(8,128)(2,1)S(1)} %get-tuple-element.52.edge_in, bf16[14,16,512]{2,1,0:T(8,128)(2,1)S(1)} %get-tuple-element.47.left_new.left_in, bf16[14,16,512]{2,1,0:T(8,128)(2,1)S(1)} %shard_map.95.right_new.right_in, f32[49,4,512]{2,1,0:T(4,128)S(1)} %bitcast.9, ...), custom_call_target="tpu_custom_call" | custom-call | flops 409600000 | tf_op jit(solution)/shard_map/pallas_call | solution.py:466
  59.8 1.9 %shard_map.97 = (bf16[10,16,512]{2,1,0:T(8,128)(2,1)S(1)}, f32[4,6,16,128]{3,2,1,0:T(8,128)S(1)}, bf16[4,8,6,16,128]{4,3,2,1,0:T(8,128)(2,1)S(1)}) custom-call(bf16[6,32,512]{2,1,0:T(8,128)(2,1)S(1)} %get-tuple-element.52.edge_in, bf16[14,16,512]{2,1,0:T(8,128)(2,1)S(1)} %get-tuple-element.47.left_new.left_in, ...), custom_call_target="tpu_custom_call" | custom-call | flops 573440000 | tf_op jit(solution)/shard_map/pallas_call | solution.py:466
  62.1 2.0 %shard_map.99 = (bf16[6,32,512]{2,1,0:T(8,128)(2,1)S(1)}, bf16[6,16,512]{2,1,0:T(8,128)(2,1)S(1)}, bf16[6,8,512]{2,1,0:T(8,128)(2,1)S(1)}) custom-call(bf16[14,16,512]{2,1,0:T(8,128)(2,1)S(1)} %get-tuple-element.47.left_new.left_in, bf16[14,16,512]{2,1,0:T(8,128)(2,1)S(1)} %shard_map.95.right_new.right_in, ...), custom_call_target="tpu_custom_call" | custom-call | flops 491520000 | tf_op jit(solution)/shard_map/pallas_call | solution.py:466
  64.2 1.3 %collective-permute-start.7 = (bf16[6,32,512]{2,1,0:T(8,128)(2,1)S(1)}, bf16[6,32,512]{2,1,0:T(8,128)(2,1)S(1)}, u32[]{:S(2)}, u32[]{:S(2)}) collective-permute-start(bf16[6,32,512]{2,1,0:T(8,128)(2,1)S(1)} %get-tuple-element.57.edge_in), channel_id=1, source_target_pairs={{0,8},{8,16},{16,24},{24,0},{1,9},{9,17},{17,25},{25,1},{2,10},{10... | collective-permute-start | bytes 589832 | tf_op jit(solution)/shard_map/ppermute | solution.py:570
  66.2 1.9 %shard_map.101.right_new.right_in = bf16[14,16,512]{2,1,0:T(8,128)(2,1)S(1)} custom-call(bf16[6,32,512]{2,1,0:T(8,128)(2,1)S(1)} %get-tuple-element.57.edge_in, bf16[10,16,512]{2,1,0:T(8,128)(2,1)S(1)} %shard_map.98.left_new.left_in, bf16[10,16,512]{2,1,0:T(8,128)(2,1)S(1)} %get-tuple-element.55.right_new.right_in, f32[49,4,512]{2,1,0:T(4,128)S(1)} %bitcast.12, ...), custom_call_target="tpu_custom_call" | custom-call | flops 344064000 | tf_op jit(solution)/shard_map/pallas_call | solution.py:466
  68.1 1.9 %collective-permute-done.6.refs_0_.lon_in = bf16[6,16,512]{2,1,0:T(8,128)(2,1)S(1)} collective-permute-done((bf16[6,16,512]{2,1,0:T(8,128)(2,1)S(1)}, bf16[6,16,512]{2,1,0:T(8,128)(2,1)S(1)}, u32[]{:S(2)}, u32[]{:S(2)}) %collective-permute-start.6) | collective-permute-done | bytes 98336 | tf_op jit(solution)/shard_map/ppermute | solution.py:569
  70.0 1.9 %shard_map.100 = (bf16[14,16,512]{2,1,0:T(8,128)(2,1)S(1)}, f32[4,6,16,128]{3,2,1,0:T(8,128)S(1)}, bf16[4,8,6,16,128]{4,3,2,1,0:T(8,128)(2,1)S(1)}) custom-call(bf16[6,32,512]{2,1,0:T(8,128)(2,1)S(1)} %get-tuple-element.57.edge_in, bf16[10,16,512]{2,1,0:T(8,128)(2,1)S(1)} %shard_map.98.left_new.left_in, ...), custom_call_target="tpu_custom_call" | custom-call | flops 1261568000 | tf_op jit(solution)/shard_map/pallas_call | solution.py:466
  72.7 2.0 %shard_map.102 = (bf16[6,32,512]{2,1,0:T(8,128)(2,1)S(1)}, bf16[8,16,512]{2,1,0:T(8,128)(2,1)S(1)}, bf16[6,8,512]{2,1,0:T(8,128)(2,1)S(1)}) custom-call(bf16[10,16,512]{2,1,0:T(8,128)(2,1)S(1)} %shard_map.98.left_new.left_in, bf16[10,16,512]{2,1,0:T(8,128)(2,1)S(1)} %get-tuple-element.55.right_new.right_in, ...), custom_call_target="tpu_custom_call" | custom-call | flops 491520000 | tf_op jit(solution)/shard_map/pallas_call | solution.py:466
  74.7 1.1 %collective-permute-start.10 = (bf16[6,32,512]{2,1,0:T(8,128)(2,1)S(1)}, bf16[6,32,512]{2,1,0:T(8,128)(2,1)S(1)}, u32[]{:S(2)}, u32[]{:S(2)}) collective-permute-start(bf16[6,32,512]{2,1,0:T(8,128)(2,1)S(1)} %get-tuple-element.64.edge_in), channel_id=1, source_target_pairs={{8,0},{16,8},{24,16},{0,24},{9,1},{17,9},{25,17},{1,25},{10,2},{18... | collective-permute-start | bytes 589832 | tf_op jit(solution)/shard_map/ppermute | solution.py:570
  75.8 2.6 %collective-permute-start.9 = (bf16[8,16,512]{2,1,0:T(8,128)(2,1)S(1)}, bf16[8,16,512]{2,1,0:T(8,128)(2,1)S(1)}, u32[]{:S(2)}, u32[]{:S(2)}) collective-permute-start(bf16[8,16,512]{2,1,0:T(8,128)(2,1)S(1)} %get-tuple-element.63), channel_id=1, source_target_pairs={{1,0},{2,1},{3,2},{4,3},{5,4},{6,5},{7,6},{0,7},{9,8},{10,9},{11,1... | collective-permute-start | bytes 393224 | tf_op jit(solution)/shard_map/ppermute | solution.py:569
  79.4 1.7 %shard_map.104.left_new = bf16[10,16,512]{2,1,0:T(8,128)(2,1)S(1)} custom-call(bf16[6,32,512]{2,1,0:T(8,128)(2,1)S(1)} %get-tuple-element.64.edge_in, bf16[14,16,512]{2,1,0:T(8,128)(2,1)S(1)} %get-tuple-element.59.left_new.left_in, bf16[14,16,512]{2,1,0:T(8,128)(2,1)S(1)} %shard_map.101.right_new.right_in, f32[49,4,512]{2,1,0:T(4,128)S(1)} %bitcast.15, ...), custom_call_target="tpu_custom_call" | custom-call | flops 409600000 | tf_op jit(solution)/shard_map/pallas_call | solution.py:466
  81.1 1.9 %shard_map.103 = (bf16[10,16,512]{2,1,0:T(8,128)(2,1)S(1)}, f32[4,6,16,128]{3,2,1,0:T(8,128)S(1)}, bf16[4,8,6,16,128]{4,3,2,1,0:T(8,128)(2,1)S(1)}) custom-call(bf16[6,32,512]{2,1,0:T(8,128)(2,1)S(1)} %get-tuple-element.64.edge_in, bf16[14,16,512]{2,1,0:T(8,128)(2,1)S(1)} %get-tuple-element.59.left_new.left_in, ...), custom_call_target="tpu_custom_call" | custom-call | flops 573440000 | tf_op jit(solution)/shard_map/pallas_call | solution.py:466
  83.1 2.7 %shard_map.105 = bf16[16,32,512]{2,1,0:T(8,128)(2,1)} custom-call(bf16[14,16,512]{2,1,0:T(8,128)(2,1)S(1)} %get-tuple-element.59.left_new.left_in, bf16[14,16,512]{2,1,0:T(8,128)(2,1)S(1)} %shard_map.101.right_new.right_in, bf16[8,16,512]{2,1,0:T(8,128)(2,1)S(1)} %collective-permute-done.9.refs_0_.lon_in, ...), custom_call_target="tpu_custom_call" | custom-call | flops 491520000 | tf_op jit(solution)/shard_map/pallas_call | solution.py:466
  (26 shorter events, 5.8 us)
Async XLA Ops:
  0.0 12.2 %copy-start.2 = (bf16[256,512]{1,0:T(8,128)(2,1)S(1)}, bf16[256,512]{1,0:T(8,128)(2,1)}, u32[]{:S(2)}) copy-start(bf16[256,512]{1,0:T(8,128)(2,1)} %proj_hbm.1) | copy-start | bytes 786436
  0.0 12.2 %copy-start.1 = (bf16[16,32,512]{2,1,0:T(8,128)(2,1)S(1)}, bf16[16,32,512]{2,1,0:T(8,128)(2,1)}, u32[]{:S(2)}) copy-start(bf16[16,32,512]{2,1,0:T(8,128)(2,1)} %back_hbm.1) | copy-start | bytes 1572868
  0.0 12.3 %copy-start.3 = (f32[4,512]{1,0:T(4,128)S(1)}, f32[4,512]{1,0:T(4,128)}, u32[]{:S(2)}) copy-start(f32[4,512]{1,0:T(4,128)} %param.17) | copy-start | bytes 24580
  4.8 36.4 %all-to-all-start = ((bf16[32,136,128]{2,1,0:T(8,128)(2,1)}), bf16[32,136,128]{2,1,0:T(8,128)(2,1)}, u32[]{:S(2)}, u32[]{:S(2)}) async-start(bf16[32,136,128]{2,1,0:T(8,128)(2,1)} %shard_map.91), calls=%async_computation | async-start | bytes 2228224 | tf_op jit(solution)/shard_map/all_to_all | solution.py:598
  12.3 33.2 %copy-start = (f32[4,7,7,512]{3,0,2,1:T(4,128)S(1)}, f32[4,7,7,512]{3,0,2,1:T(4,128)}, u32[]{:S(2)}) copy-start(f32[4,7,7,512]{3,0,2,1:T(4,128)} %param.15) | copy-start | bytes 1204228
  43.8 5.9 %collective-permute-start = (bf16[6,16,512]{2,1,0:T(8,128)(2,1)S(1)}, bf16[6,16,512]{2,1,0:T(8,128)(2,1)S(1)}, u32[]{:S(2)}, u32[]{:S(2)}) collective-permute-start(bf16[6,16,512]{2,1,0:T(8,128)(2,1)S(1)} %get-tuple-element.45), channel_id=1, source_target_pairs={{0,1},{1,2},{2,3},{3,4},{4,5},{5,6},{6,7},{7,0},{8,9},{9,10},{10,1... | collective-permute-start | bytes 294920 | tf_op jit(solution)/shard_map/ppermute | solution.py:569
  43.9 8.1 %collective-permute-start.1 = (bf16[6,32,512]{2,1,0:T(8,128)(2,1)S(1)}, bf16[6,32,512]{2,1,0:T(8,128)(2,1)S(1)}, u32[]{:S(2)}, u32[]{:S(2)}) collective-permute-start(bf16[6,32,512]{2,1,0:T(8,128)(2,1)S(1)} %get-tuple-element.42.edge_in), channel_id=1, source_target_pairs={{0,8},{8,16},{16,24},{24,0},{1,9},{9,17},{17,25},{25,1},{2,10},{10... | collective-permute-start | bytes 589832 | tf_op jit(solution)/shard_map/ppermute | solution.py:570
  44.7 7.2 %collective-permute-start.2 = (bf16[6,8,512]{2,1,0:T(8,128)(2,1)S(1)}, bf16[6,8,512]{2,1,0:T(8,128)(2,1)S(1)}, u32[]{:S(2)}, u32[]{:S(2)}) collective-permute-start(bf16[6,8,512]{2,1,0:T(8,128)(2,1)S(1)} %get-tuple-element.48), channel_id=1, source_target_pairs={{0,9},{1,10},{2,11},{3,12},{4,13},{5,14},{6,15},{7,8},{8,17},{9,18... | collective-permute-start | bytes 147464 | tf_op jit(solution)/shard_map/ppermute | solution.py:571
  53.9 8.2 %collective-permute-start.4 = (bf16[6,32,512]{2,1,0:T(8,128)(2,1)S(1)}, bf16[6,32,512]{2,1,0:T(8,128)(2,1)S(1)}, u32[]{:S(2)}, u32[]{:S(2)}) collective-permute-start(bf16[6,32,512]{2,1,0:T(8,128)(2,1)S(1)} %get-tuple-element.52.edge_in), channel_id=1, source_target_pairs={{8,0},{16,8},{24,16},{0,24},{9,1},{17,9},{25,17},{1,25},{10,2},{18... | collective-permute-start | bytes 589832 | tf_op jit(solution)/shard_map/ppermute | solution.py:570
  55.1 4.7 %collective-permute-start.3 = (bf16[8,16,512]{2,1,0:T(8,128)(2,1)S(1)}, bf16[8,16,512]{2,1,0:T(8,128)(2,1)S(1)}, u32[]{:S(2)}, u32[]{:S(2)}) collective-permute-start(bf16[8,16,512]{2,1,0:T(8,128)(2,1)S(1)} %get-tuple-element.51), channel_id=1, source_target_pairs={{1,0},{2,1},{3,2},{4,3},{5,4},{6,5},{7,6},{0,7},{9,8},{10,9},{11,1... | collective-permute-start | bytes 393224 | tf_op jit(solution)/shard_map/ppermute | solution.py:569
  57.3 4.6 %collective-permute-start.5 = (bf16[6,8,512]{2,1,0:T(8,128)(2,1)S(1)}, bf16[6,8,512]{2,1,0:T(8,128)(2,1)S(1)}, u32[]{:S(2)}, u32[]{:S(2)}) collective-permute-start(bf16[6,8,512]{2,1,0:T(8,128)(2,1)S(1)} %get-tuple-element.53), channel_id=1, source_target_pairs={{9,0},{10,1},{11,2},{12,3},{13,4},{14,5},{15,6},{8,7},{17,8},{18,9... | collective-permute-start | bytes 147464 | tf_op jit(solution)/shard_map/ppermute | solution.py:571
  64.1 5.9 %collective-permute-start.6 = (bf16[6,16,512]{2,1,0:T(8,128)(2,1)S(1)}, bf16[6,16,512]{2,1,0:T(8,128)(2,1)S(1)}, u32[]{:S(2)}, u32[]{:S(2)}) collective-permute-start(bf16[6,16,512]{2,1,0:T(8,128)(2,1)S(1)} %get-tuple-element.58), channel_id=1, source_target_pairs={{0,1},{1,2},{2,3},{3,4},{4,5},{5,6},{6,7},{7,0},{8,9},{9,10},{10,1... | collective-permute-start | bytes 294920 | tf_op jit(solution)/shard_map/ppermute | solution.py:569
  64.2 8.5 %collective-permute-start.7 = (bf16[6,32,512]{2,1,0:T(8,128)(2,1)S(1)}, bf16[6,32,512]{2,1,0:T(8,128)(2,1)S(1)}, u32[]{:S(2)}, u32[]{:S(2)}) collective-permute-start(bf16[6,32,512]{2,1,0:T(8,128)(2,1)S(1)} %get-tuple-element.57.edge_in), channel_id=1, source_target_pairs={{0,8},{8,16},{16,24},{24,0},{1,9},{9,17},{17,25},{25,1},{2,10},{10... | collective-permute-start | bytes 589832 | tf_op jit(solution)/shard_map/ppermute | solution.py:570
  65.5 7.2 %collective-permute-start.8 = (bf16[6,8,512]{2,1,0:T(8,128)(2,1)S(1)}, bf16[6,8,512]{2,1,0:T(8,128)(2,1)S(1)}, u32[]{:S(2)}, u32[]{:S(2)}) collective-permute-start(bf16[6,8,512]{2,1,0:T(8,128)(2,1)S(1)} %get-tuple-element.60), channel_id=1, source_target_pairs={{0,9},{1,10},{2,11},{3,12},{4,13},{5,14},{6,15},{7,8},{8,17},{9,18... | collective-permute-start | bytes 147464 | tf_op jit(solution)/shard_map/ppermute | solution.py:571
  74.7 8.4 %collective-permute-start.10 = (bf16[6,32,512]{2,1,0:T(8,128)(2,1)S(1)}, bf16[6,32,512]{2,1,0:T(8,128)(2,1)S(1)}, u32[]{:S(2)}, u32[]{:S(2)}) collective-permute-start(bf16[6,32,512]{2,1,0:T(8,128)(2,1)S(1)} %get-tuple-element.64.edge_in), channel_id=1, source_target_pairs={{8,0},{16,8},{24,16},{0,24},{9,1},{17,9},{25,17},{1,25},{10,2},{18... | collective-permute-start | bytes 589832 | tf_op jit(solution)/shard_map/ppermute | solution.py:570
  75.8 5.3 %collective-permute-start.9 = (bf16[8,16,512]{2,1,0:T(8,128)(2,1)S(1)}, bf16[8,16,512]{2,1,0:T(8,128)(2,1)S(1)}, u32[]{:S(2)}, u32[]{:S(2)}) collective-permute-start(bf16[8,16,512]{2,1,0:T(8,128)(2,1)S(1)} %get-tuple-element.63), channel_id=1, source_target_pairs={{1,0},{2,1},{3,2},{4,3},{5,4},{6,5},{7,6},{0,7},{9,8},{10,9},{11,1... | collective-permute-start | bytes 393224 | tf_op jit(solution)/shard_map/ppermute | solution.py:569
  78.4 4.6 %collective-permute-start.11 = (bf16[6,8,512]{2,1,0:T(8,128)(2,1)S(1)}, bf16[6,8,512]{2,1,0:T(8,128)(2,1)S(1)}, u32[]{:S(2)}, u32[]{:S(2)}) collective-permute-start(bf16[6,8,512]{2,1,0:T(8,128)(2,1)S(1)} %get-tuple-element.65), channel_id=1, source_target_pairs={{9,0},{10,1},{11,2},{12,3},{13,4},{14,5},{15,6},{8,7},{17,8},{18,9... | collective-permute-start | bytes 147464 | tf_op jit(solution)/shard_map/ppermute | solution.py:571
